TPU v7x, 32 devices: a whole 2x2x4 slice. The times are simulated.
32 devices in a mesh: section: 2 (over x), dp: 2 (over core), seq: 8 (over z, y).
Axes of the slice: x: 2, y: 2, z: 4, core: 2. Of those that a mesh axis runs over, the one named last changes fastest.
Arguments:
- inputs: bfloat16 [8, 2, 1024, 768], P('dp', None, 'seq'), may hold values from -6 to 6
- cotangent: bfloat16 [8, 2, 1024, 768], P('dp', None, 'seq'), may hold values from -6 to 6
- qkv_weight: float32 [2, 768, 2304], P('section', 'seq'), may hold values from -0.21875 to 0.21875
- out_weight: float32 [2, 768, 768], P('section', 'seq'), may hold values from -0.875 to 0.875
- up_weight: float32 [2, 768, 3072], P('section', 'seq'), may hold values from -0.21875 to 0.21875
- down_weight: float32 [2, 3072, 768], P('section', 'seq'), may hold values from -0.109375 to 0.109375
- map_weight: float32 [2, 1536, 64], P('section', 'seq'), may hold values from -1.5 to 1.5
- biases: float32 [2, 8448], P('section', 'seq'), may hold values from -1.2 to 1.2
- gains: float32 [2, 1536], P('section', 'seq'), may hold values from 0.5 to 1.5
Outputs:
- layer_out: bfloat16 [2, 8, 2, 1024, 768], P('section', 'dp', None, 'seq')
- input_grads: bfloat16 [2, 8, 2, 1024, 768], P('section', 'dp', None, 'seq')
- qkv_grad: float32 [2, 768, 2304], P('section', 'seq')
- out_grad: float32 [2, 768, 768], P('section', 'seq')
- up_grad: float32 [2, 768, 3072], P('section', 'seq')
- down_grad: float32 [2, 3072, 768], P('section', 'seq')
- map_grad: float32 [2, 1536, 64], P('section', 'seq')
- bias_grad: float32 [2, 8448], P('section', 'seq')
- gain_grad: float32 [2, 1536], P('section', 'seq')
All inputs are finite; a program needn't handle non-finite values.
Results may differ from a plain program's by a relative error of at most 0.015.
The roundings to bfloat16 on the way count: a program that leaves them out, or rounds other values in their place, can miss the bound.
Values may be sent and summed in bfloat16 or wider, within the bound.
A program may use at most 512 MiB of HBM per device.

v0:
```python
import jax
import jax.numpy as jnp
from jax import lax
from jax.sharding import PartitionSpec as P

D = 768
FF = 3072
H = 12
HEAD = 64
BLOCK = 64


MAXIMUM_ACCURACY = lax.Precision.HIGHEST
NORM_EPSILON = 1e-05


def carried_in(part, axis, combine, identity, reverse):
    count = lax.axis_size(axis)
    place = lax.axis_index(axis)
    ahead = count - 1 - place if reverse else place
    gathered = jax.tree.map(lambda a: lax.all_gather(a, axis), part)
    state = jax.tree.map(lambda a, e: jnp.zeros_like(a) + jnp.asarray(e, a.dtype), part, identity)

    def one(lap, state):
        source = count - 1 - lap if reverse else lap
        return combine(
            state, jax.tree.map(lambda a: lax.dynamic_index_in_dim(a, source, 0, False), gathered)
        )

    return lax.fori_loop(0, ahead, one, state)


def shifted(value, axis, steps):
    count = lax.axis_size(axis)
    leading, last = (max(0, -steps), min(count, count - steps))
    return lax.ppermute(value, axis, [(source, source + steps) for source in range(leading, last)])


def normalize(values, gain_vector, shift_vector):
    average = jnp.mean(values, -1, keepdims=True)
    centred = values - average
    spread = jnp.mean(centred * centred, -1, keepdims=True)
    return centred * lax.rsqrt(spread + NORM_EPSILON) * gain_vector + shift_vector


def features(logits):
    return jnp.concatenate([jax.nn.softmax(logits, -1), jax.nn.softmax(-logits, -1)], -1)


def gelu_tanh(values):
    return jax.nn.gelu(values, approximate=True)


def adding(earlier, later_part):
    return jax.tree.map(jnp.add, earlier, later_part)


def across_rows(left_side, right_side):
    return lax.dot_general(
        left_side, right_side, (((0,), (0,)), ((), ())), preferred_element_type=jnp.float32
    )


def against_rows(left_side, right_side):
    return lax.dot_general(
        left_side, right_side, (((1,), (1,)), ((), ())), preferred_element_type=jnp.float32
    )


def precise(pattern, left_side, right_side):
    return jnp.einsum(pattern, left_side, right_side, precision=MAXIMUM_ACCURACY)


def causal_mask():
    places = lax.broadcasted_iota(jnp.int32, (BLOCK, BLOCK), 0)
    others = lax.broadcasted_iota(jnp.int32, (BLOCK, BLOCK), 1)
    return (others <= places).astype(jnp.float32)


def in_blocks(source_array, batch_rows):
    return source_array.reshape((batch_rows, -1, BLOCK) + source_array.shape[1:])


def prepare(gathered):
    qkv_full, out_full, up_full, down_full, map_full, bias_full, gain_full = [
        piece_array[0] for piece_array in gathered
    ]
    feature_maps = map_full.reshape(2, H, HEAD, HEAD)
    vectors = bias_full.astype(jnp.float32)
    scales = gain_full.astype(jnp.float32)
    pieces = (
        vectors[:D],
        vectors[D : 4 * D],
        vectors[4 * D : 5 * D],
        vectors[5 * D : 6 * D],
        vectors[6 * D : 6 * D + FF],
        vectors[6 * D + FF :],
        scales[:D],
        scales[D:],
    )
    return (qkv_full, out_full, up_full, down_full, feature_maps, pieces)


def block_sums(query_map, key_map, value_rows, batch_rows):
    query_blocks = in_blocks(query_map, batch_rows)
    key_blocks = in_blocks(key_map, batch_rows)
    value_blocks = in_blocks(value_rows, batch_rows).astype(jnp.float32)
    query_wide = query_blocks.astype(jnp.float32)
    key_wide = key_blocks.astype(jnp.float32)
    score_matrix = (
        jnp.einsum(
            "bcqhf,bckhf->bchqk", query_blocks, key_blocks, preferred_element_type=jnp.float32
        )
        * causal_mask()
    )
    block_state = precise("bckhf,bckhe->bchfe", key_wide, value_blocks)
    block_total = jnp.sum(key_wide, 2)
    return (query_wide, key_wide, value_blocks, score_matrix, block_state, block_total)


def attend(query_map, key_map, value_rows, initial, batch_rows):
    query_wide, key_wide, value_blocks, score_matrix, block_state, block_total = block_sums(
        query_map, key_map, value_rows, batch_rows
    )
    state_sum = jnp.sum(block_state, 1)
    total_sum = jnp.sum(block_total, 1)
    identity = (jnp.zeros_like(state_sum), jnp.zeros_like(total_sum))
    earlier = carried_in((state_sum, total_sum), "seq", adding, identity, False)
    overall = lax.psum((state_sum, total_sum), "seq")
    start_state = initial[0] + earlier[0]
    start_total = initial[1] + earlier[1]
    block_before = start_state[:, None] + jnp.cumsum(block_state, 1) - block_state
    total_before = start_total[:, None] + jnp.cumsum(block_total, 1) - block_total
    numerator = precise("bchqk,bckhe->bcqhe", score_matrix, value_blocks) + precise(
        "bcqhf,bchfe->bcqhe", query_wide, block_before
    )
    denominator = jnp.swapaxes(jnp.sum(score_matrix, -1), 2, 3) + precise(
        "bcqhf,bchf->bcqh", query_wide, total_before
    )
    mixture = numerator / denominator[..., None]
    handed = (initial[0] + overall[0], initial[1] + overall[1])
    return (mixture.reshape(value_rows.shape), denominator, (start_state, start_total), handed)


def attend_back(
    mixture_grad, query_map, key_map, value_rows, mixture, denominator, starts, future, batch_rows
):
    query_wide, key_wide, value_blocks, score_matrix, block_state, block_total = block_sums(
        query_map, key_map, value_rows, batch_rows
    )
    block_before = starts[0][:, None] + jnp.cumsum(block_state, 1) - block_state
    total_before = starts[1][:, None] + jnp.cumsum(block_total, 1) - block_total
    scaled = in_blocks(mixture_grad, batch_rows) / denominator[..., None]
    denominator_grad = -jnp.sum(scaled * in_blocks(mixture, batch_rows), -1)
    score_grad = (
        precise("bcqhe,bckhe->bchqk", scaled, value_blocks)
        + jnp.swapaxes(denominator_grad, 2, 3)[..., None]
    ) * causal_mask()
    query_grad = precise("bchqk,bckhf->bcqhf", score_grad, key_wide) + precise(
        "bcqhe,bchfe->bcqhf", scaled, block_before
    )
    query_grad = query_grad + denominator_grad[..., None] * total_before[:, :, None]
    state_grad = precise("bcqhf,bcqhe->bchfe", query_wide, scaled)
    total_grad = precise("bcqhf,bcqh->bchf", query_wide, denominator_grad)
    state_sum = jnp.sum(state_grad, 1)
    total_sum = jnp.sum(total_grad, 1)
    identity = (jnp.zeros_like(state_sum), jnp.zeros_like(total_sum))
    later_sums = carried_in((state_sum, total_sum), "seq", adding, identity, True)
    overall = lax.psum((state_sum, total_sum), "seq")
    ahead_state = future[0] + later_sums[0]
    ahead_total = future[1] + later_sums[1]
    rest_state = ahead_state[:, None] + state_sum[:, None] - jnp.cumsum(state_grad, 1)
    rest_total = ahead_total[:, None] + total_sum[:, None] - jnp.cumsum(total_grad, 1)
    key_grad = precise("bchqk,bcqhf->bckhf", score_grad, query_wide) + precise(
        "bckhe,bchfe->bckhf", value_blocks, rest_state
    )
    key_grad = key_grad + rest_total[:, :, None]
    value_grad = precise("bchqk,bcqhe->bckhe", score_matrix, scaled) + precise(
        "bckhf,bchfe->bckhe", key_wide, rest_state
    )
    return (
        query_grad.reshape(query_map.shape),
        key_grad.reshape(key_map.shape),
        value_grad.reshape(value_rows.shape),
        overall,
    )


def forward(tokens, params, initial):
    qkv_full, out_full, up_full, down_full, feature_maps, pieces = params
    shift_one, qkv_bias, out_bias, shift_two, up_bias, down_bias, gain_one, gain_two = pieces
    batch_rows = tokens.shape[0]
    flattened = tokens.reshape(-1, D)
    row_count = flattened.shape[0]
    normed = normalize(flattened, gain_one, shift_one).astype(jnp.bfloat16)
    projected = (jnp.dot(normed, qkv_full, preferred_element_type=jnp.float32) + qkv_bias).astype(
        jnp.bfloat16
    )
    query_rows = projected[:, :D].reshape(row_count, H, HEAD)
    key_rows = projected[:, D : 2 * D].reshape(row_count, H, HEAD)
    value_rows = projected[:, 2 * D :].reshape(row_count, H, HEAD)
    query_logits = jnp.einsum(
        "rhe,hef->rhf", query_rows, feature_maps[0], preferred_element_type=jnp.float32
    )
    key_logits = jnp.einsum(
        "rhe,hef->rhf", key_rows, feature_maps[1], preferred_element_type=jnp.float32
    )
    query_map = features(query_logits).astype(jnp.bfloat16)
    key_map = features(key_logits).astype(jnp.bfloat16)
    mixture, denominator, starts, handed = attend(
        query_map, key_map, value_rows, initial, batch_rows
    )
    mixture_low = mixture.reshape(row_count, D).astype(jnp.bfloat16)
    residual = (
        flattened + jnp.dot(mixture_low, out_full, preferred_element_type=jnp.float32) + out_bias
    )
    normed_two = normalize(residual, gain_two, shift_two).astype(jnp.bfloat16)
    before_act = jnp.dot(normed_two, up_full, preferred_element_type=jnp.float32) + up_bias
    hidden = gelu_tanh(before_act).astype(jnp.bfloat16)
    result = residual + jnp.dot(hidden, down_full, preferred_element_type=jnp.float32) + down_bias
    kept_values = (
        flattened,
        normed,
        projected,
        query_logits,
        key_logits,
        query_map,
        key_map,
        mixture,
        denominator,
        starts,
        residual,
        normed_two,
        before_act,
        hidden,
    )
    return (result.reshape(tokens.shape), handed, kept_values)


def backward(upstream, params, kept_values, future):
    qkv_full, out_full, up_full, down_full, feature_maps, pieces = params
    shift_one, qkv_bias, out_bias, shift_two, up_bias, down_bias, gain_one, gain_two = pieces
    (
        flattened,
        normed,
        projected,
        query_logits,
        key_logits,
        query_map,
        key_map,
        mixture,
        denominator,
        starts,
        residual,
        normed_two,
        before_act,
        hidden,
    ) = kept_values
    batch_rows = upstream.shape[0]
    row_count = flattened.shape[0]
    out_grad = upstream.reshape(row_count, D)
    down_bias_grad = jnp.sum(out_grad, 0)
    out_low = out_grad.astype(jnp.bfloat16)
    down_weight_grad = across_rows(hidden, out_low)
    hidden_grad = against_rows(out_low, down_full)
    _, gelu_back = jax.vjp(gelu_tanh, before_act)
    before_grad = gelu_back(hidden_grad)[0].astype(jnp.bfloat16)
    up_bias_grad = jnp.sum(before_grad.astype(jnp.float32), 0)
    up_weight_grad = across_rows(normed_two, before_grad)
    normed_two_grad = against_rows(before_grad, up_full)
    _, norm_back_two = jax.vjp(normalize, residual, gain_two, shift_two)
    residual_part, gain_two_grad, shift_two_grad = norm_back_two(normed_two_grad)
    residual_grad = out_grad + residual_part
    out_bias_grad = jnp.sum(residual_grad, 0)
    residual_low = residual_grad.astype(jnp.bfloat16)
    mixture_low = mixture.reshape(row_count, D).astype(jnp.bfloat16)
    out_weight_grad = across_rows(mixture_low, residual_low)
    mixture_grad = against_rows(residual_low, out_full).reshape(row_count, H, HEAD)
    query_rows = projected[:, :D].reshape(row_count, H, HEAD)
    key_rows = projected[:, D : 2 * D].reshape(row_count, H, HEAD)
    value_rows = projected[:, 2 * D :].reshape(row_count, H, HEAD)
    query_map_grad, key_map_grad, value_grad, handed = attend_back(
        mixture_grad,
        query_map,
        key_map,
        value_rows,
        mixture,
        denominator,
        starts,
        future,
        batch_rows,
    )
    _, query_back = jax.vjp(features, query_logits)
    query_logit_grad = query_back(query_map_grad)[0]
    _, key_back = jax.vjp(features, key_logits)
    key_logit_grad = key_back(key_map_grad)[0]
    maps_wide = feature_maps.astype(jnp.float32)
    query_grad = precise("rhf,hef->rhe", query_logit_grad, maps_wide[0])
    key_grad = precise("rhf,hef->rhe", key_logit_grad, maps_wide[1])
    map_weight_grad = jnp.stack(
        [
            precise("rhe,rhf->hef", query_rows.astype(jnp.float32), query_logit_grad),
            precise("rhe,rhf->hef", key_rows.astype(jnp.float32), key_logit_grad),
        ]
    ).reshape(2 * H * HEAD, HEAD)
    projected_grad = jnp.concatenate(
        [
            query_grad.reshape(row_count, D),
            key_grad.reshape(row_count, D),
            value_grad.reshape(row_count, D),
        ],
        1,
    ).astype(jnp.bfloat16)
    qkv_bias_grad = jnp.sum(projected_grad.astype(jnp.float32), 0)
    qkv_weight_grad = across_rows(normed, projected_grad)
    normed_grad = against_rows(projected_grad, qkv_full)
    _, norm_back_one = jax.vjp(normalize, flattened, gain_one, shift_one)
    input_part, gain_one_grad, shift_one_grad = norm_back_one(normed_grad)
    input_grad = residual_grad + input_part
    bias_grad = jnp.concatenate(
        [shift_one_grad, qkv_bias_grad, out_bias_grad, shift_two_grad, up_bias_grad, down_bias_grad]
    )
    gain_grad = jnp.concatenate([gain_one_grad, gain_two_grad])
    layer_grads = (
        qkv_weight_grad,
        out_weight_grad,
        up_weight_grad,
        down_weight_grad,
        map_weight_grad,
        bias_grad,
        gain_grad,
    )
    return (input_grad.reshape(upstream.shape), handed, layer_grads)


def reduce_grads(full_grads):
    g_qkv, g_out, g_up, g_down, g_map, g_bias, g_gain = full_grads
    s_qkv, s_out, s_up, s_down, s_map, s_bias, s_gain = (
        lax.psum_scatter(g_qkv, "seq", scatter_dimension=1, tiled=True),
        lax.psum_scatter(g_out, "seq", scatter_dimension=1, tiled=True),
        lax.psum_scatter(g_up, "seq", scatter_dimension=1, tiled=True),
        lax.psum_scatter(g_down, "seq", scatter_dimension=1, tiled=True),
        lax.psum_scatter(g_map, "seq", scatter_dimension=1, tiled=True),
        lax.psum_scatter(g_bias, "seq", scatter_dimension=1, tiled=True),
        lax.psum_scatter(g_gain, "seq", scatter_dimension=1, tiled=True),
    )
    return lax.psum((s_qkv, s_out, s_up, s_down, s_map, s_bias, s_gain), "dp")


def shards(
    inputs, cotangent, qkv_weight, out_weight, up_weight, down_weight, map_weight, biases, gains
):
    section_index = lax.axis_index("section")
    batch_rows = inputs.shape[0]
    micro_count = inputs.shape[1]
    gathered = (
        lax.all_gather(qkv_weight.astype(jnp.bfloat16), "seq", axis=1, tiled=True),
        lax.all_gather(out_weight.astype(jnp.bfloat16), "seq", axis=1, tiled=True),
        lax.all_gather(up_weight.astype(jnp.bfloat16), "seq", axis=1, tiled=True),
        lax.all_gather(down_weight.astype(jnp.bfloat16), "seq", axis=1, tiled=True),
        lax.all_gather(map_weight.astype(jnp.bfloat16), "seq", axis=1, tiled=True),
        lax.all_gather(biases.astype(jnp.bfloat16), "seq", axis=1, tiled=True),
        lax.all_gather(gains.astype(jnp.bfloat16), "seq", axis=1, tiled=True),
    )
    params = prepare(gathered)
    empty_state = (
        jnp.zeros((batch_rows, H, 2 * HEAD, HEAD), jnp.float32),
        jnp.zeros((batch_rows, H, 2 * HEAD), jnp.float32),
    )
    blank_rows = jnp.zeros(inputs.shape[:1] + inputs.shape[2:], jnp.bfloat16)
    moments = jnp.arange(micro_count + 1, dtype=jnp.int32)

    def forward_moment(carry, moment):
        handed, arriving = carry
        own_tokens = lax.dynamic_index_in_dim(
            inputs, jnp.minimum(moment, micro_count - 1), 1, False
        )
        source = jnp.where(section_index == 0, own_tokens, arriving).astype(jnp.float32)
        carried = moment - section_index >= 1
        initial = (jnp.where(carried, handed[0], 0.0), jnp.where(carried, handed[1], 0.0))
        result, handed_next, kept_values = forward(source, params, initial)
        outgoing = result.astype(jnp.bfloat16)
        arriving_next = shifted(outgoing, "section", 1)
        return ((handed_next, arriving_next), (outgoing, kept_values))

    _, (result_stack, kept_stack) = lax.scan(forward_moment, (empty_state, blank_rows), moments)
    regathered = (
        lax.all_gather(qkv_weight.astype(jnp.bfloat16), "seq", axis=1, tiled=True),
        lax.all_gather(out_weight.astype(jnp.bfloat16), "seq", axis=1, tiled=True),
        lax.all_gather(up_weight.astype(jnp.bfloat16), "seq", axis=1, tiled=True),
        lax.all_gather(down_weight.astype(jnp.bfloat16), "seq", axis=1, tiled=True),
        lax.all_gather(map_weight.astype(jnp.bfloat16), "seq", axis=1, tiled=True),
        lax.all_gather(biases.astype(jnp.bfloat16), "seq", axis=1, tiled=True),
        lax.all_gather(gains.astype(jnp.bfloat16), "seq", axis=1, tiled=True),
    )
    back_params = prepare(regathered)
    zero_grads = (
        jnp.zeros((D, 3 * D), jnp.float32),
        jnp.zeros((D, D), jnp.float32),
        jnp.zeros((D, FF), jnp.float32),
        jnp.zeros((FF, D), jnp.float32),
        jnp.zeros((2 * H * HEAD, HEAD), jnp.float32),
        jnp.zeros((7 * D + FF,), jnp.float32),
        jnp.zeros((2 * D,), jnp.float32),
    )

    def backward_moment(carry, pieces):
        future, returning, grad_sums = carry
        slot, kept_values = pieces
        chosen = slot - section_index
        own_grad = lax.dynamic_index_in_dim(cotangent, jnp.maximum(slot - 1, 0), 1, False)
        live = (chosen >= 0) & (chosen < micro_count)
        upstream = jnp.where(section_index == 1, own_grad, returning).astype(jnp.float32)
        upstream = jnp.where(live, upstream, 0.0)
        later_micro = live & (chosen < micro_count - 1)
        ahead_part = (
            jnp.where(later_micro, future[0], 0.0),
            jnp.where(later_micro, future[1], 0.0),
        )
        input_grad, future_next, layer_grads = backward(
            upstream, back_params, kept_values, ahead_part
        )
        outgoing = input_grad.astype(jnp.bfloat16)
        grad_sums = tuple((previous + current for previous, current in zip(grad_sums, layer_grads)))
        returning_next = shifted(outgoing, "section", -1)
        return ((future_next, returning_next, grad_sums), outgoing)

    (_, _, grad_sums), grad_stack = lax.scan(
        backward_moment, (empty_state, blank_rows, zero_grads), (moments, kept_stack), reverse=True
    )
    layer_out = jnp.stack(
        [
            lax.dynamic_index_in_dim(result_stack, micro_index + section_index, 0, False)
            for micro_index in range(micro_count)
        ],
        1,
    )
    input_grads = jnp.stack(
        [
            lax.dynamic_index_in_dim(grad_stack, micro_index + section_index, 0, False)
            for micro_index in range(micro_count)
        ],
        1,
    )
    full_grads = tuple((grad_array[None] for grad_array in grad_sums))
    reduced = reduce_grads(full_grads)
    return (
        layer_out[None],
        input_grads[None],
        reduced[0],
        reduced[1],
        reduced[2],
        reduced[3],
        reduced[4],
        reduced[5],
        reduced[6],
    )


def solution(mesh):
    placed = (
        P("dp", None, "seq", None),
        P("dp", None, "seq", None),
        P("section", "seq", None),
        P("section", "seq", None),
        P("section", "seq", None),
        P("section", "seq", None),
        P("section", "seq", None),
        P("section", "seq"),
        P("section", "seq"),
    )
    return jax.shard_map(
        shards,
        mesh=mesh,
        in_specs=placed,
        out_specs=(
            P("section", "dp", None, "seq", None),
            P("section", "dp", None, "seq", None),
            P("section", "seq", None),
            P("section", "seq", None),
            P("section", "seq", None),
            P("section", "seq", None),
            P("section", "seq", None),
            P("section", "seq"),
            P("section", "seq"),
        ),
        check_vma=False,
    )
```

profile of v0, /device:TPU:13, one launch (start us, length us, event | category | flops | bytes accessed | tf_op | source)
XLA Modules:
  0.0 3395.3 jit_solution(12368639496665386133)
XLA Ops:
  13.4 25.2 all_gather.86
  43.5 25.7 all-reduce.4
  70.4 49.9 %all-gather.23.cloned.1.call-done = bf16[1,768,2304]{2,1,0:T(8,128)(2,1)} async-done(((bf16[1,96,2304]{2,1,0:T(8,128)(2,1)}), bf16[1,768,2304]{2,1,0:T(8,128)(2,1)}) %all-gather.23.cloned.1.call-update) | async-done | bytes 3538960 | tf_op jit(solution)/shard_map/all_gather | solution.py:357
  120.3 80.7 %all-gather.29.cloned.1.call-done = bf16[1,3072,768]{2,1,0:T(8,128)(2,1)} async-done(((bf16[1,384,768]{2,1,0:T(8,128)(2,1)}), bf16[1,3072,768]{2,1,0:T(8,128)(2,1)}) %all-gather.29.cloned.1.call-update) | async-done | bytes 4718608 | tf_op jit(solution)/shard_map/all_gather | solution.py:360
  201.0 80.7 %all-gather.27.cloned.1.call-done = bf16[1,768,3072]{2,1,0:T(8,128)(2,1)} async-done(((bf16[1,96,3072]{2,1,0:T(8,128)(2,1)}), bf16[1,768,3072]{2,1,0:T(8,128)(2,1)}) %all-gather.27.cloned.1.call-update) | async-done | bytes 4718608 | tf_op jit(solution)/shard_map/all_gather | solution.py:359
  284.3 986.5 %while.138 = (s32[]{:T(128)}, f32[4,12,128,64]{2,3,1,0:T(8,128)}, f32[4,12,128]{2,1,0:T(8,128)}, bf16[4,128,768]{2,1,0:T(8,128)(2,1)}, bf16[3,4,128,768]{3,2,1,0...) while((s32[]{:T(128)}, f32[4,12,128,64]{2,3,1,0:T(8,128)}, ...), condition=%wide.region_23.24_spmd.clone, body=%wide.region_0.23_spmd.clone.sunk | while | flops 8752316416 | bytes 462515680 | solution.py:386
  343.4 27.4 psum.109
  370.8 26.0 all-gather.13
  413.5 81.5 %all-gather.31.cloned.1.call-done = f32[32,12,128,64]{2,3,1,0:T(8,128)} async-done(((f32[4,12,128,64]{2,3,1,0:T(8,128)}), f32[32,12,128,64]{2,3,1,0:T(8,128)}) %all-gather.31.cloned.1.call-update) | async-done | bytes 12582928 | tf_op jit(solution)/shard_map/while/body/eval_jaxpr/all_gather | solution.py:21
  497.6 26.7 while.141
  651.1 58.9 %psum.109 = f32[4,12,128]{2,1,0:T(8,128)} all-reduce(f32[4,12,128]{2,1,0:T(8,128)S(1)} %get-tuple-element.2896), channel_id=1, replica_groups=mesh['section'=2,'dp'=2,'seq'=8] {'seq'}, use_global_device_ids=true, to_apply=%region_10.10 | all-reduce | flops 6144 | bytes 49152 | tf_op jit(solution)/shard_map/while/body/eval_jaxpr/psum | solution.py:129
  709.9 25.9 all-gather.13
  752.6 81.4 %all-gather.31.cloned.1.call-done = f32[32,12,128,64]{2,3,1,0:T(8,128)} async-done(((f32[4,12,128,64]{2,3,1,0:T(8,128)}), f32[32,12,128,64]{2,3,1,0:T(8,128)}) %all-gather.31.cloned.1.call-update) | async-done | bytes 12582928 | tf_op jit(solution)/shard_map/while/body/eval_jaxpr/all_gather | solution.py:21
  836.8 26.7 while.141
  989.8 58.7 %psum.109 = f32[4,12,128]{2,1,0:T(8,128)} all-reduce(f32[4,12,128]{2,1,0:T(8,128)S(1)} %get-tuple-element.2896), channel_id=1, replica_groups=mesh['section'=2,'dp'=2,'seq'=8] {'seq'}, use_global_device_ids=true, to_apply=%region_10.10 | all-reduce | flops 6144 | bytes 49152 | tf_op jit(solution)/shard_map/while/body/eval_jaxpr/psum | solution.py:129
  1048.5 26.3 all-gather.13
  1091.6 81.1 %all-gather.31.cloned.1.call-done = f32[32,12,128,64]{2,3,1,0:T(8,128)} async-done(((f32[4,12,128,64]{2,3,1,0:T(8,128)}), f32[32,12,128,64]{2,3,1,0:T(8,128)}) %all-gather.31.cloned.1.call-update) | async-done | bytes 12582928 | tf_op jit(solution)/shard_map/while/body/eval_jaxpr/all_gather | solution.py:21
  1175.3 26.7 while.141
  1275.4 1318.8 %while.140 = (s32[]{:T(128)}, f32[4,12,128,64]{2,3,1,0:T(8,128)}, f32[4,12,128]{2,1,0:T(8,128)}, bf16[4,128,768]{2,1,0:T(8,128)(2,1)}, f32[768,2304]{1,0:T(8,128...) while((s32[]{:T(128)}, f32[4,12,128,64]{2,3,1,0:T(8,128)}, ...), condition=%wide.region_65.66_spmd.clone, body=%wide.region_24.65_spmd.clone.sunk | while | flops 20271110144 | bytes 738679424 | solution.py:428
  1286.2 9.8 convert_reduce_fusion.15
  1318.5 8.7 fusion.456
  1391.5 57.3 %all-gather.15 = f32[32,12,128]{2,1,0:T(8,128)S(1)} all-gather(f32[4,12,128]{2,1,0:T(8,128)S(1)} %bitcast_reduce_fusion.4), channel_id=5, replica_groups=mesh['section'=2,'dp'=2,'seq'=8] {'seq'}, dimensions={0}, use_global_device_ids=true | all-gather | bytes 221184 | tf_op jit(solution)/shard_map/while/body/eval_jaxpr/all_gather | solution.py:21
  1502.6 35.1 %all-gather.33.cloned.1.call-done = f32[32,12,128,64]{2,3,1,0:T(8,128)} async-done(((f32[4,12,128,64]{2,3,1,0:T(8,128)}), f32[32,12,128,64]{2,3,1,0:T(8,128)}) %all-gather.33.cloned.1.call-update) | async-done | bytes 12582928 | tf_op jit(solution)/shard_map/while/body/eval_jaxpr/all_gather | solution.py:21
  1539.8 35.7 %while.142 = (s32[]{:T(128)}, f32[4,12,128,64]{3,2,1,0:T(8,128)}, f32[4,12,128]{2,1,0:T(8,128)S(1)}, s32[]{:T(128)}, f32[8,4,12,128,64]{3,4,2,1,0:T(8,128)}, /*i...) while((s32[]{:T(128)}, f32[4,12,128,64]{3,2,1,0:T(8,128)}, ...), condition=%wide.region_44.44_spmd, body=%wide.region_43.43_spmd.sunk | while | flops 399366 | bytes 11083931 | solution.py:30
  1576.3 51.5 %psum.111 = f32[4,12,128]{2,1,0:T(8,128)} all-reduce(f32[4,12,128]{2,1,0:T(8,128)S(1)} %copy-done.79), channel_id=1, replica_groups=mesh['section'=2,'dp'=2,'seq'=8] {'seq'}, use_global_device_ids=true, to_apply=%region_33.33 | all-reduce | flops 6144 | bytes 49152 | tf_op jit(solution)/shard_map/while/body/eval_jaxpr/psum | solution.py:169
  1691.4 45.3 %all-reduce.13.cloned.1.call-done = f32[4,12,128,64]{2,3,1,0:T(8,128)} async-done(((f32[4,12,128,64]{2,3,1,0:T(8,128)}), f32[4,12,128,64]{2,3,1,0:T(8,128)}) %all-reduce.13.cloned.1.call-update) | async-done | bytes 1572880 | tf_op jit(solution)/shard_map/while/body/eval_jaxpr/psum | solution.py:169
  1745.0 9.8 convert_reduce_fusion.15
  1850.3 24.4 all-gather.15
  1915.7 11.0 select_add_fusion.13
  1934.8 29.0 all-gather.33.cloned.1.call-done
  1965.9 35.7 %while.142 = (s32[]{:T(128)}, f32[4,12,128,64]{3,2,1,0:T(8,128)}, f32[4,12,128]{2,1,0:T(8,128)S(1)}, s32[]{:T(128)}, f32[8,4,12,128,64]{3,4,2,1,0:T(8,128)}, /*i...) while((s32[]{:T(128)}, f32[4,12,128,64]{3,2,1,0:T(8,128)}, ...), condition=%wide.region_44.44_spmd, body=%wide.region_43.43_spmd.sunk | while | flops 399366 | bytes 11083931 | solution.py:30
  2002.4 51.4 %psum.111 = f32[4,12,128]{2,1,0:T(8,128)} all-reduce(f32[4,12,128]{2,1,0:T(8,128)S(1)} %copy-done.79), channel_id=1, replica_groups=mesh['section'=2,'dp'=2,'seq'=8] {'seq'}, use_global_device_ids=true, to_apply=%region_33.33 | all-reduce | flops 6144 | bytes 49152 | tf_op jit(solution)/shard_map/while/body/eval_jaxpr/psum | solution.py:169
  2119.5 45.0 %all-reduce.13.cloned.1.call-done = f32[4,12,128,64]{2,3,1,0:T(8,128)} async-done(((f32[4,12,128,64]{2,3,1,0:T(8,128)}), f32[4,12,128,64]{2,3,1,0:T(8,128)}) %all-reduce.13.cloned.1.call-update) | async-done | bytes 1572880 | tf_op jit(solution)/shard_map/while/body/eval_jaxpr/psum | solution.py:169
  2172.8 9.8 convert_reduce_fusion.15
  2278.1 24.4 all-gather.15
  2343.6 11.0 select_add_fusion.13
  2362.7 28.9 all-gather.33.cloned.1.call-done
  2393.6 35.7 %while.142 = (s32[]{:T(128)}, f32[4,12,128,64]{3,2,1,0:T(8,128)}, f32[4,12,128]{2,1,0:T(8,128)S(1)}, s32[]{:T(128)}, f32[8,4,12,128,64]{3,4,2,1,0:T(8,128)}, /*i...) while((s32[]{:T(128)}, f32[4,12,128,64]{3,2,1,0:T(8,128)}, ...), condition=%wide.region_44.44_spmd, body=%wide.region_43.43_spmd.sunk | while | flops 399366 | bytes 11083931 | solution.py:30
  2430.9 51.5 %psum.111 = f32[4,12,128]{2,1,0:T(8,128)} all-reduce(f32[4,12,128]{2,1,0:T(8,128)S(1)} %copy-done.79), channel_id=1, replica_groups=mesh['section'=2,'dp'=2,'seq'=8] {'seq'}, use_global_device_ids=true, to_apply=%region_33.33 | all-reduce | flops 6144 | bytes 49152 | tf_op jit(solution)/shard_map/while/body/eval_jaxpr/psum | solution.py:169
  2548.5 42.6 %all-reduce.13.cloned.1.call-done = f32[4,12,128,64]{2,3,1,0:T(8,128)} async-done(((f32[4,12,128,64]{2,3,1,0:T(8,128)}), f32[4,12,128,64]{2,3,1,0:T(8,128)}) %all-reduce.13.cloned.1.call-update) | async-done | bytes 1572880 | tf_op jit(solution)/shard_map/while/body/eval_jaxpr/psum | solution.py:169
  2606.0 58.2 %reduce-scatter.16.cloned.1.call-done = f32[1,96,768]{2,1,0:T(8,128)} async-done(((f32[1,768,768]{2,1,0:T(8,128)}), f32[1,96,768]{2,1,0:T(8,128)}) %reduce-scatter.16.cloned.1.call-update) | async-done | bytes 294928 | tf_op jit(solution)/shard_map/reduce_scatter | solution.py:340
  2664.2 133.2 %reduce-scatter.14.cloned.1.call-done = f32[1,96,2304]{2,1,0:T(8,128)} async-done(((f32[1,768,2304]{2,1,0:T(8,128)}), f32[1,96,2304]{2,1,0:T(8,128)}) %reduce-scatter.14.cloned.1.call-update) | async-done | bytes 884752 | tf_op jit(solution)/shard_map/reduce_scatter | solution.py:339
  2797.4 166.1 %reduce-scatter.18.cloned.1.call-done = f32[1,96,3072]{2,1,0:T(8,128)} async-done(((f32[1,768,3072]{2,1,0:T(8,128)}), f32[1,96,3072]{2,1,0:T(8,128)}) %reduce-scatter.18.cloned.1.call-update) | async-done | bytes 1179664 | tf_op jit(solution)/shard_map/reduce_scatter | solution.py:341
  2963.5 166.3 %reduce-scatter.20.cloned.1.call-done = f32[1,384,768]{2,1,0:T(8,128)} async-done(((f32[1,3072,768]{2,1,0:T(8,128)}), f32[1,384,768]{2,1,0:T(8,128)}) %reduce-scatter.20.cloned.1.call-update) | async-done | bytes 1179664 | tf_op jit(solution)/shard_map/reduce_scatter | solution.py:342
  3134.6 60.5 %reduce-scatter.26.cloned.1.call-done = f32[192,1]{1,0:T(8,128)} async-done(((f32[1536,1]{1,0:T(8,128)}), f32[192,1]{1,0:T(8,128)}) %reduce-scatter.26.cloned.1.call-update) | async-done | bytes 784
  3196.0 93.5 %reduce-scatter.24.cloned.1.call-done = f32[1056,1]{1,0:T(8,128)} async-done(((f32[8448,1]{1,0:T(8,128)}), f32[1056,1]{1,0:T(8,128)}) %reduce-scatter.24.cloned.1.call-update) | async-done | bytes 4240
  3290.8 63.1 %reduce-scatter.22.cloned.1.call-done = f32[192,64]{1,0:T(8,128)} async-done(((f32[1536,64]{1,0:T(8,128)}), f32[192,64]{1,0:T(8,128)}) %reduce-scatter.22.cloned.1.call-update) | async-done | bytes 49168
  3361.4 20.8 all-reduce.9.cloned.1.call-done
  (1566 shorter events, 1320.0 us)
Async XLA Ops:
  7.2 63.2 %all-gather.25.cloned.1.call-start = ((), (), s32[]{:S(2)}) async-start(), calls=%async_computation.8 | async-start | bytes 1327104 | tf_op jit(solution)/shard_map/all_gather | solution.py:358
  9.1 111.2 %all-gather.23.cloned.1.call-start = ((), (), s32[]{:S(2)}) async-start(), calls=%async_computation.7 | async-start | bytes 3981312 | tf_op jit(solution)/shard_map/all_gather | solution.py:357
  11.1 189.9 %all-gather.29.cloned.1.call-start = ((), (), s32[]{:S(2)}) async-start(), calls=%async_computation.10 | async-start | bytes 5308416 | tf_op jit(solution)/shard_map/all_gather | solution.py:360
  12.1 269.6 %all-gather.27.cloned.1.call-start = ((), (), s32[]{:S(2)}) async-start(), calls=%async_computation.9 | async-start | bytes 5308416 | tf_op jit(solution)/shard_map/all_gather | solution.py:359
  284.7 210.4 %all-gather.31.cloned.1.call-start = ((), (), s32[]{:S(2)}) async-start(), calls=%async_computation.20 | async-start | bytes 14155776 | tf_op jit(solution)/shard_map/while/body/eval_jaxpr/all_gather | solution.py:21
  315.9 95.7 %copy-start.7 = (f32[4,2,12,128,64]{3,4,2,1,0:T(8,128)}, f32[4,2,12,128,64]{3,4,2,1,0:T(8,128)S(1)}, u32[]{:S(2)}) copy-start(f32[4,2,12,128,64]{3,4,2,1,0:T(8,128)S(1)} %get-tuple-element.2905) | copy-start | bytes 9437188 | tf_op jit(solution)/shard_map/while
  495.1 94.1 %all-reduce.11.cloned.1.call-start = ((), (), s32[]{:S(2)}) async-start(), calls=%async_computation.19 | async-start | bytes 3145728 | tf_op jit(solution)/shard_map/while/body/eval_jaxpr/psum | solution.py:129
  562.1 29.2 collective-permute-start.1
  592.9 241.1 %all-gather.31.cloned.1.call-start = ((), (), s32[]{:S(2)}) async-start(), calls=%async_computation.20 | async-start | bytes 14155776 | tf_op jit(solution)/shard_map/while/body/eval_jaxpr/all_gather | solution.py:21
  623.7 127.0 %copy-start.7 = (f32[4,2,12,128,64]{3,4,2,1,0:T(8,128)}, f32[4,2,12,128,64]{3,4,2,1,0:T(8,128)S(1)}, u32[]{:S(2)}) copy-start(f32[4,2,12,128,64]{3,4,2,1,0:T(8,128)S(1)} %get-tuple-element.2905) | copy-start | bytes 9437188 | tf_op jit(solution)/shard_map/while
  834.0 94.0 %all-reduce.11.cloned.1.call-start = ((), (), s32[]{:S(2)}) async-start(), calls=%async_computation.19 | async-start | bytes 3145728 | tf_op jit(solution)/shard_map/while/body/eval_jaxpr/psum | solution.py:129
  901.4 28.7 collective-permute-start.1
  931.5 241.2 %all-gather.31.cloned.1.call-start = ((), (), s32[]{:S(2)}) async-start(), calls=%async_computation.20 | async-start | bytes 14155776 | tf_op jit(solution)/shard_map/while/body/eval_jaxpr/all_gather | solution.py:21
  962.4 127.3 %copy-start.7 = (f32[4,2,12,128,64]{3,4,2,1,0:T(8,128)}, f32[4,2,12,128,64]{3,4,2,1,0:T(8,128)S(1)}, u32[]{:S(2)}) copy-start(f32[4,2,12,128,64]{3,4,2,1,0:T(8,128)S(1)} %get-tuple-element.2905) | copy-start | bytes 9437188 | tf_op jit(solution)/shard_map/while
  1172.7 93.5 %all-reduce.11.cloned.1.call-start = ((), (), s32[]{:S(2)}) async-start(), calls=%async_computation.19 | async-start | bytes 3145728 | tf_op jit(solution)/shard_map/while/body/eval_jaxpr/psum | solution.py:129
  1239.7 28.7 collective-permute-start.1
  1278.1 259.6 %all-gather.33.cloned.1.call-start = ((), (), s32[]{:S(2)}) async-start(), calls=%async_computation.22 | async-start | bytes 14155776 | tf_op jit(solution)/shard_map/while/body/eval_jaxpr/all_gather | solution.py:21
  1312.5 43.2 %copy-start.92 = (f32[4,2,64,12]{2,3,1,0:T(8,128)}, f32[4,2,64,12]{2,3,1,0:T(8,128)S(1)}, u32[]{:S(2)}) copy-start(f32[4,2,64,12]{2,3,1,0:T(8,128)S(1)} %copy.525) | copy-start | bytes 73732 | tf_op jit(solution)/shard_map/while
  1366.9 274.4 %copy-start.77 = (f32[512,12]{0,1:T(8,128)}, f32[512,12]{0,1:T(8,128)S(1)}, u32[]{:S(2)}) copy-start(f32[512,12]{0,1:T(8,128)S(1)} %get-tuple-element.2979) | copy-start | bytes 73732 | tf_op jit(solution)/shard_map/while
  1387.3 62.9 %copy-start = (f32[1,512,12,64]{3,1,2,0:T(8,128)S(1)}, f32[1,512,12,64]{3,1,2,0:T(8,128)}, u32[]{:S(2)}) copy-start(f32[1,512,12,64]{3,1,2,0:T(8,128)} %copy.530) | copy-start | bytes 4718596 | tf_op jit(solution)/shard_map/while
  1539.8 35.7 %copy-start.79 = (f32[4,12,128]{2,1,0:T(8,128)S(1)}, f32[4,12,128]{2,1,0:T(8,128)}, u32[]{:S(2)}) copy-start(f32[4,12,128]{2,1,0:T(8,128)} %copy-done.78) | copy-start | bytes 73732 | tf_op jit(solution)/shard_map/while
  1634.8 101.9 %all-reduce.13.cloned.1.call-start = ((), (), s32[]{:S(2)}) async-start(), calls=%async_computation.21 | async-start | bytes 3145728 | tf_op jit(solution)/shard_map/while/body/eval_jaxpr/psum | solution.py:169
  1682.4 54.3 %collective-permute-start = (bf16[4,128,768]{2,1,0:T(8,128)(2,1)S(1)}, bf16[4,128,768]{2,1,0:T(8,128)(2,1)}, u32[]{:S(2)}, u32[]{:S(2)}) collective-permute-start(bf16[4,128,768]{2,1,0:T(8,128)(2,1)S(1)} %bitcast.659), channel_id=1, source_target_pairs={{16,0},{17,1},{18,2},{19,3},{20,4},{21,5},{22,6},{23,7},{24,8},{25... | collective-permute-start | bytes 2359304 | tf_op jit(solution)/shard_map/while/body/eval_jaxpr/ppermute | solution.py:36
  1685.3 51.4 %copy-start.69 = (bf16[768,768]{1,0:T(8,128)(2,1)S(1)}, bf16[768,768]{1,0:T(8,128)(2,1)}, u32[]{:S(2)}) copy-start(bf16[768,768]{1,0:T(8,128)(2,1)} %get-tuple-element.3450) | copy-start | bytes 3538948 | tf_op jit(solution)/shard_map/while
  1685.3 51.4 %copy-start.138 = (s32[3]{0:T(128)S(1)}, s32[3]{0:T(128)}, u32[]{:S(2)}) copy-start(s32[3]{0:T(128)} %copy-done.137) | copy-start | bytes 40 | tf_op jit(solution)/shard_map/while
  1736.9 226.9 %all-gather.33.cloned.1.call-start = ((), (), s32[]{:S(2)}) async-start(), calls=%async_computation.22 | async-start | bytes 14155776 | tf_op jit(solution)/shard_map/while/body/eval_jaxpr/all_gather | solution.py:21
  1771.3 43.6 %copy-start.92 = (f32[4,2,64,12]{2,3,1,0:T(8,128)}, f32[4,2,64,12]{2,3,1,0:T(8,128)S(1)}, u32[]{:S(2)}) copy-start(f32[4,2,64,12]{2,3,1,0:T(8,128)S(1)} %copy.525) | copy-start | bytes 73732 | tf_op jit(solution)/shard_map/while
  1826.1 241.2 %copy-start.77 = (f32[512,12]{0,1:T(8,128)}, f32[512,12]{0,1:T(8,128)S(1)}, u32[]{:S(2)}) copy-start(f32[512,12]{0,1:T(8,128)S(1)} %get-tuple-element.2979) | copy-start | bytes 73732 | tf_op jit(solution)/shard_map/while
  1965.9 35.7 %copy-start.79 = (f32[4,12,128]{2,1,0:T(8,128)S(1)}, f32[4,12,128]{2,1,0:T(8,128)}, u32[]{:S(2)}) copy-start(f32[4,12,128]{2,1,0:T(8,128)} %copy-done.78) | copy-start | bytes 73732 | tf_op jit(solution)/shard_map/while
  2060.9 103.6 %all-reduce.13.cloned.1.call-start = ((), (), s32[]{:S(2)}) async-start(), calls=%async_computation.21 | async-start | bytes 3145728 | tf_op jit(solution)/shard_map/while/body/eval_jaxpr/psum | solution.py:169
  2108.3 56.2 %collective-permute-start = (bf16[4,128,768]{2,1,0:T(8,128)(2,1)S(1)}, bf16[4,128,768]{2,1,0:T(8,128)(2,1)}, u32[]{:S(2)}, u32[]{:S(2)}) collective-permute-start(bf16[4,128,768]{2,1,0:T(8,128)(2,1)S(1)} %bitcast.659), channel_id=1, source_target_pairs={{16,0},{17,1},{18,2},{19,3},{20,4},{21,5},{22,6},{23,7},{24,8},{25... | collective-permute-start | bytes 2359304 | tf_op jit(solution)/shard_map/while/body/eval_jaxpr/ppermute | solution.py:36
  2111.2 53.3 %copy-start.69 = (bf16[768,768]{1,0:T(8,128)(2,1)S(1)}, bf16[768,768]{1,0:T(8,128)(2,1)}, u32[]{:S(2)}) copy-start(bf16[768,768]{1,0:T(8,128)(2,1)} %get-tuple-element.3450) | copy-start | bytes 3538948 | tf_op jit(solution)/shard_map/while
  2111.2 53.3 %copy-start.138 = (s32[3]{0:T(128)S(1)}, s32[3]{0:T(128)}, u32[]{:S(2)}) copy-start(s32[3]{0:T(128)} %copy-done.137) | copy-start | bytes 40 | tf_op jit(solution)/shard_map/while
  2164.7 226.8 %all-gather.33.cloned.1.call-start = ((), (), s32[]{:S(2)}) async-start(), calls=%async_computation.22 | async-start | bytes 14155776 | tf_op jit(solution)/shard_map/while/body/eval_jaxpr/all_gather | solution.py:21
  2199.1 43.7 %copy-start.92 = (f32[4,2,64,12]{2,3,1,0:T(8,128)}, f32[4,2,64,12]{2,3,1,0:T(8,128)S(1)}, u32[]{:S(2)}) copy-start(f32[4,2,64,12]{2,3,1,0:T(8,128)S(1)} %copy.525) | copy-start | bytes 73732 | tf_op jit(solution)/shard_map/while
  2254.0 242.3 %copy-start.77 = (f32[512,12]{0,1:T(8,128)}, f32[512,12]{0,1:T(8,128)S(1)}, u32[]{:S(2)}) copy-start(f32[512,12]{0,1:T(8,128)S(1)} %get-tuple-element.2979) | copy-start | bytes 73732 | tf_op jit(solution)/shard_map/while
  2489.9 101.2 %all-reduce.13.cloned.1.call-start = ((), (), s32[]{:S(2)}) async-start(), calls=%async_computation.21 | async-start | bytes 3145728 | tf_op jit(solution)/shard_map/while/body/eval_jaxpr/psum | solution.py:169
  2537.3 53.8 %collective-permute-start = (bf16[4,128,768]{2,1,0:T(8,128)(2,1)S(1)}, bf16[4,128,768]{2,1,0:T(8,128)(2,1)}, u32[]{:S(2)}, u32[]{:S(2)}) collective-permute-start(bf16[4,128,768]{2,1,0:T(8,128)(2,1)S(1)} %bitcast.659), channel_id=1, source_target_pairs={{16,0},{17,1},{18,2},{19,3},{20,4},{21,5},{22,6},{23,7},{24,8},{25... | collective-permute-start | bytes 2359304 | tf_op jit(solution)/shard_map/while/body/eval_jaxpr/ppermute | solution.py:36
  2540.2 50.9 %copy-start.69 = (bf16[768,768]{1,0:T(8,128)(2,1)S(1)}, bf16[768,768]{1,0:T(8,128)(2,1)}, u32[]{:S(2)}) copy-start(bf16[768,768]{1,0:T(8,128)(2,1)} %get-tuple-element.3450) | copy-start | bytes 3538948 | tf_op jit(solution)/shard_map/while
  2540.2 50.9 %copy-start.138 = (s32[3]{0:T(128)S(1)}, s32[3]{0:T(128)}, u32[]{:S(2)}) copy-start(s32[3]{0:T(128)} %copy-done.137) | copy-start | bytes 40 | tf_op jit(solution)/shard_map/while
  2594.2 70.0 %reduce-scatter.16.cloned.1.call-start = ((), (), s32[]{:S(2)}) async-start(), calls=%async_computation.12 | async-start | bytes 2654208 | tf_op jit(solution)/shard_map/reduce_scatter | solution.py:340
  2594.8 202.6 %reduce-scatter.14.cloned.1.call-start = ((), (), s32[]{:S(2)}) async-start(), calls=%async_computation.11 | async-start | bytes 7962624 | tf_op jit(solution)/shard_map/reduce_scatter | solution.py:339
  2595.4 368.1 %reduce-scatter.18.cloned.1.call-start = ((), (), s32[]{:S(2)}) async-start(), calls=%async_computation.13 | async-start | bytes 10616832 | tf_op jit(solution)/shard_map/reduce_scatter | solution.py:341
  2596.1 533.7 %reduce-scatter.20.cloned.1.call-start = ((), (), s32[]{:S(2)}) async-start(), calls=%async_computation.14 | async-start | bytes 10616832 | tf_op jit(solution)/shard_map/reduce_scatter | solution.py:342
  2596.7 598.4 %reduce-scatter.26.cloned.1.call-start = ((), (), s32[]{:S(2)}) async-start(), calls=%async_computation.17 | async-start | bytes 884736
  2598.0 691.5 %reduce-scatter.24.cloned.1.call-start = ((), (), s32[]{:S(2)}) async-start(), calls=%async_computation.16 | async-start | bytes 4866048
  2602.8 751.1 %reduce-scatter.22.cloned.1.call-start = ((), (), s32[]{:S(2)}) async-start(), calls=%async_computation.15 | async-start | bytes 884736
  2605.9 776.3 %all-reduce.9.cloned.1.call-start = ((), (), s32[]{:S(2)}) async-start(), calls=%async_computation.18 | async-start | bytes 7077888 | tf_op jit(solution)/shard_map/psum | solution.py:347
  (392 other events, 2253.8 us)
Sparse Core Ops, SparseCore 0:
  10.2 44.1 all-gather.24
  57.2 63.0 all-gather.22
  123.1 77.9 all-gather.28
  203.6 78.0 all-gather.26
  316.1 178.9 all-gather.30
  499.5 89.6 all-reduce.10
  623.9 210.1 all-gather.30
  838.8 89.2 all-reduce.10
  962.5 210.1 all-gather.30
  1177.2 89.0 all-reduce.10
  1327.4 210.2 all-gather.32
  1639.8 96.8 all-reduce.12
  1786.2 177.5 all-gather.32
  2065.9 98.5 all-reduce.12
  2214.0 177.4 all-gather.32
  2494.9 96.1 all-reduce.12
  2598.2 65.9 reduce-scatter.15
  2667.8 129.6 reduce-scatter.13
  2801.4 162.0 reduce-scatter.17
  2967.3 162.3 reduce-scatter.19
  3134.0 61.0 reduce-scatter.25
  3198.7 90.8 reduce-scatter.23
  3293.8 60.1 reduce-scatter.21
  3356.3 25.8 all-reduce.8
where the time goes:
time: 3410 us; the launch traced here: 3400 us
  waiting for transfers between devices  1460 us (43%)
  local copies, waits for them, and re-layouts  543 us (16%)
  blocking collectives  541 us (16%)
  matrix products  439 us (13%)
  other arithmetic  360 us (11%)
    all_gather x6, waiting for transfers between devices, carried_in(): gathered = jax.tree.map(lambda a: lax.all_gather(a, axis), part)  337 us
    unnamed x15, waiting for transfers between devices  220 us
    dot_general x54, matrix products, precise(): jnp.einsum(pattern, left_side, right_side, precision=MAXIMUM_ACCURACY)  195 us
    all_gather x6, blocking collectives, carried_in(): gathered = jax.tree.map(lambda a: lax.all_gather(a, axis), part)  184 us
    reduce_scatter x1, waiting for transfers between devices, reduce_grads(): lax.psum_scatter(g_down, 'seq', scatter_dimension=1, tiled=True)  166 us
    reduce_scatter x1, waiting for transfers between devices, reduce_grads(): lax.psum_scatter(g_up, 'seq', scatter_dimension=1, tiled=True)  166 us
    psum x3, blocking collectives, attend_back(): overall = lax.psum((state_sum, total_sum), 'seq')  154 us
    psum x3, blocking collectives, attend(): overall = lax.psum((state_sum, total_sum), 'seq')  145 us
  transfers between devices with their start and end apart: 30, of which 23 were waited for; matrix products, arithmetic and copies ran while one was open for 27% of the time, Pallas kernels for 0%

commit v1 on v0

v1 whole, which is shorter than its diff:
```python
import functools

import jax
import jax.numpy as jnp
from jax import lax
from jax.experimental import pallas as pl
from jax.experimental.pallas import tpu as pltpu
from jax.sharding import PartitionSpec as P

D = 768
FF = 3072
H = 12
HEAD = 64
CH = 128
PAIRS = H // 2
QB = 2 * H * HEAD
STATE_ROWS = D + 16
EPS = 1e-05
TILE = 256
AXES = ("section", "dp", "seq")
f32 = jnp.float32
bf16 = jnp.bfloat16

VMEM = pl.BlockSpec(memory_space=pltpu.VMEM)
SMEM = pl.BlockSpec(memory_space=pltpu.SMEM)
ANY = pl.BlockSpec(memory_space=pl.ANY)


def nn(a, b):
    return lax.dot_general(a, b, (((1,), (0,)), ((), ())), preferred_element_type=f32)


def nt(a, b):
    return lax.dot_general(a, b, (((1,), (1,)), ((), ())), preferred_element_type=f32)


def tn(a, b):
    return lax.dot_general(a, b, (((0,), (0,)), ((), ())), preferred_element_type=f32)


def loop(count, body):
    lax.fori_loop(0, count, lambda i, c: (body(i), c)[1], 0)


def span(i, size):
    return pl.ds(pl.multiple_of(i * size, size), size)


class Weight:
    def __init__(self, arrays, layer, col=0, width=None):
        self.arrays = list(arrays)
        self.layer = layer
        self.col = col
        self.width = width

    def issue(self, refs, dst, sem, place):
        if len(self.arrays) == 1:
            pltpu.make_async_copy(refs[0], dst, sem).start()
            return
        x, d, z, y = (place[i] for i in range(4))
        nz, r = self.arrays[0].shape[:2]
        c = self.width
        for lay in range(2):

            @pl.when(x == (self.layer if lay == 0 else 1 - self.layer))
            def _():
                for yy in range(2):
                    for cc in range(2):
                        src = refs[lay * 4 + yy * 2 + cc]
                        half = jnp.where(d == 0, cc, 1 - cc)
                        ypos = jnp.where(y == 0, yy, 1 - yy)
                        for o in range(nz):
                            row = (lax.rem(z - o + nz, nz) * 2 + ypos) * r
                            pltpu.make_async_copy(
                                src.at[o, :, pl.ds(self.col, c)],
                                dst.at[
                                    pl.ds(pl.multiple_of(row, r), r),
                                    pl.ds(pl.multiple_of(half * c, c), c),
                                ],
                                sem,
                            ).start()


def finish(dst, sem):
    pltpu.make_async_copy(dst, dst, sem).wait()


def call(kernel, outs, scratch, specs, args, flops, out_specs=None, vmem=60):
    if out_specs is None:
        out_specs = [VMEM] * len(outs)
    moved = sum(a.size * a.dtype.itemsize for a in args if a.ndim > 0)
    moved += sum(o.size * o.dtype.itemsize for o in outs)
    return pl.pallas_call(
        kernel,
        out_shape=outs,
        in_specs=specs,
        out_specs=out_specs,
        scratch_shapes=scratch,
        compiler_params=pltpu.CompilerParams(vmem_limit_bytes=vmem * 1024 * 1024),
        cost_estimate=pl.CostEstimate(flops=flops, bytes_accessed=moved, transcendentals=0),
    )(*args)


def shape(dims, kind):
    return jax.ShapeDtypeStruct(dims, kind)


def standardize(u):
    cen = u - jnp.mean(u, -1, keepdims=True)
    rstd = lax.rsqrt(jnp.mean(cen * cen, -1, keepdims=True) + EPS)
    return cen * rstd, rstd


def lanes(rows):
    return lax.broadcasted_iota(jnp.int32, (rows, CH), 1)


def half_sums(t, low):
    s1 = jnp.sum(jnp.where(low, t, 0.0), -1, keepdims=True)
    s2 = jnp.sum(jnp.where(low, 0.0, t), -1, keepdims=True)
    return jnp.where(low, s1, s2)


def half_softmax(l, low):
    m1 = jnp.max(jnp.where(low, l, -jnp.inf), -1, keepdims=True)
    m2 = jnp.max(jnp.where(low, -jnp.inf, l), -1, keepdims=True)
    p = jnp.exp(l - jnp.where(low, m1, m2))
    return p / half_sums(p, low)


def project_kernel(w, nw, place, u, gain, shift, bias, bd, *rest):
    refs, (a, qkv, ph, st, wv, sem) = rest[:nw], rest[nw:]
    w.issue(refs, wv, sem, place)
    t = u.shape[0]

    def norm(i):
        xh, _ = standardize(u[span(i, CH), :].astype(f32))
        a[span(i, CH), :] = (xh * gain[...] + shift[...]).astype(bf16)

    loop(t // CH, norm)
    finish(wv, sem)

    def column(j):
        cols = span(j, TILE)
        qkv[:, cols] = (nn(a[...], wv[:, cols]) + bias[:, cols]).astype(bf16)

    loop(3 * D // TILE, column)
    low = lanes(CH) < HEAD

    def pair(p):
        def rows(i):
            lg = nn(qkv[span(i, CH), span(p, CH)], bd[p])
            for hh in range(2):
                ph[span(i, CH), span(2 * p + hh, CH)] = half_softmax(
                    lg[:, hh * CH : (hh + 1) * CH], low
                ).astype(bf16)

        loop(t // CH, rows)

    loop(2 * PAIRS, pair)

    def state(p):
        v = qkv[:, pl.ds(pl.multiple_of(2 * D + p * CH, CH), CH)]
        for hh in range(2):
            k = ph[:, pl.ds(pl.multiple_of((H + 2 * p + hh) * CH, CH), CH)]
            full = tn(v, k)
            st[span(2 * p + hh, HEAD), :] = full[hh * HEAD : (hh + 1) * HEAD]
            st[pl.ds(D + 2 * p + hh, 1), :] = jnp.sum(k.astype(f32), 0, keepdims=True)

    loop(PAIRS, state)
    st[D + H :, :] = jnp.zeros((STATE_ROWS - D - H, CH), f32)


def project(layer, place, u, vecs, bd, w):
    t = u.shape[0]
    return call(
        functools.partial(project_kernel, w, len(w.arrays)),
        [
            shape((t, D), bf16),
            shape((t, 3 * D), bf16),
            shape((t, 2 * QB), bf16),
            shape((STATE_ROWS, CH), f32),
        ],
        [pltpu.VMEM((D, 3 * D), bf16), pltpu.SemaphoreType.DMA],
        [SMEM] + [VMEM] * 5 + [ANY] * len(w.arrays),
        [place, u, vecs["gain1"], vecs["shift1"], vecs["qkv_bias"], bd] + w.arrays,
        2 * t * D * 3 * D,
    )


def sum_states(dst, parts):
    dst[...] = functools.reduce(jnp.add, [part[...] for part in parts])


def mix_kernel(ws, ns, np_, place, qkv, ph, u, outb, gain, shift, upb, downb, *rest):
    wo, wu, wd = ws
    no, nu, nd = ns
    parts, rest = rest[:np_], rest[np_:]
    ro, ru, rd = rest[:no], rest[no : no + nu], rest[no + nu : no + nu + nd]
    o, inv, ob, r, n2, hid, gp, res, wov, wuv, wdv, s0, sems = rest[no + nu + nd :]
    wo.issue(ro, wov, sems.at[0], place)
    wu.issue(ru, wuv, sems.at[1], place)
    wd.issue(rd, wdv, sems.at[2], place)
    t = u.shape[0]
    sum_states(s0, parts)
    low = lanes(CH) < HEAD
    tril = lax.broadcasted_iota(jnp.int32, (CH, CH), 0) >= lanes(CH)

    def pair(p):
        cols = span(p, CH)
        s = s0[cols, :]
        tot = [s0[pl.ds(D + 2 * p + hh, 1), :] for hh in range(2)]
        for c in range(t // CH):
            rows = pl.ds(c * CH, CH)
            v = qkv[rows, pl.ds(pl.multiple_of(2 * D + p * CH, CH), CH)]
            sl = s.astype(bf16)
            got = []
            new = []
            for hh in range(2):
                q = ph[rows, span(2 * p + hh, CH)]
                k = ph[rows, pl.ds(pl.multiple_of((H + 2 * p + hh) * CH, CH), CH)]
                score = jnp.where(tril, nt(q, k), 0.0)
                num = nn(score.astype(bf16), v) + nt(q, sl)
                den = jnp.sum(score + q.astype(f32) * tot[hh], -1, keepdims=True)
                rec = 1.0 / den
                got.append((num * rec, rec))
                new.append(tn(v, k)[hh * HEAD : (hh + 1) * HEAD])
                tot[hh] = tot[hh] + jnp.sum(k.astype(f32), 0, keepdims=True)
            s = s + jnp.concatenate(new, 0)
            both = jnp.where(low, got[0][0], got[1][0])
            o[rows, cols] = both
            ob[rows, cols] = both.astype(bf16)
            inv[rows, cols] = jnp.where(low, got[0][1], got[1][1])

    loop(PAIRS, pair)
    finish(wov, sems.at[0])

    def out_col(j):
        cols = span(j, TILE)
        r[:, cols] = u[:, cols].astype(f32) + nn(ob[...], wov[:, cols]) + outb[:, cols]

    loop(D // TILE, out_col)

    def norm(i):
        xh, _ = standardize(r[span(i, CH), :])
        n2[span(i, CH), :] = (xh * gain[...] + shift[...]).astype(bf16)

    loop(t // CH, norm)
    finish(wuv, sems.at[1])

    def up_col(j):
        cols = span(j, TILE)
        zt = nn(n2[...], wuv[:, cols]) + upb[:, cols]
        z2 = zt * zt
        th = jnp.tanh(GELU_C * zt * (1.0 + GELU_A * z2))
        half = 0.5 * (1.0 + th)
        hid[:, cols] = (zt * half).astype(bf16)
        gp[:, cols] = half + 0.5 * zt * (1.0 - th * th) * (GELU_C * (1.0 + 3.0 * GELU_A * z2))

    loop(FF // TILE, up_col)
    finish(wdv, sems.at[2])

    def down_col(j):
        cols = span(j, TILE)
        res[:, cols] = (r[:, cols] + nn(hid[...], wdv[:, cols]) + downb[:, cols]).astype(bf16)

    loop(D // TILE, down_col)


GELU_C = 0.7978845608028654
GELU_A = 0.044715


def mix(layer, place, qkv, ph, u, vecs, parts, wo, wu, wd):
    t = u.shape[0]
    ws = (wo, wu, wd)
    ns = tuple(len(w.arrays) for w in ws)
    return call(
        functools.partial(mix_kernel, ws, ns, len(parts)),
        [
            shape((t, D), f32),
            shape((t, D), f32),
            shape((t, D), bf16),
            shape((t, D), f32),
            shape((t, D), bf16),
            shape((t, FF), bf16),
            shape((t, FF), f32),
            shape((t, D), bf16),
        ],
        [
            pltpu.VMEM((D, D), bf16),
            pltpu.VMEM((D, FF), bf16),
            pltpu.VMEM((FF, D), bf16),
            pltpu.VMEM((STATE_ROWS, CH), f32),
            pltpu.SemaphoreType.DMA((3,)),
        ],
        [SMEM] + [VMEM] * (8 + len(parts)) + [ANY] * sum(ns),
        [place, qkv, ph, u, vecs["out_bias"], vecs["gain2"], vecs["shift2"], vecs["up_bias"]]
        + [vecs["down_bias"]]
        + list(parts)
        + wo.arrays
        + wu.arrays
        + wd.arrays,
        2 * t * D * (D + 2 * FF) + 6 * t * H * CH * CH,
    )


def back_mlp_kernel(ws, ns, place, g, gp, r, o, inv, ph, gain, *rest):
    wo, wu, wd = ws
    no, nu, nd = ns
    ro, ru, rd = rest[:no], rest[no : no + nu], rest[no + nu : no + nu + nd]
    dz, dr, drb, gs, es, dst, s_dz, s_g, s_dr, s_sh, s_gn, wov, wuv, wdv, tmp, sems = rest[
        no + nu + nd :
    ]
    wd.issue(rd, wdv, sems.at[2], place)
    wu.issue(ru, wuv, sems.at[1], place)
    wo.issue(ro, wov, sems.at[0], place)
    t = g.shape[0]
    finish(wdv, sems.at[2])

    def hid_col(j):
        cols = span(j, TILE)
        part = (nt(g[...], wdv[cols, :]) * gp[:, cols]).astype(bf16)
        dz[:, cols] = part
        s_dz[:, cols] = jnp.sum(part.astype(f32), 0, keepdims=True)

    loop(FF // TILE, hid_col)
    finish(wuv, sems.at[1])

    def n2_col(j):
        cols = span(j, TILE)
        tmp[:, cols] = nt(dz[...], wuv[cols, :])

    loop(D // TILE, n2_col)
    for ref in (s_g, s_dr, s_sh, s_gn):
        ref[...] = jnp.zeros(ref.shape, f32)

    def norm(i):
        rows = span(i, CH)
        xh, rstd = standardize(r[rows, :])
        dn = tmp[rows, :]
        s_sh[...] += jnp.sum(dn, 0, keepdims=True)
        s_gn[...] += jnp.sum(dn * xh, 0, keepdims=True)
        dx = dn * gain[...]
        back = rstd * (
            dx - jnp.mean(dx, -1, keepdims=True) - xh * jnp.mean(dx * xh, -1, keepdims=True)
        )
        up = g[rows, :].astype(f32)
        total = up + back
        s_g[...] += jnp.sum(up, 0, keepdims=True)
        s_dr[...] += jnp.sum(total, 0, keepdims=True)
        dr[rows, :] = total
        drb[rows, :] = total.astype(bf16)

    loop(t // CH, norm)
    finish(wov, sems.at[0])

    def do_col(j):
        cols = span(j, TILE)
        gs[:, cols] = (nt(drb[...], wov[cols, :]) * inv[:, cols]).astype(bf16)

    loop(D // TILE, do_col)
    lane = lanes(t)
    low = lane < HEAD

    def pair(p):
        cols = span(p, CH)
        gv = gs[:, cols]
        prod = gv.astype(f32) * o[:, cols]
        e0 = -jnp.sum(jnp.where(low, prod, 0.0), -1, keepdims=True)
        e1 = -jnp.sum(jnp.where(low, 0.0, prod), -1, keepdims=True)
        swapped = jnp.where(low, e1, e0)
        es[:, cols] = swapped
        for hh in range(2):
            ge = with_error(gv, swapped, lane, hh)
            full = tn(ge, ph[:, span(2 * p + hh, CH)])
            dst[span(2 * p + hh, HEAD), :] = full[hh * HEAD : (hh + 1) * HEAD]
            at = HEAD * (1 - hh)
            dst[pl.ds(D + 2 * p + hh, 1), :] = full[at : at + 1] + full[at + 1 : at + 2]

    loop(PAIRS, pair)
    dst[D + H :, :] = jnp.zeros((STATE_ROWS - D - H, CH), f32)


def with_error(gv, swapped, lane, hh):
    first = HEAD * (1 - hh)
    hi = swapped.astype(bf16)
    lo = (swapped - hi.astype(f32)).astype(bf16)
    own = (lane < HEAD) if hh == 0 else (lane >= HEAD)
    zero = jnp.zeros_like(gv)
    spare = jnp.where(lane == first + 1, lo, jnp.where((lane == first) | (lane == first + 2), hi, zero))
    return jnp.where(own, gv, spare)


def with_ones(v, lane, hh):
    first = HEAD * (1 - hh)
    own = (lane < HEAD) if hh == 0 else (lane >= HEAD)
    spare = jnp.where((lane == first) | (lane == first + 1), jnp.ones_like(v), jnp.zeros_like(v))
    return jnp.where(own, v, spare)


def with_totals(s, tot, row, hh, again):
    first = HEAD * (1 - hh)
    hi = tot.astype(bf16).astype(f32)
    lo = tot - hi
    own = (row < HEAD) if hh == 0 else (row >= HEAD)
    if again:
        spare = jnp.where(
            (row == first) | (row == first + 1), hi, jnp.where(row == first + 2, lo, 0.0)
        )
    else:
        spare = jnp.where(row == first, hi, jnp.where(row == first + 1, lo, 0.0))
    return jnp.where(own, s, spare).astype(bf16)


def back_mlp(layer, place, g, gp, r, o, inv, ph, vecs, wo, wu, wd):
    t = g.shape[0]
    ws = (wo, wu, wd)
    ns = tuple(len(w.arrays) for w in ws)
    return call(
        functools.partial(back_mlp_kernel, ws, ns),
        [
            shape((t, FF), bf16),
            shape((t, D), f32),
            shape((t, D), bf16),
            shape((t, D), bf16),
            shape((t, D), f32),
            shape((STATE_ROWS, CH), f32),
            shape((1, FF), f32),
            shape((1, D), f32),
            shape((1, D), f32),
            shape((1, D), f32),
            shape((1, D), f32),
        ],
        [
            pltpu.VMEM((D, D), bf16),
            pltpu.VMEM((D, FF), bf16),
            pltpu.VMEM((FF, D), bf16),
            pltpu.VMEM((t, D), f32),
            pltpu.SemaphoreType.DMA((3,)),
        ],
        [SMEM] + [VMEM] * 7 + [ANY] * sum(ns),
        [place, g, gp, r, o, inv, ph, vecs["gain2"]] + wo.arrays + wu.arrays + wd.arrays,
        2 * t * D * (D + 2 * FF),
    )


def back_mix_kernel(w, nw, nf, nb, place, qkv, ph, gs, es, u, dr, gain, bd, *rest):
    firsts, lasts, rest = rest[:nf], rest[nf : nf + nb], rest[nf + nb :]
    refs, rest = rest[:nw], rest[nw:]
    dqkv, du, mg, s_q, s_sh, s_gn, wv, s0, s1, tmp, sem = rest
    w.issue(refs, wv, sem, place)
    t = u.shape[0]
    nc = t // CH
    sum_states(s0, firsts)
    sum_states(s1, lasts)
    lane = lanes(CH)
    low = lane < HEAD
    row = lax.broadcasted_iota(jnp.int32, (CH, CH), 0)
    tril = row >= lane
    triu = row <= lane

    def pair(p):
        cols = span(p, CH)
        vcols = pl.ds(pl.multiple_of(2 * D + p * CH, CH), CH)
        kcols = pl.ds(pl.multiple_of(D + p * CH, CH), CH)
        before = []
        s = s0[cols, :]
        tot = [s0[pl.ds(D + 2 * p + hh, 1), :] for hh in range(2)]
        for c in range(nc):
            rows = pl.ds(c * CH, CH)
            before.append([with_totals(s, tot[hh], row, hh, True) for hh in range(2)])
            if c < nc - 1:
                v = qkv[rows, vcols]
                new = []
                for hh in range(2):
                    k = ph[rows, pl.ds(pl.multiple_of((H + 2 * p + hh) * CH, CH), CH)]
                    new.append(tn(v, k)[hh * HEAD : (hh + 1) * HEAD])
                    tot[hh] = tot[hh] + jnp.sum(k.astype(f32), 0, keepdims=True)
                s = s + jnp.concatenate(new, 0)
        ds = s1[cols, :]
        dtot = [s1[pl.ds(D + 2 * p + hh, 1), :] for hh in range(2)]
        acc_q = jnp.zeros((CH, 2 * CH), f32)
        acc_k = jnp.zeros((CH, 2 * CH), f32)
        sums = [jnp.zeros((1, CH), f32) for _ in range(3)]
        for c in reversed(range(nc)):
            rows = pl.ds(c * CH, CH)
            v = qkv[rows, vcols]
            gv = gs[rows, cols]
            ev = es[rows, cols]
            dsl = ds.astype(bf16)
            dl_q, dl_k, dv, new = [], [], [], []
            for hh in range(2):
                q = ph[rows, span(2 * p + hh, CH)]
                k = ph[rows, pl.ds(pl.multiple_of((H + 2 * p + hh) * CH, CH), CH)]
                ge = with_error(gv, ev, lane, hh)
                v1 = with_ones(v, lane, hh)
                after = with_totals(ds, dtot[hh], row, hh, False)
                da = jnp.where(tril, nt(ge, v1), 0.0).astype(bf16)
                dat = jnp.where(triu, nt(v1, ge), 0.0).astype(bf16)
                at = jnp.where(triu, nt(k, q), 0.0).astype(bf16)
                dq = nn(da, k) + nn(ge, before[c][hh])
                dk = nn(dat, q) + nn(v1, after)
                dv.append(nn(at, gv) + nt(k, dsl))
                for p_, d_, to in ((q, dq, dl_q), (k, dk, dl_k)):
                    pf = p_.astype(f32)
                    to.append((pf * (d_ - half_sums(pf * d_, low))).astype(bf16))
                full = tn(ge, q)
                new.append(full[hh * HEAD : (hh + 1) * HEAD])
                first = HEAD * (1 - hh)
                dtot[hh] = dtot[hh] + full[first : first + 1] + full[first + 1 : first + 2]
            ds = ds + jnp.concatenate(new, 0)
            dl_q = jnp.concatenate(dl_q, 1)
            dl_k = jnp.concatenate(dl_k, 1)
            acc_q = acc_q + tn(qkv[rows, cols], dl_q)
            acc_k = acc_k + tn(qkv[rows, kcols], dl_k)
            parts = (
                (cols, nt(dl_q, bd[p])),
                (kcols, nt(dl_k, bd[PAIRS + p])),
                (vcols, jnp.where(low, dv[0], dv[1])),
            )
            for i, (where, val) in enumerate(parts):
                val = val.astype(bf16)
                dqkv[rows, where] = val
                sums[i] = sums[i] + jnp.sum(val.astype(f32), 0, keepdims=True)
        for where, val in zip((cols, kcols, vcols), sums):
            s_q[:, where] = val
        for which, acc in enumerate((acc_q, acc_k)):
            for hh in range(2):
                blk = acc[hh * HEAD : (hh + 1) * HEAD, hh * CH : (hh + 1) * CH]
                mg[which * H + 2 * p + hh] = blk - pltpu.roll(blk, HEAD, 1)

    loop(PAIRS, pair)
    finish(wv, sem)

    def n1_col(j):
        cols = span(j, TILE)
        tmp[:, cols] = nt(dqkv[...], wv[cols, :])

    loop(D // TILE, n1_col)
    s_sh[...] = jnp.zeros(s_sh.shape, f32)
    s_gn[...] = jnp.zeros(s_gn.shape, f32)

    def norm(i):
        rows = span(i, CH)
        xh, rstd = standardize(u[rows, :].astype(f32))
        dn = tmp[rows, :]
        s_sh[...] += jnp.sum(dn, 0, keepdims=True)
        s_gn[...] += jnp.sum(dn * xh, 0, keepdims=True)
        dx = dn * gain[...]
        back = rstd * (
            dx - jnp.mean(dx, -1, keepdims=True) - xh * jnp.mean(dx * xh, -1, keepdims=True)
        )
        du[rows, :] = (dr[rows, :] + back).astype(bf16)

    loop(nc, norm)


def back_mix(layer, place, qkv, ph, gs, es, u, dr, vecs, bd, firsts, lasts, w):
    t = u.shape[0]
    nw = len(w.arrays)
    return call(
        functools.partial(back_mix_kernel, w, nw, len(firsts), len(lasts)),
        [
            shape((t, 3 * D), bf16),
            shape((t, D), bf16),
            shape((2 * H, HEAD, CH), f32),
            shape((1, 3 * D), f32),
            shape((1, D), f32),
            shape((1, D), f32),
        ],
        [
            pltpu.VMEM((D, 3 * D), bf16),
            pltpu.VMEM((STATE_ROWS, CH), f32),
            pltpu.VMEM((STATE_ROWS, CH), f32),
            pltpu.VMEM((t, D), f32),
            pltpu.SemaphoreType.DMA,
        ],
        [SMEM] + [VMEM] * (8 + len(firsts) + len(lasts)) + [ANY] * nw,
        [place, qkv, ph, gs, es, u, dr, vecs["gain1"], bd]
        + list(firsts)
        + list(lasts)
        + w.arrays,
        2 * t * D * 3 * D + 14 * t * H * CH * CH,
    )


def grad_tiles(lhs, rhs, place, other, width, put):
    d = place[1]
    base = jnp.where(d == 0, other, 1 - other) * width
    rows = lhs.shape[1]
    step = D if rows == D else 512
    tile = width if rows != D else (384 if width % 384 == 0 else 128)
    for i in range(rows // step):
        for j in range(width // tile):
            cols = pl.ds(pl.multiple_of(base + j * tile, CH), tile)
            put(pl.ds(i * step, step), pl.ds(j * tile, tile), tn(lhs[:, i * step : (i + 1) * step], rhs[:, cols]))


def grad_send_kernel(place, lhs, rhs, out):
    def put(rows, cols, val):
        out[rows, cols] = val.astype(bf16)

    grad_tiles(lhs, rhs, place, 1, out.shape[1], put)


def grad_send(place, lhs, rhs):
    rows, cols = lhs.shape[1], rhs.shape[1] // 2
    return call(
        grad_send_kernel,
        [shape((rows, cols), bf16)],
        [],
        [SMEM, VMEM, VMEM],
        [place, lhs, rhs],
        2 * lhs.shape[0] * rows * cols,
    )[0]


def grad_keep_kernel(place, lhs, rhs, got, keep, send, buf, sem):
    def put(rows, cols, val):
        buf[rows, cols] = (val + got[rows, cols].astype(f32)).astype(bf16)

    grad_tiles(lhs, rhs, place, 0, buf.shape[1], put)
    nz, r = keep.shape[:2]
    y = place[3]
    copies = []
    for i in range(nz):
        for out, yy in ((send, 1 - y), (keep, y)):
            row = pl.multiple_of((i * 2 + yy) * r, r)
            copies.append(pltpu.make_async_copy(buf.at[pl.ds(row, r), :], out.at[i], sem))
    for copy in copies:
        copy.start()
    finish(buf, sem)


def grad_keep(place, lhs, rhs, got, nz):
    rows, cols = got.shape
    half = shape((nz, rows // nz // 2, cols), bf16)
    return call(
        grad_keep_kernel,
        [half, half],
        [pltpu.VMEM((rows, cols), bf16), pltpu.SemaphoreType.DMA],
        [SMEM, VMEM, VMEM, VMEM],
        [place, lhs, rhs, got],
        2 * lhs.shape[0] * rows * cols,
        [ANY, ANY],
    )


def shards(inputs, cotangent, *weights):
    n = lax.axis_size("seq")
    nz = n // 2
    group = n // 4
    x, d, j = (lax.axis_index(a) for a in AXES)
    z, y = j // 2, j % 2
    i_seq, jj = j // group, j % group
    place = jnp.stack([x, d, z, y]).astype(jnp.int32)
    t = 4 * CH

    def move(value, rule):
        pairs = []
        for xx in range(2):
            for dd in range(2):
                for k in range(n):
                    to = rule(xx, dd, k)
                    if to is not None:
                        pairs.append(((xx * 2 + dd) * n + k, (to[0] * 2 + to[1]) * n + to[2]))
        return lax.ppermute(value, AXES, pairs)

    def swap_x(value):
        return move(value, lambda xx, dd, k: (1 - xx, dd, k))

    def swap_d(value):
        return move(value, lambda xx, dd, k: (xx, 1 - dd, k))

    def swap_y(value):
        return move(value, lambda xx, dd, k: (xx, dd, k ^ 1))

    def shift_z(value, o):
        return move(value, lambda xx, dd, k: (xx, dd, (k + 2 * o) % n))

    def spread(own, y_last):
        zs = jnp.stack([own] + [shift_z(own, o) for o in range(1, nz)])
        ys = swap_y(zs)
        xs = swap_x(zs)
        xys = swap_y(xs) if y_last else swap_x(ys)
        return zs, ys, xs, xys

    def halved(w):
        width = w.shape[1] // 2
        return lax.dynamic_slice_in_dim(w, d * width, width, 1).astype(bf16)

    def with_cores(arrays):
        return [piece for a in arrays for piece in (a, swap_d(a))]

    qkv_w, out_w, up_w, down_w, map_w, bias_w, gain_w = (w[0] for w in weights)
    rows = [w.shape[0] for w in (qkv_w, out_w, up_w, down_w, map_w, bias_w, gain_w)]
    whole = rows[0] % 16 != 0

    def collect(source):
        mine = lax.dynamic_index_in_dim(source, x, 1, False)
        got = []
        for s in range(4):
            part = lax.dynamic_index_in_dim(mine, (j + s) % 4, 0, False)
            got.append(move(part, lambda xx, dd, k, s=s: (xx, dd, ((k + s) % 4) * group + k // 4)))
        ring = jnp.stack(got[::-1] + got[::-1])
        return lax.dynamic_slice_in_dim(ring, 3 - i_seq, 4, 0).reshape(t, D)

    small = jnp.concatenate([map_w.reshape(-1), bias_w, gain_w]).astype(bf16)
    unit = small.shape[0]
    padded = -(-unit // 2048) * 2048
    small = jnp.pad(small, (0, padded - unit)).reshape(-1, CH)
    zs, ys, xs, xys = spread(small, False)
    tokens = collect(inputs)

    def in_order(a, b):
        both = jnp.stack([a, b], 1)
        both = jnp.where(y == 0, both, both[:, ::-1])
        both = both[::-1]
        both = lax.dynamic_slice_in_dim(jnp.concatenate([both, both]), nz - 1 - z, nz, 0)
        return both.reshape(n, padded)[:, :unit]

    near, far = in_order(zs, ys), in_order(xs, xys)
    smalls = (jnp.where(x == 0, near, far), jnp.where(x == 0, far, near))

    if whole:
        everything = [
            lax.all_gather(
                lax.all_gather(w.astype(bf16), "seq", axis=0, tiled=True), "section", axis=0
            )
            for w in (qkv_w, out_w, up_w, down_w)
        ]

        def weight_set(layer):
            return [Weight([w[layer]], layer) for w in everything]

    else:
        g_qkv = with_cores(spread(halved(qkv_w), True))
        g_mid = with_cores(
            spread(jnp.concatenate([halved(out_w), halved(up_w)], 1), False)
        )
        g_down = with_cores(spread(halved(down_w), True))

        def weight_set(layer):
            return [
                Weight(g_qkv, layer, 0, 3 * D // 2),
                Weight(g_mid, layer, 0, D // 2),
                Weight(g_mid, layer, D // 2, FF // 2),
                Weight(g_down, layer, 0, D // 2),
            ]

    sets = [weight_set(0), weight_set(1)]

    def unpack(flat):
        m, b, g = rows[4] * HEAD, rows[5], rows[6]
        maps = flat[:, :m].reshape(2 * H, HEAD, HEAD)
        vec = flat[:, m : m + b].reshape(1, -1).astype(f32)
        gains = flat[:, m + b : m + b + g].reshape(1, -1).astype(f32)
        signed = jnp.concatenate([maps, -maps], -1).reshape(2 * PAIRS, 2, HEAD, CH)
        zero = jnp.zeros_like(signed[:, 0])
        bd = jnp.concatenate(
            [
                jnp.concatenate([signed[:, 0], zero], -1),
                jnp.concatenate([zero, signed[:, 1]], -1),
            ],
            1,
        )
        names = ("shift1", "qkv_bias", "out_bias", "shift2", "up_bias", "down_bias")
        sizes = (D, 3 * D, D, D, FF, D)
        vecs, at = {}, 0
        for name, size in zip(names, sizes):
            vecs[name] = vec[:, at : at + size]
            at += size
        vecs["gain1"], vecs["gain2"] = gains[:, :D], gains[:, D:]
        return vecs, bd

    params = [unpack(flat) for flat in smalls]

    members = 2 * group

    def others(value, sign):
        def rule(o):
            def to(xx, dd, k):
                place_ = xx * group + k % group + sign * o
                if not 0 <= place_ < members:
                    return None
                return (place_ // group, dd, (k // group) * group + place_ % group)

            return to

        return [move(value, rule(o)) for o in range(1, members)]

    u = tokens
    kept = []
    for layer in range(2):
        vecs, bd = params[layer]
        wq, wo, wu, wd = sets[layer]
        a, qkv, ph, st = project(layer, place, u, vecs, bd, wq)
        firsts = others(st, 1)
        o, inv, ob, r, n2, hid, gp, res = mix(layer, place, qkv, ph, u, vecs, firsts, wo, wu, wd)
        kept.append((u, a, qkv, ph, firsts, o, inv, ob, r, n2, hid, gp, res))
        u = res

    def reduce_grad(lhs, rhs, layer):
        send = grad_send(place, lhs, rhs)
        keep, send = grad_keep(place, lhs, rhs, swap_d(send), 1 if whole else nz)
        if whole:
            both = jnp.stack([keep[0], send[0]])
            both = jnp.where(y == 0, both, both[::-1]).reshape(nz, 2, -1, keep.shape[-1])
            keep = jnp.where(y == 0, both[:, 0], both[:, 1])
            send = jnp.where(y == 0, both[:, 1], both[:, 0])
        return after_core(keep, send, layer)

    def after_core(keep, send, layer):
        kind = keep.dtype
        part = (keep.astype(f32) + swap_y(send).astype(f32)).astype(kind)
        total = lax.dynamic_index_in_dim(part, z, 0, False).astype(f32)
        for o in range(1, nz):
            piece = lax.dynamic_index_in_dim(part, (z + o) % nz, 0, False)
            total = total + shift_z(piece, o).astype(f32)
        got = move(
            total.astype(kind), lambda xx, dd, k: (layer, dd, k) if xx == 1 - layer else None
        )
        return total + got.astype(f32)

    def joined(part):
        other = swap_d(part)
        return jnp.where(
            d == 0,
            jnp.concatenate([part, other], 1),
            jnp.concatenate([other, part], 1),
        )

    g = collect(cotangent)
    results = [None, None]
    input_grads = [None, None]
    for layer in (1, 0):
        vecs, bd = params[layer]
        wq, wo, wu, wd = sets[layer]
        u, a, qkv, ph, firsts, o, inv, ob, r, n2, hid, gp, res = kept[layer]
        dz, dr, drb, gs, es, dst, s_dz, s_g, s_dr, s_sh2, s_gn2 = back_mlp(
            layer, place, g, gp, r, o, inv, ph, vecs, wo, wu, wd
        )
        lasts = others(dst, -1)
        g_down = reduce_grad(hid, g, layer)
        g_up = reduce_grad(n2, dz, layer)
        g_out = reduce_grad(ob, drb, layer)
        dqkv, du, mg, s_q, s_sh1, s_gn1 = back_mix(
            layer, place, qkv, ph, gs, es, u, dr, vecs, bd, firsts, lasts, wq
        )
        g_qkv_ = reduce_grad(a, dqkv, layer)
        bias = jnp.concatenate([s_sh1, s_q, s_dr, s_sh2, s_dz, s_g], 1).reshape(n, -1)
        gain = jnp.concatenate([s_gn1, s_gn2], 1).reshape(n, -1)
        flat = jnp.concatenate([mg[:, :, :HEAD].reshape(n, -1), bias, gain], 1)
        flat = jnp.pad(flat, ((0, 0), (0, padded - unit))).reshape(nz, 2, -1, CH)
        flat = flat + swap_d(flat)
        pair = jnp.where(y == 0, flat, flat[:, ::-1])
        small_grad = after_core(pair[:, 0], pair[:, 1], layer)
        results[layer] = (g_qkv_, g_out, g_up, g_down, small_grad)
        input_grads[layer] = du
        g = du

    def deliver(pair):
        own = jnp.where(x == 0, pair[0], pair[1]).reshape(4, CH, D)
        other = jnp.where(x == 0, pair[1], pair[0]).reshape(4, CH, D)
        halves = []
        for flip, source in enumerate((own, other)):
            got = []
            for s in range(4):
                part = lax.dynamic_index_in_dim(source, (i_seq + s) % 4, 0, False)

                def rule(xx, dd, k, s=s, flip=flip):
                    return (xx ^ flip, dd, (k % group) * 4 + (k // group + s) % 4)

                got.append(move(part, rule))
            ring = jnp.stack(got[::-1] + got[::-1])
            halves.append(lax.dynamic_slice_in_dim(ring, 3 - j % 4, 4, 0))
        micro = [jnp.where(x == 0, halves[0], halves[1]), jnp.where(x == 0, halves[1], halves[0])]
        return jnp.stack(micro, 1)[None]

    layer_out = deliver((kept[0][-1], kept[1][-1]))
    grads_out = deliver(input_grads)
    final = [jnp.where(x == 0, p, q) for p, q in zip(results[0], results[1])]
    mats = [joined(m)[None] for m in final[:4]]
    flat = final[4].reshape(1, -1)
    m, b = rows[4] * HEAD, rows[5]
    return (
        layer_out,
        grads_out,
        mats[0],
        mats[1],
        mats[2],
        mats[3],
        flat[:, :m].reshape(1, rows[4], HEAD),
        flat[:, m : m + b],
        flat[:, m + b : unit],
    )


def solution(mesh):
    tokens = P("dp", None, "seq", None)
    matrix = P("section", "seq", None)
    vector = P("section", "seq")
    stacked = P("section", "dp", None, "seq", None)
    return jax.shard_map(
        shards,
        mesh=mesh,
        in_specs=(tokens, tokens) + (matrix,) * 5 + (vector,) * 2,
        out_specs=(stacked, stacked) + (matrix,) * 5 + (vector,) * 2,
        check_vma=False,
    )
```

time: 3410 us -> 1040 us (0.30)
  waiting for transfers between devices: 1460 us -> 393 us
  blocking collectives: 541 us -> 0 us
  local copies, waits for them, and re-layouts: 543 us -> 53.3 us
  matrix products: 439 us -> 0 us
  other arithmetic: 360 us -> 37.4 us
  Pallas kernels: 0 us -> 295 us
  starting transfers between devices: 16.6 us -> 249 us
    all_gather x10 -> x0, waiting for transfers between devices: 548 us -> none  [the longest x6 337 us: carried_in(): gathered = jax.tree.map(lambda a: lax.all_gather(a, axis), part)]
    reduce_scatter x4 -> x0, waiting for transfers between devices: 524 us -> none  [the longest x1 166 us: reduce_grads(): lax.psum_scatter(g_down, 'seq', scatter_dimension=1, tiled=True)]
    dot_general x102 -> x0, matrix products: 418 us -> none  [the longest x54 195 us: precise(): jnp.einsum(pattern, left_side, right_side, precision=MAXIMUM_ACCURACY)]
    ppermute x6 -> x136, waiting for transfers between devices: 0.02 us -> 393 us  [move(): return lax.ppermute(value, AXES, pairs)]
    psum x7 -> x0, blocking collectives: 306 us -> none  [the longest x3 154 us: attend_back(): overall = lax.psum((state_sum, total_sum), 'seq')]
    pallas_call x0 -> x24, Pallas kernels: none -> 295 us  [call(): pl.pallas_call(kernel, out_shape=outs, in_specs=specs, out_specs=out_spec...]
    ppermute x6 -> x136, starting transfers between devices: 15.9 us -> 249 us  [move(): return lax.ppermute(value, AXES, pairs)]
    unnamed x15 -> x0, waiting for transfers between devices: 220 us -> none
  transfers between devices with their start and end apart: 30 -> 136, of which waited for: 23 -> 59; matrix products, arithmetic and copies ran while one was open for 27% -> 8% of each run, Pallas kernels for 0% -> 18%
where the time goes in v1:
time: 1040 us; the launch traced here: 1030 us
  waiting for transfers between devices  393 us (38%)
  Pallas kernels  295 us (28%)
  starting transfers between devices  249 us (24%)
  local copies, waits for them, and re-layouts  53.3 us (5%)
  other arithmetic  37.4 us (4%)
    ppermute x136, waiting for transfers between devices, move(): return lax.ppermute(value, AXES, pairs)  393 us
    pallas_call x24, Pallas kernels, call(): pl.pallas_call(kernel, out_shape=outs, in_specs=specs, out_specs=out_spec...  295 us
    ppermute x136, starting transfers between devices, move(): return lax.ppermute(value, AXES, pairs)  249 us
  transfers between devices with their start and end apart: 136, of which 59 were waited for; matrix products, arithmetic and copies ran while one was open for 8% of the time, Pallas kernels for 18%

profile of v1, /device:TPU:13, one launch (start us, length us, event | category | flops | bytes accessed | tf_op | source)
XLA Modules:
  0.0 1030.2 jit_solution(16509745185008820293)
XLA Ops:
  34.1 11.3 %collective-permute-start.3 = (bf16[128,768]{1,0:T(8,128)(2,1)}, bf16[128,768]{1,0:T(8,128)(2,1)S(1)}, u32[]{:S(2)}, u32[]{:S(2)}) collective-permute-start(bf16[128,768]{1,0:T(8,128)(2,1)} %get-tuple-element.178), channel_id=1, source_target_pairs={{0,0},{1,2},{2,4},{3,6},{4,1},{5,3},{6,5},{7,7},{8,8},{9,10},{10,1... | collective-permute-start | bytes 589832 | tf_op jit(solution)/shard_map/ppermute | solution.py:668
  45.6 6.0 collective-permute-done.3
  62.6 24.4 %collective-permute-done.54 = bf16[128,768]{1,0:T(8,128)(2,1)S(1)} collective-permute-done((bf16[128,768]{1,0:T(8,128)(2,1)S(1)}, bf16[128,768]{1,0:T(8,128)(2,1)S(1)}, u32[]{:S(2)}, u32[]{:S(2)}) %collective-permute-start.54) | collective-permute-done | bytes 196640 | tf_op jit(solution)/shard_map/ppermute | solution.py:668
  90.3 5.7 collective-permute-done.56
  109.9 14.3 %collective-permute-done.34 = bf16[384,384]{1,0:T(8,128)(2,1)S(1)} collective-permute-done((bf16[384,384]{1,0:T(8,128)(2,1)S(1)}, bf16[384,384]{1,0:T(8,128)(2,1)S(1)}, u32[]{:S(2)}, u32[]{:S(2)}) %collective-permute-start.34) | collective-permute-done | bytes 294944 | tf_op jit(solution)/shard_map/ppermute | solution.py:668
  129.1 8.7 collective-permute-start.39
  144.1 21.3 %collective-permute-done.39.rest_23_.rest_20_ = bf16[4,384,384]{2,1,0:T(8,128)(2,1)} collective-permute-done((bf16[4,384,384]{2,1,0:T(8,128)(2,1)}, bf16[4,384,384]{2,1,0:T(8,128)(2,1)}, u32[]{:S(2)}, u32[]{:S(2)}) %collective-permute-start.39) | collective-permute-done | bytes 1179680 | tf_op jit(solution)/shard_map/ppermute | solution.py:668
  166.8 14.5 %collective-permute-done.37.rest_21_.rest_18_ = bf16[4,384,384]{2,1,0:T(8,128)(2,1)} collective-permute-done((bf16[4,384,384]{2,1,0:T(8,128)(2,1)}, bf16[4,384,384]{2,1,0:T(8,128)(2,1)}, u32[]{:S(2)}, u32[]{:S(2)}) %collective-permute-start.37) | collective-permute-done | bytes 1179680 | tf_op jit(solution)/shard_map/ppermute | solution.py:668
  190.3 6.7 collective-permute-done.29.rest_7_.rest_15_.rest_4_.rest_12_
  200.2 7.0 collective-permute-start.40
  211.9 15.2 %collective-permute-done.41.rest_25_.rest_22_ = bf16[4,384,384]{2,1,0:T(8,128)(2,1)} collective-permute-done((bf16[4,384,384]{2,1,0:T(8,128)(2,1)}, bf16[4,384,384]{2,1,0:T(8,128)(2,1)}, u32[]{:S(2)}, u32[]{:S(2)}) %collective-permute-start.41) | collective-permute-done | bytes 1179680 | tf_op jit(solution)/shard_map/ppermute | solution.py:668
  231.9 29.8 %shard_map.160 = (bf16[512,768]{1,0:T(8,128)(2,1)}, bf16[512,2304]{1,0:T(8,128)(2,1)}, bf16[512,3072]{1,0:T(8,128)(2,1)}, f32[784,128]{1,0:T(8,128)}) custom-call(s32[4]{0:T(128)} %pad_add_fusion.place, bf16[512,768]{1,0:T(8,128)(2,1)} %bitcast.354, f32[1,768]{1,0:T(1,128)} %get-tuple-element.255.gain, f32[1,768]{1,0:T(1,128)} %get-tuple-element.249.shift, ...), custom_call_target="tpu_custom_call" | custom-call | flops 1811939328 | bytes 15358992 | tf_op jit(solution)/shard_map/pallas_call | solution.py:93
  267.4 7.3 collective-permute-done.20.rest_0_
  279.3 5.7 collective-permute-done.21.rest_1_
  295.8 25.8 %shard_map.161 = (f32[512,768]{1,0:T(8,128)}, f32[512,768]{1,0:T(8,128)}, bf16[512,768]{1,0:T(8,128)(2,1)}, f32[512,768]{1,0:T(8,128)}, bf16[512,768]{1,0:T(8,12...) custom-call(s32[4]{0:T(128)} %pad_add_fusion.place, ...), custom_call_target="tpu_custom_call" | custom-call | flops 6039797760 | bytes 57065488 | tf_op jit(solution)/shard_map/pallas_call | solution.py:93
  321.6 29.9 %shard_map.162 = (bf16[512,768]{1,0:T(8,128)(2,1)}, bf16[512,2304]{1,0:T(8,128)(2,1)}, bf16[512,3072]{1,0:T(8,128)(2,1)}, f32[784,128]{1,0:T(8,128)}) custom-call(s32[4]{0:T(128)} %pad_add_fusion.place, bf16[512,768]{1,0:T(8,128)(2,1)} %get-tuple-element.86.u, f32[1,768]{1,0:T(1,128)} %get-tuple-element.253.gain, f32[1,768]{1,0:T(1,128)} %get-tuple-element.245.shift, ...), custom_call_target="tpu_custom_call" | custom-call | flops 1811939328 | bytes 15358992 | tf_op jit(solution)/shard_map/pallas_call | solution.py:93
  365.3 7.4 collective-permute-done.44.rest_1_
  373.5 25.6 %shard_map.163 = (f32[512,768]{1,0:T(8,128)}, f32[512,768]{1,0:T(8,128)}, bf16[512,768]{1,0:T(8,128)(2,1)}, f32[512,768]{1,0:T(8,128)}, bf16[512,768]{1,0:T(8,12...) custom-call(s32[4]{0:T(128)} %pad_add_fusion.place, ...), custom_call_target="tpu_custom_call" | custom-call | flops 6039797760 | bytes 57065488 | tf_op jit(solution)/shard_map/pallas_call | solution.py:93
  399.2 24.4 %shard_map.164 = (bf16[512,3072]{1,0:T(8,128)(2,1)}, f32[512,768]{1,0:T(8,128)}, bf16[512,768]{1,0:T(8,128)(2,1)}, bf16[512,768]{1,0:T(8,128)(2,1)}, f32[512,768...) custom-call(s32[4]{0:T(128)} %pad_add_fusion.place, ...), custom_call_target="tpu_custom_call" | custom-call | flops 5435817984 | bytes 56265744 | tf_op jit(solution)/shard_map/pallas_call | solution.py:93
  456.8 7.9 collective-permute-done.47
  469.4 7.7 collective-permute-done.48
  479.1 8.0 collective-permute-done.49
  487.2 6.2 collective-permute-done.50
  498.3 7.9 collective-permute-done.51
  506.1 8.3 collective-permute-start.52
  514.4 9.1 collective-permute-done.52
  523.5 8.2 collective-permute-done.53
  535.2 28.8 %shard_map.165 = (bf16[512,2304]{1,0:T(8,128)(2,1)}, bf16[512,768]{1,0:T(8,128)(2,1)}, f32[24,64,128]{2,1,0:T(8,128)}, f32[1,2304]{1,0:T(1,128)}, f32[1,768]{1,0:T(1,128)}, /*index=5*/f32[1,768]{1,0:T(1,128)}) custom-call(s32[4]{0:T(128)} %pad_add_fusion.place, bf16[512,2304]{1,0:T(8,128)(2,1)} %get-tuple-element.87.qkv, ...), custom_call_target="tpu_custom_call" | custom-call | flops 3221225472 | bytes 24446992 | tf_op jit(solution)/shard_map/pallas_call | solution.py:93
  564.1 24.3 %shard_map.166 = (bf16[512,3072]{1,0:T(8,128)(2,1)}, f32[512,768]{1,0:T(8,128)}, bf16[512,768]{1,0:T(8,128)(2,1)}, bf16[512,768]{1,0:T(8,128)(2,1)}, f32[512,768...) custom-call(s32[4]{0:T(128)} %pad_add_fusion.place, ...), custom_call_target="tpu_custom_call" | custom-call | flops 5435817984 | bytes 56265744 | tf_op jit(solution)/shard_map/pallas_call | solution.py:93
  618.4 28.8 %shard_map.167 = (bf16[512,2304]{1,0:T(8,128)(2,1)}, bf16[512,768]{1,0:T(8,128)(2,1)}, f32[24,64,128]{2,1,0:T(8,128)}, f32[1,2304]{1,0:T(1,128)}, f32[1,768]{1,0:T(1,128)}, /*index=5*/f32[1,768]{1,0:T(1,128)}) custom-call(s32[4]{0:T(128)} %pad_add_fusion.place, bf16[512,2304]{1,0:T(8,128)(2,1)} %get-tuple-element.83.qkv, ...), custom_call_target="tpu_custom_call" | custom-call | flops 3221225472 | bytes 24446992 | tf_op jit(solution)/shard_map/pallas_call | solution.py:93
  681.4 6.5 collective-permute-done.64
  694.2 13.6 %collective-permute-done.66 = bf16[128,768]{1,0:T(8,128)(2,1)S(1)} collective-permute-done((bf16[128,768]{1,0:T(8,128)(2,1)}, bf16[128,768]{1,0:T(8,128)(2,1)S(1)}, u32[]{:S(2)}, u32[]{:S(2)}) %collective-permute-start.66) | collective-permute-done | bytes 196640 | tf_op jit(solution)/shard_map/ppermute | solution.py:668
  707.8 8.9 collective-permute-start.68
  722.5 7.6 collective-permute-done.69
  730.1 5.7 collective-permute-start.71
  736.5 8.3 collective-permute-done.70
  745.5 5.9 collective-permute-start.86
  819.6 6.2 shard_map.183
  825.8 6.1 shard_map.179
  844.2 6.2 shard_map.181
  851.1 6.1 shard_map.177
  865.5 17.7 %collective-permute-done.118 = bf16[4,384,384]{2,1,0:T(8,128)(2,1)S(1)} collective-permute-done((bf16[4,384,384]{2,1,0:T(8,128)(2,1)}, bf16[4,384,384]{2,1,0:T(8,128)(2,1)S(1)}, u32[]{:S(2)}, u32[]{:S(2)}) %collective-permute-start.118) | collective-permute-done | bytes 1179680 | tf_op jit(solution)/shard_map/ppermute | solution.py:668
  883.7 24.8 %collective-permute-done.105 = bf16[4,96,1536]{2,1,0:T(8,128)(2,1)S(1)} collective-permute-done((bf16[4,96,1536]{2,1,0:T(8,128)(2,1)}, bf16[4,96,1536]{2,1,0:T(8,128)(2,1)S(1)}, u32[]{:S(2)}, u32[]{:S(2)}) %collective-permute-start.105) | collective-permute-done | bytes 1179680 | tf_op jit(solution)/shard_map/ppermute | solution.py:668
  916.5 13.3 %collective-permute-done.120 = bf16[384,384]{1,0:T(8,128)(2,1)S(1)} collective-permute-done((bf16[384,384]{1,0:T(8,128)(2,1)S(1)}, bf16[384,384]{1,0:T(8,128)(2,1)S(1)}, u32[]{:S(2)}, u32[]{:S(2)}) %collective-permute-start.120) | collective-permute-done | bytes 294944 | tf_op jit(solution)/shard_map/ppermute | solution.py:668
  929.9 12.6 %collective-permute-done.121 = bf16[384,384]{1,0:T(8,128)(2,1)S(1)} collective-permute-done((bf16[384,384]{1,0:T(8,128)(2,1)S(1)}, bf16[384,384]{1,0:T(8,128)(2,1)S(1)}, u32[]{:S(2)}, u32[]{:S(2)}) %collective-permute-start.121) | collective-permute-done | bytes 294944 | tf_op jit(solution)/shard_map/ppermute | solution.py:668
  959.3 9.0 collective-permute-done.99
  971.7 9.2 collective-permute-done.114
  985.0 13.3 %collective-permute-done.115 = bf16[384,384]{1,0:T(8,128)(2,1)S(1)} collective-permute-done((bf16[384,384]{1,0:T(8,128)(2,1)S(1)}, bf16[384,384]{1,0:T(8,128)(2,1)S(1)}, u32[]{:S(2)}, u32[]{:S(2)}) %collective-permute-start.115) | collective-permute-done | bytes 294944 | tf_op jit(solution)/shard_map/ppermute | solution.py:668
  (590 shorter events, 409.3 us)
Async XLA Ops:
  8.9 42.7 %collective-permute-start.10 = (bf16[96,1152]{1,0:T(8,128)(2,1)}, bf16[96,1152]{1,0:T(8,128)(2,1)}, u32[]{:S(2)}, u32[]{:S(2)}) collective-permute-start(bf16[96,1152]{1,0:T(8,128)(2,1)} %fusion.55), channel_id=1, source_target_pairs={{0,2},{1,3},{2,4},{3,5},{4,6},{5,7},{6,0},{7,1},{8,10},{9,11},{10,... | collective-permute-start | bytes 663560 | tf_op jit(solution)/shard_map/ppermute | solution.py:668
  9.0 44.6 %collective-permute-start.11 = (bf16[96,1152]{1,0:T(8,128)(2,1)}, bf16[96,1152]{1,0:T(8,128)(2,1)}, u32[]{:S(2)}, u32[]{:S(2)}) collective-permute-start(bf16[96,1152]{1,0:T(8,128)(2,1)} %fusion.55), channel_id=1, source_target_pairs={{0,4},{1,5},{2,6},{3,7},{4,0},{5,1},{6,2},{7,3},{8,12},{9,13},{10,... | collective-permute-start | bytes 663560 | tf_op jit(solution)/shard_map/ppermute | solution.py:668
  20.3 36.3 %collective-permute-start.12 = (bf16[96,1152]{1,0:T(8,128)(2,1)}, bf16[96,1152]{1,0:T(8,128)(2,1)S(1)}, u32[]{:S(2)}, u32[]{:S(2)}) collective-permute-start(bf16[96,1152]{1,0:T(8,128)(2,1)} %fusion.55), channel_id=1, source_target_pairs={{0,6},{1,7},{2,0},{3,1},{4,2},{5,3},{6,4},{7,5},{8,14},{9,15},{10,... | collective-permute-start | bytes 663560 | tf_op jit(solution)/shard_map/ppermute | solution.py:668
  45.5 50.6 %collective-permute-start.23 = (bf16[96,1920]{1,0:T(8,128)(2,1)S(1)}, bf16[96,1920]{1,0:T(8,128)(2,1)S(1)}, u32[]{:S(2)}, u32[]{:S(2)}) collective-permute-start(bf16[96,1920]{1,0:T(8,128)(2,1)S(1)} %copy-done.32), channel_id=1, source_target_pairs={{0,2},{1,3},{2,4},{3,5},{4,6},{5,7},{6,0},{7,1},{8,10},{9,11},{10,... | collective-permute-start | bytes 1105928 | tf_op jit(solution)/shard_map/ppermute | solution.py:668
  51.5 48.6 %collective-permute-start.24 = (bf16[96,1920]{1,0:T(8,128)(2,1)S(1)}, bf16[96,1920]{1,0:T(8,128)(2,1)S(1)}, u32[]{:S(2)}, u32[]{:S(2)}) collective-permute-start(bf16[96,1920]{1,0:T(8,128)(2,1)S(1)} %copy-done.32), channel_id=1, source_target_pairs={{0,4},{1,5},{2,6},{3,7},{4,0},{5,1},{6,2},{7,3},{8,12},{9,13},{10,... | collective-permute-start | bytes 1105928 | tf_op jit(solution)/shard_map/ppermute | solution.py:668
  51.6 35.5 %collective-permute-start.54 = (bf16[128,768]{1,0:T(8,128)(2,1)S(1)}, bf16[128,768]{1,0:T(8,128)(2,1)S(1)}, u32[]{:S(2)}, u32[]{:S(2)}) collective-permute-start(bf16[128,768]{1,0:T(8,128)(2,1)S(1)} %copy-done.50), channel_id=1, source_target_pairs={{0,6},{1,0},{2,2},{3,4},{4,7},{5,1},{6,3},{7,5},{8,14},{9,8},{10,1... | collective-permute-start | bytes 589832 | tf_op jit(solution)/shard_map/ppermute | solution.py:668
  53.6 35.4 %collective-permute-start.55 = (bf16[128,768]{1,0:T(8,128)(2,1)S(1)}, bf16[128,768]{1,0:T(8,128)(2,1)S(1)}, u32[]{:S(2)}, u32[]{:S(2)}) collective-permute-start(bf16[128,768]{1,0:T(8,128)(2,1)S(1)} %copy-done.49), channel_id=1, source_target_pairs={{0,4},{1,6},{2,0},{3,2},{4,5},{5,7},{6,1},{7,3},{8,12},{9,14},{10,... | collective-permute-start | bytes 589832 | tf_op jit(solution)/shard_map/ppermute | solution.py:668
  60.5 40.8 %collective-permute-start.25 = (bf16[96,1920]{1,0:T(8,128)(2,1)S(1)}, bf16[96,1920]{1,0:T(8,128)(2,1)S(1)}, u32[]{:S(2)}, u32[]{:S(2)}) collective-permute-start(bf16[96,1920]{1,0:T(8,128)(2,1)S(1)} %copy-done.32), channel_id=1, source_target_pairs={{0,6},{1,7},{2,0},{3,1},{4,2},{5,3},{6,4},{7,5},{8,14},{9,15},{10,... | collective-permute-start | bytes 1105928 | tf_op jit(solution)/shard_map/ppermute | solution.py:668
  89.0 49.2 %collective-permute-start.16 = (bf16[4,96,1152]{2,1,0:T(8,128)(2,1)}, bf16[4,96,1152]{2,1,0:T(8,128)(2,1)}, u32[]{:S(2)}, u32[]{:S(2)}) collective-permute-start(bf16[4,96,1152]{2,1,0:T(8,128)(2,1)} %pad_maximum_fusion.2.rest_0_.rest_6_), channel_id=1, source_target_pairs={{0,16},{1,17},{2,18},{3,19},{4,20},{5,21},{6,22},{7,23},{8,24},{9,... | collective-permute-start | bytes 2654216 | tf_op jit(solution)/shard_map/ppermute | solution.py:668
  100.1 38.7 %collective-permute-start.14 = (bf16[4,96,1152]{2,1,0:T(8,128)(2,1)}, bf16[4,96,1152]{2,1,0:T(8,128)(2,1)}, u32[]{:S(2)}, u32[]{:S(2)}) collective-permute-start(bf16[4,96,1152]{2,1,0:T(8,128)(2,1)} %pad_maximum_fusion.2.rest_0_.rest_6_), channel_id=1, source_target_pairs={{0,1},{1,0},{2,3},{3,2},{4,5},{5,4},{6,7},{7,6},{8,9},{9,8},{10,11... | collective-permute-start | bytes 2654216 | tf_op jit(solution)/shard_map/ppermute | solution.py:668
  124.3 63.0 %collective-permute-start.27 = (bf16[4,96,1920]{2,1,0:T(8,128)(2,1)S(1)}, bf16[4,96,1920]{2,1,0:T(8,128)(2,1)S(1)}, u32[]{:S(2)}, u32[]{:S(2)}) collective-permute-start(bf16[4,96,1920]{2,1,0:T(8,128)(2,1)S(1)} %pad_maximum_fusion.rest_3_.rest_11_.rest_0_.rest_8_), channel_id=1, source_target_pairs={{0,1},{1,0},{2,3},{3,2},{4,5},{5,4},{6,7},{7,6},{8,9},{9,8},{10,11... | collective-permute-start | bytes 4423688 | tf_op jit(solution)/shard_map/ppermute | solution.py:668
  129.1 36.3 %collective-permute-start.39 = (bf16[4,384,384]{2,1,0:T(8,128)(2,1)}, bf16[4,384,384]{2,1,0:T(8,128)(2,1)}, u32[]{:S(2)}, u32[]{:S(2)}) collective-permute-start(bf16[4,384,384]{2,1,0:T(8,128)(2,1)} %pad_maximum_fusion.1.rest_19_.rest_16_), channel_id=1, source_target_pairs={{0,16},{1,17},{2,18},{3,19},{4,20},{5,21},{6,22},{7,23},{8,24},{9,... | collective-permute-start | bytes 3538952 | tf_op jit(solution)/shard_map/ppermute | solution.py:668
  137.9 43.4 %collective-permute-start.37 = (bf16[4,384,384]{2,1,0:T(8,128)(2,1)}, bf16[4,384,384]{2,1,0:T(8,128)(2,1)}, u32[]{:S(2)}, u32[]{:S(2)}) collective-permute-start(bf16[4,384,384]{2,1,0:T(8,128)(2,1)} %pad_maximum_fusion.1.rest_19_.rest_16_), channel_id=1, source_target_pairs={{0,1},{1,0},{2,3},{3,2},{4,5},{5,4},{6,7},{7,6},{8,9},{9,8},{10,11... | collective-permute-start | bytes 3538952 | tf_op jit(solution)/shard_map/ppermute | solution.py:668
  138.2 45.3 %collective-permute-start.36 = (bf16[4,384,384]{2,1,0:T(8,128)(2,1)}, bf16[4,384,384]{2,1,0:T(8,128)(2,1)}, u32[]{:S(2)}, u32[]{:S(2)}) collective-permute-start(bf16[4,384,384]{2,1,0:T(8,128)(2,1)} %pad_maximum_fusion.1.rest_19_.rest_16_), channel_id=1, source_target_pairs={{0,8},{1,9},{2,10},{3,11},{4,12},{5,13},{6,14},{7,15},{8,0},{9,1},... | collective-permute-start | bytes 3538952 | tf_op jit(solution)/shard_map/ppermute | solution.py:668
  142.9 54.1 %collective-permute-start.29 = (bf16[4,96,1920]{2,1,0:T(8,128)(2,1)S(1)}, bf16[4,96,1920]{2,1,0:T(8,128)(2,1)}, u32[]{:S(2)}, u32[]{:S(2)}) collective-permute-start(bf16[4,96,1920]{2,1,0:T(8,128)(2,1)S(1)} %pad_maximum_fusion.rest_3_.rest_11_.rest_0_.rest_8_), channel_id=1, source_target_pairs={{0,16},{1,17},{2,18},{3,19},{4,20},{5,21},{6,22},{7,23},{8,24},{9,... | collective-permute-start | bytes 4423688 | tf_op jit(solution)/shard_map/ppermute | solution.py:668
  165.4 33.2 %collective-permute-start.26 = (bf16[4,96,1920]{2,1,0:T(8,128)(2,1)S(1)}, bf16[4,96,1920]{2,1,0:T(8,128)(2,1)}, u32[]{:S(2)}, u32[]{:S(2)}) collective-permute-start(bf16[4,96,1920]{2,1,0:T(8,128)(2,1)S(1)} %pad_maximum_fusion.rest_3_.rest_11_.rest_0_.rest_8_), channel_id=1, source_target_pairs={{0,8},{1,9},{2,10},{3,11},{4,12},{5,13},{6,14},{7,15},{8,0},{9,1},... | collective-permute-start | bytes 4423688 | tf_op jit(solution)/shard_map/ppermute | solution.py:668
  197.0 33.0 %collective-permute-start.31 = (bf16[4,96,1920]{2,1,0:T(8,128)(2,1)S(1)}, bf16[4,96,1920]{2,1,0:T(8,128)(2,1)}, u32[]{:S(2)}, u32[]{:S(2)}) collective-permute-start(bf16[4,96,1920]{2,1,0:T(8,128)(2,1)S(1)} %collective-permute-done.27.rest_5_.rest_13_.rest_2_.rest_10_), channel_id=1, source_target_pairs={{0,16},{1,17},{2,18},{3,19},{4,20},{5,21},{6,22},{7,23},{8,24},{9,... | collective-permute-start | bytes 4423688 | tf_op jit(solution)/shard_map/ppermute | solution.py:668
  200.2 61.5 %collective-permute-start.40 = (bf16[4,384,384]{2,1,0:T(8,128)(2,1)}, bf16[4,384,384]{2,1,0:T(8,128)(2,1)}, u32[]{:S(2)}, u32[]{:S(2)}) collective-permute-start(bf16[4,384,384]{2,1,0:T(8,128)(2,1)} %collective-permute-done.39.rest_23_.rest_20_), channel_id=1, source_target_pairs={{0,8},{1,9},{2,10},{3,11},{4,12},{5,13},{6,14},{7,15},{8,0},{9,1},... | collective-permute-start | bytes 3538952 | tf_op jit(solution)/shard_map/ppermute | solution.py:668
  207.3 57.8 %collective-permute-start.38 = (bf16[4,384,384]{2,1,0:T(8,128)(2,1)}, bf16[4,384,384]{2,1,0:T(8,128)(2,1)}, u32[]{:S(2)}, u32[]{:S(2)}) collective-permute-start(bf16[4,384,384]{2,1,0:T(8,128)(2,1)} %collective-permute-done.37.rest_21_.rest_18_), channel_id=1, source_target_pairs={{0,8},{1,9},{2,10},{3,11},{4,12},{5,13},{6,14},{7,15},{8,0},{9,1},... | collective-permute-start | bytes 3538952 | tf_op jit(solution)/shard_map/ppermute | solution.py:668
  227.1 67.6 %collective-permute-start.28 = (bf16[4,96,1920]{2,1,0:T(8,128)(2,1)S(1)}, bf16[4,96,1920]{2,1,0:T(8,128)(2,1)S(1)}, u32[]{:S(2)}, u32[]{:S(2)}) collective-permute-start(bf16[4,96,1920]{2,1,0:T(8,128)(2,1)S(1)} %collective-permute-done.27.rest_5_.rest_13_.rest_2_.rest_10_), channel_id=1, source_target_pairs={{0,8},{1,9},{2,10},{3,11},{4,12},{5,13},{6,14},{7,15},{8,0},{9,1},... | collective-permute-start | bytes 4423688 | tf_op jit(solution)/shard_map/ppermute | solution.py:668
  229.7 65.0 %collective-permute-start.30 = (bf16[4,96,1920]{2,1,0:T(8,128)(2,1)}, bf16[4,96,1920]{2,1,0:T(8,128)(2,1)}, u32[]{:S(2)}, u32[]{:S(2)}) collective-permute-start(bf16[4,96,1920]{2,1,0:T(8,128)(2,1)} %collective-permute-done.29.rest_7_.rest_15_.rest_4_.rest_12_), channel_id=1, source_target_pairs={{0,8},{1,9},{2,10},{3,11},{4,12},{5,13},{6,14},{7,15},{8,0},{9,1},... | collective-permute-start | bytes 4423688 | tf_op jit(solution)/shard_map/ppermute | solution.py:668
  230.1 64.6 %collective-permute-start.32 = (bf16[4,96,1920]{2,1,0:T(8,128)(2,1)}, bf16[4,96,1920]{2,1,0:T(8,128)(2,1)}, u32[]{:S(2)}, u32[]{:S(2)}) collective-permute-start(bf16[4,96,1920]{2,1,0:T(8,128)(2,1)} %collective-permute-done.31.rest_9_.rest_17_.rest_6_.rest_14_), channel_id=1, source_target_pairs={{0,8},{1,9},{2,10},{3,11},{4,12},{5,13},{6,14},{7,15},{8,0},{9,1},... | collective-permute-start | bytes 4423688 | tf_op jit(solution)/shard_map/ppermute | solution.py:668
  423.6 111.6 %collective-permute-start.58 = (f32[784,128]{1,0:T(8,128)}, f32[784,128]{1,0:T(8,128)}, u32[]{:S(2)}, u32[]{:S(2)}) collective-permute-start(f32[784,128]{1,0:T(8,128)} %get-tuple-element.98), channel_id=1, source_target_pairs={{1,0},{3,2},{5,4},{7,6},{9,8},{11,10},{13,12},{15,14},{16,1},{17,1... | collective-permute-start | bytes 1204232 | tf_op jit(solution)/shard_map/ppermute | solution.py:668
  428.9 106.2 %collective-permute-start.59 = (f32[784,128]{1,0:T(8,128)}, f32[784,128]{1,0:T(8,128)}, u32[]{:S(2)}, u32[]{:S(2)}) collective-permute-start(f32[784,128]{1,0:T(8,128)} %get-tuple-element.98), channel_id=1, source_target_pairs={{16,0},{17,1},{18,2},{19,3},{20,4},{21,5},{22,6},{23,7},{24,8},{25... | collective-permute-start | bytes 1204232 | tf_op jit(solution)/shard_map/ppermute | solution.py:668
  430.2 104.9 %collective-permute-start.60 = (f32[784,128]{1,0:T(8,128)}, f32[784,128]{1,0:T(8,128)}, u32[]{:S(2)}, u32[]{:S(2)}) collective-permute-start(f32[784,128]{1,0:T(8,128)} %get-tuple-element.98), channel_id=1, source_target_pairs={{17,0},{19,2},{21,4},{23,6},{25,8},{27,10},{29,12},{31,14}} | collective-permute-start | bytes 1204232 | tf_op jit(solution)/shard_map/ppermute | solution.py:668
  437.1 375.8 %collective-permute-start.117 = (bf16[3072,384]{1,0:T(8,128)(2,1)}, bf16[3072,384]{1,0:T(8,128)(2,1)S(1)}, u32[]{:S(2)}, u32[]{:S(2)}) collective-permute-start(bf16[3072,384]{1,0:T(8,128)(2,1)} %shard_map.182), channel_id=1, source_target_pairs={{0,8},{1,9},{2,10},{3,11},{4,12},{5,13},{6,14},{7,15},{8,0},{9,1},... | collective-permute-start | bytes 7077896 | tf_op jit(solution)/shard_map/ppermute | solution.py:668
  531.8 83.0 %collective-permute-start.91 = (bf16[768,384]{1,0:T(8,128)(2,1)}, bf16[768,384]{1,0:T(8,128)(2,1)}, u32[]{:S(2)}, u32[]{:S(2)}) collective-permute-start(bf16[768,384]{1,0:T(8,128)(2,1)} %shard_map.174), channel_id=1, source_target_pairs={{0,8},{1,9},{2,10},{3,11},{4,12},{5,13},{6,14},{7,15},{8,0},{9,1},... | collective-permute-start | bytes 1769480 | tf_op jit(solution)/shard_map/ppermute | solution.py:668
  614.8 46.7 %collective-permute-start.130 = (f32[4,2,112,128]{3,2,0,1:T(8,128)}, f32[4,2,112,128]{3,2,0,1:T(8,128)}, u32[]{:S(2)}, u32[]{:S(2)}) collective-permute-start(f32[4,2,112,128]{3,2,0,1:T(8,128)} %copy.38), channel_id=1, source_target_pairs={{0,8},{1,9},{2,10},{3,11},{4,12},{5,13},{6,14},{7,15},{8,0},{9,1},... | collective-permute-start | bytes 1376264 | tf_op jit(solution)/shard_map/ppermute | solution.py:668
  618.1 58.0 %collective-permute-start.85 = (bf16[768,384]{1,0:T(8,128)(2,1)}, bf16[768,384]{1,0:T(8,128)(2,1)}, u32[]{:S(2)}, u32[]{:S(2)}) collective-permute-start(bf16[768,384]{1,0:T(8,128)(2,1)} %shard_map.172), channel_id=1, source_target_pairs={{0,8},{1,9},{2,10},{3,11},{4,12},{5,13},{6,14},{7,15},{8,0},{9,1},... | collective-permute-start | bytes 1769480 | tf_op jit(solution)/shard_map/ppermute | solution.py:668
  618.4 44.2 %collective-permute-start.92 = (bf16[4,96,384]{2,1,0:T(8,128)(2,1)}, bf16[4,96,384]{2,1,0:T(8,128)(2,1)}, u32[]{:S(2)}, u32[]{:S(2)}) collective-permute-start(bf16[4,96,384]{2,1,0:T(8,128)(2,1)} %get-tuple-element.124), channel_id=1, source_target_pairs={{0,1},{1,0},{2,3},{3,2},{4,5},{5,4},{6,7},{7,6},{8,9},{9,8},{10,11... | collective-permute-start | bytes 884744 | tf_op jit(solution)/shard_map/ppermute | solution.py:668
  667.0 139.4 %collective-permute-start.78 = (bf16[768,1152]{1,0:T(8,128)(2,1)}, bf16[768,1152]{1,0:T(8,128)(2,1)}, u32[]{:S(2)}, u32[]{:S(2)}) collective-permute-start(bf16[768,1152]{1,0:T(8,128)(2,1)} %shard_map.170), channel_id=1, source_target_pairs={{0,8},{1,9},{2,10},{3,11},{4,12},{5,13},{6,14},{7,15},{8,0},{9,1},... | collective-permute-start | bytes 5308424 | tf_op jit(solution)/shard_map/ppermute | solution.py:668
  669.5 82.7 %collective-permute-start.124 = (f32[4,2,112,128]{3,2,0,1:T(8,128)}, f32[4,2,112,128]{3,2,0,1:T(8,128)}, u32[]{:S(2)}, u32[]{:S(2)}) collective-permute-start(f32[4,2,112,128]{3,2,0,1:T(8,128)} %copy.36), channel_id=1, source_target_pairs={{0,8},{1,9},{2,10},{3,11},{4,12},{5,13},{6,14},{7,15},{8,0},{9,1},... | collective-permute-start | bytes 1376264 | tf_op jit(solution)/shard_map/ppermute | solution.py:668
  776.2 49.6 %collective-permute-start.104 = (bf16[768,1536]{1,0:T(8,128)(2,1)}, bf16[768,1536]{1,0:T(8,128)(2,1)}, u32[]{:S(2)}, u32[]{:S(2)}) collective-permute-start(bf16[768,1536]{1,0:T(8,128)(2,1)} %shard_map.178), channel_id=1, source_target_pairs={{0,8},{1,9},{2,10},{3,11},{4,12},{5,13},{6,14},{7,15},{8,0},{9,1},... | collective-permute-start | bytes 7077896 | tf_op jit(solution)/shard_map/ppermute | solution.py:668
  797.8 34.2 %collective-permute-start.72 = (bf16[768,1152]{1,0:T(8,128)(2,1)}, bf16[768,1152]{1,0:T(8,128)(2,1)}, u32[]{:S(2)}, u32[]{:S(2)}) collective-permute-start(bf16[768,1152]{1,0:T(8,128)(2,1)} %shard_map.168), channel_id=1, source_target_pairs={{0,8},{1,9},{2,10},{3,11},{4,12},{5,13},{6,14},{7,15},{8,0},{9,1},... | collective-permute-start | bytes 5308424 | tf_op jit(solution)/shard_map/ppermute | solution.py:668
  804.9 38.9 %collective-permute-start.111 = (bf16[3072,384]{1,0:T(8,128)(2,1)}, bf16[3072,384]{1,0:T(8,128)(2,1)}, u32[]{:S(2)}, u32[]{:S(2)}) collective-permute-start(bf16[3072,384]{1,0:T(8,128)(2,1)} %shard_map.180), channel_id=1, source_target_pairs={{0,8},{1,9},{2,10},{3,11},{4,12},{5,13},{6,14},{7,15},{8,0},{9,1},... | collective-permute-start | bytes 7077896 | tf_op jit(solution)/shard_map/ppermute | solution.py:668
  806.4 43.9 %collective-permute-start.98 = (bf16[768,1536]{1,0:T(8,128)(2,1)}, bf16[768,1536]{1,0:T(8,128)(2,1)}, u32[]{:S(2)}, u32[]{:S(2)}) collective-permute-start(bf16[768,1536]{1,0:T(8,128)(2,1)} %shard_map.176), channel_id=1, source_target_pairs={{0,8},{1,9},{2,10},{3,11},{4,12},{5,13},{6,14},{7,15},{8,0},{9,1},... | collective-permute-start | bytes 7077896 | tf_op jit(solution)/shard_map/ppermute | solution.py:668
  850.4 32.8 %collective-permute-start.118 = (bf16[4,384,384]{2,1,0:T(8,128)(2,1)}, bf16[4,384,384]{2,1,0:T(8,128)(2,1)S(1)}, u32[]{:S(2)}, u32[]{:S(2)}) collective-permute-start(bf16[4,384,384]{2,1,0:T(8,128)(2,1)} %get-tuple-element.138), channel_id=1, source_target_pairs={{0,1},{1,0},{2,3},{3,2},{4,5},{5,4},{6,7},{7,6},{8,9},{9,8},{10,11... | collective-permute-start | bytes 3538952 | tf_op jit(solution)/shard_map/ppermute | solution.py:668
  857.3 51.2 %collective-permute-start.105 = (bf16[4,96,1536]{2,1,0:T(8,128)(2,1)}, bf16[4,96,1536]{2,1,0:T(8,128)(2,1)S(1)}, u32[]{:S(2)}, u32[]{:S(2)}) collective-permute-start(bf16[4,96,1536]{2,1,0:T(8,128)(2,1)} %get-tuple-element.132), channel_id=1, source_target_pairs={{0,1},{1,0},{2,3},{3,2},{4,5},{5,4},{6,7},{7,6},{8,9},{9,8},{10,11... | collective-permute-start | bytes 3538952 | tf_op jit(solution)/shard_map/ppermute | solution.py:668
  864.0 46.3 %collective-permute-start.74 = (bf16[96,1152]{1,0:T(8,128)(2,1)S(1)}, bf16[96,1152]{1,0:T(8,128)(2,1)S(1)}, u32[]{:S(2)}, u32[]{:S(2)}) collective-permute-start(bf16[96,1152]{1,0:T(8,128)(2,1)S(1)} %get-tuple-element.194), channel_id=1, source_target_pairs={{0,2},{1,3},{2,4},{3,5},{4,6},{5,7},{6,0},{7,1},{8,10},{9,11},{10,... | collective-permute-start | bytes 663560 | tf_op jit(solution)/shard_map/ppermute | solution.py:668
  864.0 48.2 %collective-permute-start.75 = (bf16[96,1152]{1,0:T(8,128)(2,1)S(1)}, bf16[96,1152]{1,0:T(8,128)(2,1)S(1)}, u32[]{:S(2)}, u32[]{:S(2)}) collective-permute-start(bf16[96,1152]{1,0:T(8,128)(2,1)S(1)} %get-tuple-element.196), channel_id=1, source_target_pairs={{0,4},{1,5},{2,6},{3,7},{4,0},{5,1},{6,2},{7,3},{8,12},{9,13},{10,... | collective-permute-start | bytes 663560 | tf_op jit(solution)/shard_map/ppermute | solution.py:668
  864.1 48.1 %collective-permute-start.76 = (bf16[96,1152]{1,0:T(8,128)(2,1)S(1)}, bf16[96,1152]{1,0:T(8,128)(2,1)S(1)}, u32[]{:S(2)}, u32[]{:S(2)}) collective-permute-start(bf16[96,1152]{1,0:T(8,128)(2,1)S(1)} %get-tuple-element.195), channel_id=1, source_target_pairs={{0,6},{1,7},{2,0},{3,1},{4,2},{5,3},{6,4},{7,5},{8,14},{9,15},{10,... | collective-permute-start | bytes 663560 | tf_op jit(solution)/shard_map/ppermute | solution.py:668
  911.1 44.4 %collective-permute-start.112 = (bf16[4,384,384]{2,1,0:T(8,128)(2,1)S(1)}, bf16[4,384,384]{2,1,0:T(8,128)(2,1)S(1)}, u32[]{:S(2)}, u32[]{:S(2)}) collective-permute-start(bf16[4,384,384]{2,1,0:T(8,128)(2,1)S(1)} %copy-done.70), channel_id=1, source_target_pairs={{0,1},{1,0},{2,3},{3,2},{4,5},{5,4},{6,7},{7,6},{8,9},{9,8},{10,11... | collective-permute-start | bytes 3538952 | tf_op jit(solution)/shard_map/ppermute | solution.py:668
  912.3 35.5 %collective-permute-start.106 = (bf16[96,1536]{1,0:T(8,128)(2,1)S(1)}, bf16[96,1536]{1,0:T(8,128)(2,1)S(1)}, u32[]{:S(2)}, u32[]{:S(2)}) collective-permute-start(bf16[96,1536]{1,0:T(8,128)(2,1)S(1)} %get-tuple-element.191), channel_id=1, source_target_pairs={{0,2},{1,3},{2,4},{3,5},{4,6},{5,7},{6,0},{7,1},{8,10},{9,11},{10,... | collective-permute-start | bytes 884744 | tf_op jit(solution)/shard_map/ppermute | solution.py:668
  913.7 40.4 %collective-permute-start.107 = (bf16[96,1536]{1,0:T(8,128)(2,1)S(1)}, bf16[96,1536]{1,0:T(8,128)(2,1)S(1)}, u32[]{:S(2)}, u32[]{:S(2)}) collective-permute-start(bf16[96,1536]{1,0:T(8,128)(2,1)S(1)} %get-tuple-element.193), channel_id=1, source_target_pairs={{0,4},{1,5},{2,6},{3,7},{4,0},{5,1},{6,2},{7,3},{8,12},{9,13},{10,... | collective-permute-start | bytes 884744 | tf_op jit(solution)/shard_map/ppermute | solution.py:668
  968.7 33.8 %collective-permute-start.100 = (bf16[96,1536]{1,0:T(8,128)(2,1)S(1)}, bf16[96,1536]{1,0:T(8,128)(2,1)S(1)}, u32[]{:S(2)}, u32[]{:S(2)}) collective-permute-start(bf16[96,1536]{1,0:T(8,128)(2,1)S(1)} %get-tuple-element.188), channel_id=1, source_target_pairs={{0,2},{1,3},{2,4},{3,5},{4,6},{5,7},{6,0},{7,1},{8,10},{9,11},{10,... | collective-permute-start | bytes 884744 | tf_op jit(solution)/shard_map/ppermute | solution.py:668
  970.2 36.0 %collective-permute-start.101 = (bf16[96,1536]{1,0:T(8,128)(2,1)S(1)}, bf16[96,1536]{1,0:T(8,128)(2,1)S(1)}, u32[]{:S(2)}, u32[]{:S(2)}) collective-permute-start(bf16[96,1536]{1,0:T(8,128)(2,1)S(1)} %get-tuple-element.190), channel_id=1, source_target_pairs={{0,4},{1,5},{2,6},{3,7},{4,0},{5,1},{6,2},{7,3},{8,12},{9,13},{10,... | collective-permute-start | bytes 884744 | tf_op jit(solution)/shard_map/ppermute | solution.py:668
  970.2 40.8 %collective-permute-start.102 = (bf16[96,1536]{1,0:T(8,128)(2,1)S(1)}, bf16[96,1536]{1,0:T(8,128)(2,1)S(1)}, u32[]{:S(2)}, u32[]{:S(2)}) collective-permute-start(bf16[96,1536]{1,0:T(8,128)(2,1)S(1)} %get-tuple-element.189), channel_id=1, source_target_pairs={{0,6},{1,7},{2,0},{3,1},{4,2},{5,3},{6,4},{7,5},{8,14},{9,15},{10,... | collective-permute-start | bytes 884744 | tf_op jit(solution)/shard_map/ppermute | solution.py:668
  980.9 31.5 %collective-permute-start.122 = (bf16[384,384]{1,0:T(8,128)(2,1)S(1)}, bf16[384,384]{1,0:T(8,128)(2,1)S(1)}, u32[]{:S(2)}, u32[]{:S(2)}) collective-permute-start(bf16[384,384]{1,0:T(8,128)(2,1)S(1)} %fusion.32), channel_id=1, source_target_pairs={{0,16},{1,17},{2,18},{3,19},{4,20},{5,21},{6,22},{7,23},{8,24},{9,... | collective-permute-start | bytes 884744 | tf_op jit(solution)/shard_map/ppermute | solution.py:668
  (160 other events, 2865.1 us)

commit v2 on v0

--- a/solution.py
+++ b/solution.py
@@ -1,7 +1,13 @@
+import functools
+from typing import Any, NamedTuple
+
 import jax
 import jax.numpy as jnp
 from jax import lax
+from jax.experimental import pallas as pl
+from jax.experimental.pallas import tpu as pltpu
 from jax.sharding import PartitionSpec as P
+
 
 D = 768
 FF = 3072
@@ -347,7 +353,7 @@
     return lax.psum((s_qkv, s_out, s_up, s_down, s_map, s_bias, s_gain), "dp")
 
 
-def shards(
+def plain_shards(
     inputs, cotangent, qkv_weight, out_weight, up_weight, down_weight, map_weight, biases, gains
 ):
     section_index = lax.axis_index("section")
@@ -457,32 +463,1679 @@
     )
 
 
+CH = 128
+PAIRS = H // 2
+QB = 2 * H * HEAD
+STATE_ROWS = D + 16
+EPS = 1e-05
+TILE = 256
+AXES = ("section", "dp", "seq")
+MESH = pl.DeviceIdType.MESH
+f32 = jnp.float32
+bf16 = jnp.bfloat16
+GELU_C = 0.7978845608028654
+GELU_A = 0.044715
+SMALL_ROWS = 208
+VEC_ROWS = 72
+GAIN_ROWS = 16
+SHIFT1, QKV_BIAS, OUT_BIAS, SHIFT2, UP_BIAS, DOWN_BIAS = 0, 6, 24, 30, 36, 60
+
+
+class Kept(NamedTuple):
+    a: Any
+    qkv: Any
+    ph: Any
+    o: Any
+    inv: Any
+    ob: Any
+    r: Any
+    n2: Any
+    hid: Any
+    gp: Any
+    res: Any
+    pre: Any
+
+
+class ForwardRefs(NamedTuple):
+    tokens: Any
+    cot: Any
+    small: Any
+    wq: Any
+    wo: Any
+    wu: Any
+    wd: Any
+    gq: Any
+    go: Any
+    gu: Any
+    gd: Any
+    lay: Any
+    gv: Any
+    bd: Any
+    tok_out: Any
+    cot_out: Any
+
+
+class ForwardScratch(NamedTuple):
+    tok: Any
+    sm: Any
+    vec: Any
+    st: Any
+    got: Any
+    vq: Any
+    vo: Any
+    vu: Any
+    vd: Any
+    g_send: Any
+    g_recv: Any
+    g_local: Any
+    c_send: Any
+    c_recv: Any
+    s_send: Any
+    s_recv: Any
+    d_send: Any
+    d_recv: Any
+    w_sem: Any
+    o_sem: Any
+    m_sem: Any
+
+
+class Weights(NamedTuple):
+    q: Any
+    o: Any
+    u: Any
+    d: Any = None
+
+
+VMEM = pl.BlockSpec(memory_space=pltpu.VMEM)
+SMEM = pl.BlockSpec(memory_space=pltpu.SMEM)
+ANY = pl.BlockSpec(memory_space=pl.ANY)
+
+
+def nn(a, b):
+    return lax.dot_general(a, b, (((1,), (0,)), ((), ())), preferred_element_type=f32)
+
+
+def nt(a, b):
+    return lax.dot_general(a, b, (((1,), (1,)), ((), ())), preferred_element_type=f32)
+
+
+def tn(a, b):
+    return lax.dot_general(a, b, (((0,), (0,)), ((), ())), preferred_element_type=f32)
+
+
+def loop(count, body, events=None):
+    events = events or {}
+
+    def step(i, c):
+        body(i)
+        for at, event in events.items():
+
+            @pl.when(i == at)
+            def _():
+                event()
+
+        return c
+
+    lax.fori_loop(0, count, step, 0)
+
+
+def span(i, size):
+    return pl.ds(pl.multiple_of(i * size, size), size)
+
+
+def wide(ref, layer, row, count):
+    return jnp.concatenate([ref[layer, pl.ds(row + i, 1), :] for i in range(count)], 1)
+
+
+def finish(dst, sem):
+    pltpu.make_async_copy(dst, dst, sem).wait()
+
+
+def shape(dims, kind):
+    return jax.ShapeDtypeStruct(dims, kind)
+
+
+def call(kernel, outs, scratch, specs, args, flops, out_specs=None, vmem=60, cid=None):
+    if out_specs is None:
+        out_specs = [VMEM] * len(outs)
+    moved = sum(a.size * a.dtype.itemsize for a in args if a.ndim > 0)
+    moved += sum(o.size * o.dtype.itemsize for o in outs)
+    params = dict(vmem_limit_bytes=vmem * 1024 * 1024)
+    if cid is not None:
+        params.update(collective_id=cid, has_side_effects=True)
+    return pl.pallas_call(
+        kernel,
+        out_shape=outs,
+        in_specs=specs,
+        out_specs=out_specs,
+        scratch_shapes=scratch,
+        compiler_params=pltpu.CompilerParams(**params),
+        cost_estimate=pl.CostEstimate(flops=flops, bytes_accessed=moved, transcendentals=0),
+    )(*args)
+
+
+def standardize(u):
+    cen = u - jnp.mean(u, -1, keepdims=True)
+    rstd = lax.rsqrt(jnp.mean(cen * cen, -1, keepdims=True) + EPS)
+    return cen * rstd, rstd
+
+
+def lanes(rows):
+    return lax.broadcasted_iota(jnp.int32, (rows, CH), 1)
+
+
+def half_sums(t, low):
+    s1 = jnp.sum(jnp.where(low, t, 0.0), -1, keepdims=True)
+    s2 = jnp.sum(jnp.where(low, 0.0, t), -1, keepdims=True)
+    return jnp.where(low, s1, s2)
+
+
+def half_softmax(l, low):
+    m1 = jnp.max(jnp.where(low, l, -jnp.inf), -1, keepdims=True)
+    m2 = jnp.max(jnp.where(low, -jnp.inf, l), -1, keepdims=True)
+    p = jnp.exp(l - jnp.where(low, m1, m2))
+    return p / half_sums(p, low)
+
+
+class Place:
+    def __init__(self, n):
+        self.n, self.nz, self.group = n, n // 2, n // 4
+        self.x = lax.axis_index("section")
+        self.d = lax.axis_index("dp")
+        self.j = lax.axis_index("seq")
+        self.z, self.y = lax.div(self.j, 2), lax.rem(self.j, 2)
+        self.i = lax.div(self.j, self.group)
+        self.jj = lax.rem(self.j, self.group)
+        self.r = self.x * self.group + self.jj
+
+    def at(self, x=None, d=None, z=None, y=None, j=None):
+        x = self.x if x is None else x
+        d = self.d if d is None else d
+        if j is None:
+            j = (self.z if z is None else z) * 2 + (self.y if y is None else y)
+        return (x, d, j)
+
+    def zpos(self, o):
+        return lax.rem(self.z + o + self.nz, self.nz)
+
+    def meet(self):
+        barrier = pltpu.get_barrier_semaphore()
+        for dx in range(2):
+            for o in range(self.n):
+                if dx == 0 and o == 0:
+                    continue
+                other = (
+                    lax.rem(self.x + dx, 2),
+                    self.d,
+                    lax.rem(self.j + o, self.n),
+                )
+                pl.semaphore_signal(barrier, inc=1, device_id=other, device_id_type=MESH)
+        pl.semaphore_signal(
+            barrier, inc=1, device_id=(self.x, 1 - self.d, self.j), device_id_type=MESH
+        )
+        pl.semaphore_wait(barrier, 2 * self.n)
+
+
+def remote(src, dst, send, recv, to):
+    return pltpu.make_async_remote_copy(
+        src_ref=src, dst_ref=dst, send_sem=send, recv_sem=recv, device_id=to, device_id_type=MESH
+    )
+
+
+class Gather:
+    def __init__(self, place, src, buf, send, recv, local, y_last, halves=True):
+        self.p, self.src, self.buf = place, src, buf
+        self.send, self.recv, self.local = send, recv, local
+        self.y_last, self.halves = y_last, halves
+        self.width = src.shape[1]
+        self.sent = []
+
+    def columns(self):
+        if not self.halves:
+            return slice(None)
+        return pl.ds(pl.multiple_of(self.p.d * self.width, CH), self.width)
+
+    def shard(self, x, z, y):
+        return self.buf.at[x, z, y, :, self.columns()]
+
+    def column(self, x, y):
+        return self.buf.at[x, :, y, :, self.columns()]
+
+    def go(self, src, dst, slot, to):
+        remote(src, dst, self.send.at[slot], self.recv.at[slot], to).start()
+        self.sent.append(slot)
+
+    def got(self, ref, slot):
+        finish(ref, self.recv.at[slot])
+
+    def start(self):
+        p = self.p
+        own = self.shard(p.x, p.z, p.y)
+        pltpu.make_async_copy(self.src, own, self.local).start()
+        for o in range(1, p.nz):
+            self.go(self.src, own, o - 1, p.at(z=p.zpos(o)))
+
+    def first(self, o):
+        p = self.p
+        zi = p.zpos(-o)
+        here = self.shard(p.x, zi, p.y)
+        src = self.src if o == 0 else here
+        if o > 0:
+            self.got(here, o - 1)
+        self.go(src, here, 3 + o, p.at(y=1 - p.y))
+        self.go(src, here, 7 + o, p.at(x=1 - p.x))
+
+    def second(self, o):
+        p = self.p
+        zi = p.zpos(-o)
+        if self.y_last:
+            here = self.shard(1 - p.x, zi, p.y)
+            self.got(here, 7 + o)
+            self.go(here, here, 11 + o, p.at(y=1 - p.y))
+        else:
+            here = self.shard(p.x, zi, 1 - p.y)
+            self.got(here, 3 + o)
+            self.go(here, here, 11 + o, p.at(x=1 - p.x))
+
+    def core(self, q):
+        p = self.p
+        x = p.x if q < 2 else 1 - p.x
+        y = p.y if q % 2 == 0 else 1 - p.y
+        if q == 0:
+            own = self.shard(p.x, p.z, p.y)
+            finish(own, self.local)
+        elif q == 3 or q == (1 if self.y_last else 2):
+            base = 11 if q == 3 else (3 if self.y_last else 7)
+            for o in range(p.nz):
+                self.got(self.shard(x, p.zpos(-o), y), base + o)
+        if self.halves:
+            part = self.column(x, y)
+            self.go(part, part, 15 + q, p.at(d=1 - p.d))
+
+    def done(self):
+        p = self.p
+        if self.halves:
+            for q in range(4):
+                x = p.x if q < 2 else 1 - p.x
+                y = p.y if q % 2 == 0 else 1 - p.y
+                other = pl.ds(pl.multiple_of((1 - p.d) * self.width, CH), self.width)
+                self.got(self.buf.at[x, :, y, :, other], 15 + q)
+
+    def close(self):
+        p = self.p
+        for slot in self.sent:
+            ref = self.column(p.x, p.y) if slot >= 15 else self.shard(p.x, p.z, p.y)
+            finish(ref, self.send.at[slot])
+
+
+def forward_kernel(n, *refs):
+    ref = ForwardRefs(*refs[:16])
+    saved = [Kept(*refs[16:28]), Kept(*refs[28:40])]
+    v = Kept(*refs[40:52])
+    own = ForwardScratch(*refs[52:])
+    p = Place(n)
+    nz, group = p.nz, p.group
+    t = v.a.shape[0]
+    nc = t // CH
+    p.meet()
+
+    def gather(k, src, buf, y_last, halves=True):
+        return Gather(
+            p, src, buf, own.g_send.at[k], own.g_recv.at[k], own.g_local.at[k], y_last, halves
+        )
+
+    gs = gather(0, ref.small, own.sm, False, False)
+    gq = gather(1, ref.wq, ref.gq, True)
+    go = gather(2, ref.wo, ref.go, False)
+    gu = gather(3, ref.wu, ref.gu, False)
+    gd = gather(4, ref.wd, ref.gd, True)
+    gathers = (gs, gq, go, gu, gd)
+
+    def collect(which, s):
+        i = lax.rem(p.j + s, 4)
+        to = i * group + lax.div(p.j, 4)
+        slot = lax.rem(p.j, 4)
+        src = (ref.cot if which else ref.tokens).at[i, p.x]
+        dst = (ref.cot_out if which else own.tok).at[span(slot, CH), :]
+        send, recv = own.c_send.at[which], own.c_recv.at[which]
+        copy = remote(src, dst, send.at[s], recv.at[slot], p.at(j=to))
+
+        @pl.when(to != p.j)
+        def _():
+            copy.start()
+
+        @pl.when(to == p.j)
+        def _():
+            pltpu.make_async_copy(src, dst, recv.at[slot]).start()
+
+        def close():
+            @pl.when(to != p.j)
+            def _():
+                copy.wait_send()
+
+        return close
+
+    gs.start()
+    gs.first(0)
+    gq.start()
+    gq.first(0)
+    closing = [collect(0, s) for s in range(4)]
+    for o in range(1, nz):
+        gs.first(o)
+        gq.first(o)
+    go.start()
+    gu.start()
+    go.first(0)
+    gu.first(0)
+    for o in range(nz):
+        gs.second(o)
+    for o in range(nz):
+        gq.second(o)
+    for q in range(4):
+        gs.core(q)
+    for q in range(3):
+        gq.core(q)
+
+    vec, gv, bd, sm = own.vec, ref.gv, ref.bd, own.sm
+    vec[...] = jnp.zeros(vec.shape, f32)
+    gv[...] = jnp.zeros(gv.shape, f32)
+    bd[...] = jnp.zeros(bd.shape, bf16)
+    for layer in range(2):
+        for k in range(n):
+            part = sm[layer, k // 2, k % 2, 0:16, :].astype(f32)
+            row, grow = (33 * k) // 4, (3 * k) // 2
+            vec[layer, row : row + 9, :] += part[0:9]
+            gv[layer, grow : grow + 2, :] += part[9:11]
+        for head in range(2 * H):
+            k, at, odd = head // 3, 16 + (head % 3) * HEAD, head % 2
+            bd[layer, head // 2, odd * HEAD : (odd + 1) * HEAD, odd * CH : (odd + 1) * CH] = sm[
+                layer, k // 2, k % 2, at : at + HEAD, :
+            ]
+
+    for k in range(4):
+        finish(own.tok.at[pl.ds(k * CH, CH), :], own.c_recv.at[0, k])
+
+    def load(g, dst, layer, k):
+        pltpu.make_async_copy(g.buf.at[layer], dst, own.w_sem.at[k]).start()
+
+    def loaded(dst, k):
+        finish(dst, own.w_sem.at[k])
+
+    pending = [[], []]
+
+    def save(layer, *sources):
+        for src in sources:
+            k = [src is x for x in v].index(True)
+            if src is v.res:
+                src = src.at[layer]
+            copy = pltpu.make_async_copy(src, saved[layer][k], own.o_sem.at[layer, k])
+            copy.start()
+            pending[layer].append(copy)
+
+    flat = Weights(
+        own.vq.reshape(D, 3 * D),
+        own.vo.reshape(D, D),
+        own.vu.reshape(D, FF),
+        own.vd.reshape(FF, D),
+    )
+    low = lanes(CH) < HEAD
+    tril = lax.broadcasted_iota(jnp.int32, (CH, CH), 0) >= lanes(CH)
+
+    def norm_rows(layer, src, dst, which, shift):
+        gain = wide(gv, layer, which * 6, 6)
+        bias = wide(vec, layer, shift, 6)
+
+        def body(i):
+            xh, _ = standardize(src[span(i, CH), :].astype(f32))
+            dst[span(i, CH), :] = (xh * gain + bias).astype(bf16)
+
+        loop(nc, body)
+
+    def bias_cols(layer, at, j):
+        return wide(vec, layer, at + 2 * j, 2)
+
+    def project(layer, u, events):
+        a, qkv, ph, st = v.a, v.qkv, v.ph, own.st
+        if layer == 1:
+            for copy in pending[0]:
+                copy.wait()
+        norm_rows(layer, u, a, 0, SHIFT1)
+        loaded(own.vq, 0)
+        save(layer, v.a)
+
+        def column(j):
+            cols = span(j, TILE)
+            qkv[:, cols] = (
+                nn(a[...], flat.q[:, cols]) + bias_cols(layer, QKV_BIAS, j)
+            ).astype(bf16)
+
+        loop(3 * D // TILE, column, events[0])
+        save(layer, v.qkv)
+
+        def pair(k):
+            def rows(i):
+                lg = nn(qkv[span(i, CH), span(k, CH)], bd[layer, k])
+                for hh in range(2):
+                    ph[span(i, CH), span(2 * k + hh, CH)] = half_softmax(
+                        lg[:, hh * CH : (hh + 1) * CH], low
+                    ).astype(bf16)
+
+            loop(nc, rows)
+
+        loop(2 * PAIRS, pair, events[1])
+        save(layer, v.ph)
+
+        def state(k):
+            val = qkv[:, pl.ds(pl.multiple_of(2 * D + k * CH, CH), CH)]
+            for hh in range(2):
+                key = ph[:, pl.ds(pl.multiple_of((H + 2 * k + hh) * CH, CH), CH)]
+                full = tn(val, key)
+                st[layer, span(2 * k + hh, HEAD), :] = full[hh * HEAD : (hh + 1) * HEAD]
+                st[layer, pl.ds(D + 2 * k + hh, 1), :] = jnp.sum(
+                    key.astype(f32), 0, keepdims=True
+                )
+
+        loop(PAIRS, state)
+        st[layer, D + H :, :] = jnp.zeros((STATE_ROWS - D - H, CH), f32)
+        send_states(layer, st, 1)
+
+    members = 2 * group
+
+    def state_to(o, sign):
+        other = p.r + sign * o
+        return (lax.div(other, group), p.d, p.i * group + lax.rem(other, group))
+
+    def send_states(layer, st, sign):
+        for o in range(1, members):
+            ok = (p.r + o < members) if sign > 0 else (p.r - o >= 0)
+
+            @pl.when(ok)
+            def _():
+                remote(
+                    st.at[layer],
+                    own.got.at[layer, o - 1],
+                    own.s_send.at[layer, o - 1],
+                    own.s_recv.at[layer, o - 1],
+                    state_to(o, sign),
+                ).start()
+
+    def take_states(layer, sign):
+        pre = v.pre
+        pre[...] = jnp.zeros(pre.shape, f32)
+        for o in range(1, members):
+            ok = (p.r - o >= 0) if sign > 0 else (p.r + o < members)
+
+            @pl.when(ok)
+            def _():
+                finish(own.got.at[layer, o - 1], own.s_recv.at[layer, o - 1])
+                pre[...] += own.got[layer, o - 1]
+
+    def close_states(layer, sign):
+        for o in range(1, members):
+            ok = (p.r + o < members) if sign > 0 else (p.r - o >= 0)
+
+            @pl.when(ok)
+            def _():
+                finish(own.st.at[layer], own.s_send.at[layer, o - 1])
+
+    def mix(layer, u, events):
+        qkv, ph, o_, inv, ob = v.qkv, v.ph, v.o, v.inv, v.ob
+        r, n2, hid, gp = v.r, v.n2, v.hid, v.gp
+        res = v.res.at[layer]
+        take_states(layer, 1)
+        save(layer, v.pre)
+        s0 = v.pre
+
+        def pair(k):
+            cols = span(k, CH)
+            s = s0[cols, :]
+            tot = [s0[pl.ds(D + 2 * k + hh, 1), :] for hh in range(2)]
+            for c in range(nc):
+                rows = pl.ds(c * CH, CH)
+                val = qkv[rows, pl.ds(pl.multiple_of(2 * D + k * CH, CH), CH)]
+                sl = s.astype(bf16)
+                done = []
+                new = []
+                for hh in range(2):
+                    qh = ph[rows, span(2 * k + hh, CH)]
+                    kh = ph[rows, pl.ds(pl.multiple_of((H + 2 * k + hh) * CH, CH), CH)]
+                    score = jnp.where(tril, nt(qh, kh), 0.0)
+                    num = nn(score.astype(bf16), val) + nt(qh, sl)
+                    den = jnp.sum(score + qh.astype(f32) * tot[hh], -1, keepdims=True)
+                    rec = 1.0 / den
+                    done.append((num * rec, rec))
+                    new.append(tn(val, kh)[hh * HEAD : (hh + 1) * HEAD])
+                    tot[hh] = tot[hh] + jnp.sum(kh.astype(f32), 0, keepdims=True)
+                s = s + jnp.concatenate(new, 0)
+                both = jnp.where(low, done[0][0], done[1][0])
+                o_[rows, cols] = both
+                ob[rows, cols] = both.astype(bf16)
+                inv[rows, cols] = jnp.where(low, done[0][1], done[1][1])
+
+        loop(PAIRS, pair, events[0])
+        save(layer, v.o, v.inv, v.ob)
+        events[1]()
+        loaded(own.vo, 1)
+
+        def out_col(j):
+            cols = span(j, TILE)
+            r[:, cols] = (
+                u[:, cols].astype(f32)
+                + nn(ob[...], flat.o[:, cols])
+                + bias_cols(layer, OUT_BIAS, j)
+            )
+
+        loop(D // TILE, out_col)
+        norm_rows(layer, r, n2, 1, SHIFT2)
+        save(layer, v.r, v.n2)
+        events[2]()
+        loaded(own.vu, 2)
+
+        def up_col(j):
+            cols = span(j, TILE)
+            zt = nn(n2[...], flat.u[:, cols]) + bias_cols(layer, UP_BIAS, j)
+            z2 = zt * zt
+            th = jnp.tanh(GELU_C * zt * (1.0 + GELU_A * z2))
+            half = 0.5 * (1.0 + th)
+            hid[:, cols] = (zt * half).astype(bf16)
+            gp[:, cols] = (
+                half + 0.5 * zt * (1.0 - th * th) * (GELU_C * (1.0 + 3.0 * GELU_A * z2))
+            ).astype(bf16)
+
+        loop(FF // TILE, up_col, events[3])
+        save(layer, v.hid, v.gp)
+        events[4]()
+        loaded(own.vd, 3)
+
+        def down_col(j):
+            cols = span(j, TILE)
+            res[:, cols] = (
+                r[:, cols] + nn(hid[...], flat.d[:, cols]) + bias_cols(layer, DOWN_BIAS, j)
+            ).astype(bf16)
+
+        loop(D // TILE, down_col)
+        save(layer, v.res)
+        for k in range(4):
+            to = p.jj * 4 + k
+            src = res.at[pl.ds(k * CH, CH), :]
+            dst = ref.lay.at[0, p.i, p.x]
+            slot = p.i * 2 + p.x
+            mine = (to == p.j) & (p.x == layer)
+            copy = remote(
+                src, dst, own.d_send.at[layer, k], own.d_recv.at[slot], p.at(x=layer, j=to)
+            )
+
+            @pl.when(jnp.logical_not(mine))
+            def _():
+                copy.start()
+
+            @pl.when(mine)
+            def _():
+                pltpu.make_async_copy(src, dst, own.d_recv.at[slot]).start()
+
+            def close(copy=copy, mine=mine):
+                @pl.when(jnp.logical_not(mine))
+                def _():
+                    copy.wait_send()
+
+            closing.append(close)
+
+    def run(*steps):
+        def go_():
+            for step in steps:
+                step()
+
+        return go_
+
+    def each(count, fn, first=0):
+        return [functools.partial(fn, o) for o in range(first, count)]
+
+    nothing = run()
+    gq.core(3)
+    gq.done()
+    load(gq, own.vq, 0, 0)
+    tok_out = pltpu.make_async_copy(own.tok, ref.tok_out, own.m_sem)
+    tok_out.start()
+    project(
+        0,
+        own.tok,
+        [
+            {
+                1: run(*each(nz, go.first, 1)),
+                3: run(functools.partial(gu.first, 1)),
+                5: run(functools.partial(gu.first, 2)),
+                7: run(functools.partial(gu.first, 3), gd.start, functools.partial(gd.first, 0)),
+            },
+            {
+                1: run(*each(nz, go.second)),
+                3: run(*each(2, gu.second)),
+                5: run(functools.partial(gu.second, 2), *each(3, go.core)),
+                7: run(functools.partial(gu.second, 3), functools.partial(gd.first, 1)),
+                9: run(*each(3, gu.core), functools.partial(gd.first, 2)),
+                11: run(functools.partial(gd.first, 3)),
+            },
+        ],
+    )
+    mix(
+        0,
+        own.tok,
+        [
+            {
+                1: run(functools.partial(go.core, 3), *each(2, gd.second)),
+                3: run(*each(nz, gd.second, 2)),
+            },
+            run(go.done, functools.partial(load, go, own.vo, 0, 1), *each(3, gd.core)),
+            run(
+                functools.partial(gu.core, 3), gu.done, functools.partial(load, gu, own.vu, 0, 2)
+            ),
+            {},
+            run(
+                functools.partial(gd.core, 3),
+                gd.done,
+                functools.partial(load, gd, own.vd, 0, 3),
+                functools.partial(load, gq, own.vq, 1, 0),
+                functools.partial(load, go, own.vo, 1, 1),
+                functools.partial(load, gu, own.vu, 1, 2),
+            ),
+        ],
+    )
+    closing.extend([collect(1, s) for s in range(4)])
+    project(1, v.res.at[0], [{}, {0: functools.partial(load, gd, own.vd, 1, 3)}])
+    mix(1, v.res.at[0], [{}, nothing, nothing, {}, nothing])
+
+    for g in gathers:
+        g.close()
+    for close in closing:
+        close()
+    for k in range(4):
+        finish(ref.cot_out.at[pl.ds(k * CH, CH), :], own.c_recv.at[1, k])
+    for layer in range(2):
+        close_states(layer, 1)
+
+        @pl.when(p.x == layer)
+        def _():
+            for slot in range(8):
+                finish(ref.lay.at[0, slot // 2, slot % 2], own.d_recv.at[slot])
+
+    tok_out.wait()
+    for copy in pending[1]:
+        copy.wait()
+
+
+def forward_pass(n, tokens, cotangent, small, wq, wo, wu, wd):
+    t = 4 * CH
+    nz = n // 2
+    full = [
+        shape((2, nz, 2, w.shape[0], 2 * w.shape[1]), bf16) for w in (wq, wo, wu, wd)
+    ]
+    kept = [
+        shape((t, D), bf16),
+        shape((t, 3 * D), bf16),
+        shape((t, 2 * QB), bf16),
+        shape((t, D), f32),
+        shape((t, D), f32),
+        shape((t, D), bf16),
+        shape((t, D), f32),
+        shape((t, D), bf16),
+        shape((t, FF), bf16),
+        shape((t, FF), bf16),
+        shape((t, D), bf16),
+        shape((STATE_ROWS, CH), f32),
+    ]
+    outs = full + [shape((1, 4, 2, CH, D), bf16)]
+    outs += [shape((2, GAIN_ROWS, CH), f32), shape((2, 2 * PAIRS, CH, 2 * CH), bf16)]
+    outs += [shape((t, D), bf16)] * 2 + kept * 2
+    specs = [ANY] * 5 + [VMEM] * 2 + [ANY] * (len(outs) - 7)
+    scratch = [pltpu.VMEM(k.shape, k.dtype) for k in kept]
+    scratch[10] = pltpu.VMEM((2, t, D), bf16)
+    scratch += [
+        pltpu.VMEM((t, D), bf16),
+        pltpu.VMEM((2, nz, 2, SMALL_ROWS, CH), bf16),
+        pltpu.VMEM((2, VEC_ROWS, CH), f32),
+        pltpu.VMEM((2, STATE_ROWS, CH), f32),
+        pltpu.VMEM((2, n // 2 - 1, STATE_ROWS, CH), f32),
+    ]
+    scratch += [pltpu.VMEM(w.shape[1:], bf16) for w in full]
+    dma = pltpu.SemaphoreType.DMA
+    scratch += [dma((5, 19)), dma((5, 19)), dma((5,)), dma((2, 4)), dma((2, 4))]
+    scratch += [dma((2, n // 2 - 1)), dma((2, n // 2 - 1)), dma((2, 4)), dma((8,)), dma((4,))]
+    scratch += [dma((2, 12)), dma]
+    got = call(
+        functools.partial(forward_kernel, n),
+        outs,
+        scratch,
+        [ANY] * 7,
+        [tokens, cotangent, small, wq, wo, wu, wd],
+        4 * t * D * (4 * D + 2 * FF),
+        specs,
+        cid=0,
+    )
+    layers = [Kept(*got[9:21]), Kept(*got[21:33])]
+    return got[:4], got[4], got[5], got[6], got[7], got[8], layers
+
+
+def with_error(gv, swapped, lane, hh):
+    first = HEAD * (1 - hh)
+    hi = swapped.astype(bf16)
+    lo = (swapped - hi.astype(f32)).astype(bf16)
+    own = (lane < HEAD) if hh == 0 else (lane >= HEAD)
+    spare = jnp.where(
+        lane == first + 1,
+        lo,
+        jnp.where((lane == first) | (lane == first + 2), hi, jnp.zeros_like(gv)),
+    )
+    return jnp.where(own, gv, spare)
+
+
+def with_ones(v, lane, hh):
+    first = HEAD * (1 - hh)
+    own = (lane < HEAD) if hh == 0 else (lane >= HEAD)
+    spare = jnp.where((lane == first) | (lane == first + 1), jnp.ones_like(v), jnp.zeros_like(v))
+    return jnp.where(own, v, spare)
+
+
+def with_totals(s, tot, row, hh, again):
+    first = HEAD * (1 - hh)
+    hi = tot.astype(bf16).astype(f32)
+    lo = tot - hi
+    own = (row < HEAD) if hh == 0 else (row >= HEAD)
+    if again:
+        spare = jnp.where(
+            (row == first) | (row == first + 1), hi, jnp.where(row == first + 2, lo, 0.0)
+        )
+    else:
+        spare = jnp.where(row == first, hi, jnp.where(row == first + 1, lo, 0.0))
+    return jnp.where(own, s, spare).astype(bf16)
+
+
+def put_rows(ref, layer, row, val):
+    for i in range(val.shape[1] // CH):
+        ref[layer, pl.ds(row + i, 1), :] = val[:, i * CH : (i + 1) * CH]
+
+
+class Reduce:
+    def __init__(self, place, layer, buf, temp, land, out, fin, send, recv, local, last):
+        self.p, self.layer, self.buf, self.temp = place, layer, buf, temp
+        self.land_d, self.land_y, self.land_z, self.land_x = land
+        self.out, self.fin, self.local, self.last = out, fin, local, last
+        self.send, self.recv = send, recv
+        self.r, self.c = buf.shape[2], buf.shape[3]
+
+    def go(self, src, dst, slot, to):
+        remote(src, dst, self.send.at[slot], self.recv.at[slot], to).start()
+
+    def fetch(self, src, dst):
+        copy = pltpu.make_async_copy(src, dst, self.local)
+        copy.start()
+        copy.wait()
+
+    def send_core(self):
+        self.go(self.buf, self.land_d, 0, self.p.at(d=1 - self.p.d))
+
+    def got_core(self):
+        finish(self.buf, self.send.at[0])
+        finish(self.land_d, self.recv.at[0])
+
+    def send_y(self):
+        p = self.p
+        self.go(self.buf.at[:, 1 - p.y], self.land_y, 1, p.at(y=1 - p.y))
+
+    def step_y(self):
+        p = self.p
+        finish(self.land_y, self.recv.at[1])
+        self.fetch(self.land_y, self.temp)
+        for i in range(1, p.nz + 1):
+            zi = p.zpos(i)
+            self.buf[zi, p.y] = (
+                self.buf[zi, p.y].astype(f32) + self.temp[zi].astype(f32)
+            ).astype(bf16)
+            if i < p.nz:
+                self.go(self.buf.at[zi, p.y], self.land_z.at[i - 1], 1 + i, p.at(z=zi))
+
+    def step_z(self):
+        p = self.p
+        for i in range(1, p.nz):
+            finish(self.land_z.at[i - 1], self.recv.at[1 + i])
+        self.fetch(self.land_z, self.temp.at[pl.ds(0, p.nz - 1)])
+        total = self.buf[p.z, p.y].astype(f32)
+        for i in range(p.nz - 1):
+            total = total + self.temp[i].astype(f32)
+
+        @pl.when(p.x == self.layer)
+        def _():
+            self.fin[...] = total
+
+        @pl.when(p.x != self.layer)
+        def _():
+            self.buf[p.z, p.y] = total.astype(bf16)
+            self.go(self.buf.at[p.z, p.y], self.land_x, 5, p.at(x=1 - p.x))
+
+    def half(self):
+        return pl.ds(pl.multiple_of(self.p.d * self.c, CH), self.c)
+
+    def other(self):
+        return pl.ds(pl.multiple_of((1 - self.p.d) * self.c, CH), self.c)
+
+    def step_x(self):
+        p = self.p
+
+        @pl.when(p.x == self.layer)
+        def _():
+            finish(self.land_x, self.recv.at[5])
+            self.fetch(self.land_x, self.temp.at[0])
+            self.fin[...] += self.temp[0].astype(f32)
+            own = self.out.at[:, self.half()]
+            self.go(self.fin, own, 6, p.at(d=1 - p.d))
+            pltpu.make_async_copy(self.fin, own, self.last).start()
+
+    def close(self):
+        p = self.p
+        finish(self.buf.at[:, 0], self.send.at[1])
+        for i in range(1, p.nz):
+            finish(self.buf.at[0, 0], self.send.at[1 + i])
+
+        @pl.when(p.x != self.layer)
+        def _():
+            finish(self.buf.at[0, 0], self.send.at[5])
+
+    def end(self):
+        @pl.when(self.p.x == self.layer)
+        def _():
+            finish(self.fin, self.send.at[6])
+            finish(self.out.at[:, self.other()], self.recv.at[6])
+            finish(self.fin, self.last)
+
+
+class SmallReduce:
+    def __init__(self, place, layer, buf, land, out, send, recv):
+        self.p, self.layer, self.buf, self.out = place, layer, buf, out
+        self.land_d, self.land_y, self.land_z, self.land_x = land
+        self.send, self.recv = send, recv
+
+    def go(self, src, dst, slot, to):
+        remote(src, dst, self.send.at[slot], self.recv.at[slot], to).start()
+
+    def send_core(self):
+        self.go(self.buf, self.land_d, 0, self.p.at(d=1 - self.p.d))
+
+    def step_d(self):
+        p = self.p
+        finish(self.buf, self.send.at[0])
+        finish(self.land_d, self.recv.at[0])
+        self.buf[...] += self.land_d[...]
+        self.go(self.buf.at[:, 1 - p.y], self.land_y, 1, p.at(y=1 - p.y))
+
+    def step_y(self):
+        p = self.p
+        finish(self.land_y, self.recv.at[1])
+        for i in range(1, p.nz + 1):
+            zi = p.zpos(i)
+            self.buf[zi, p.y] += self.land_y[zi]
+            if i < p.nz:
+                self.go(self.buf.at[zi, p.y], self.land_z.at[i - 1], 1 + i, p.at(z=zi))
+
+    def step_z(self):
+        p = self.p
+        for i in range(1, p.nz):
+            finish(self.land_z.at[i - 1], self.recv.at[1 + i])
+        total = self.buf[p.z, p.y]
+        for i in range(p.nz - 1):
+            total = total + self.land_z[i]
+        self.buf[p.z, p.y] = total
+
+        @pl.when(p.x != self.layer)
+        def _():
+            self.go(self.buf.at[p.z, p.y], self.land_x, 5, p.at(x=1 - p.x))
+
+    def step_x(self):
+        p = self.p
+
+        @pl.when(p.x == self.layer)
+        def _():
+            finish(self.land_x, self.recv.at[5])
+            self.out[...] = self.buf[p.z, p.y] + self.land_x[...]
+
+    def close(self):
+        p = self.p
+        finish(self.buf.at[:, 0], self.send.at[1])
+        for i in range(1, p.nz):
+            finish(self.buf.at[0, 0], self.send.at[1 + i])
+
+        @pl.when(p.x != self.layer)
+        def _():
+            finish(self.buf.at[0, 0], self.send.at[5])
+
+
+SMALL_OUT = 112
+
+
+class Loaded(NamedTuple):
+    gp: Any
+    r: Any
+    o: Any
+    inv: Any
+    ph: Any
+    qkv: Any
+    n2: Any
+    ob: Any
+    a: Any
+    u: Any
+    pre: Any
+
+
+class BackwardRefs(NamedTuple):
+    cot: Any
+    gv: Any
+    bd: Any
+    wq: Any
+    wo: Any
+    wu: Any
+    wd: Any
+
+
+class BackwardScratch(NamedTuple):
+    g: Any
+    drb: Any
+    gs: Any
+    tmp: Any
+    acc: Any
+    st: Any
+    got: Any
+    mg: Any
+    vr: Any
+    gr: Any
+    hidr: Any
+    wdr: Any
+    vq: Any
+    vo: Any
+    vu: Any
+    bq: Any
+    bo: Any
+    bu: Any
+    bd_: Any
+    tmp96: Any
+    tmpd: Any
+    fq: Any
+    fo: Any
+    fu: Any
+    fd: Any
+    ty96: Any
+    tyd: Any
+    sb: Any
+    sd: Any
+    sy: Any
+    sz: Any
+    sx: Any
+    r_send: Any
+    r_recv: Any
+    r_local: Any
+    q_send: Any
+    q_recv: Any
+    s_send: Any
+    s_recv: Any
+    d_send: Any
+    d_recv: Any
+    w_sem: Any
+    l_sem: Any
+    h_sem: Any
+    t_sem: Any
+    k_sem: Any
+
+
+Q, O, U, DN = range(4)
+
+
+def backward_kernel(n, *refs):
+    ref = BackwardRefs(*refs[:7])
+    source = [Loaded(*refs[7:18]), Loaded(*refs[18:29])]
+    hidden = refs[29:31]
+    gin, small_out = refs[31], refs[36]
+    wgrads = refs[32:36]
+    lands = refs[37:69]
+    v = Loaded(*refs[69:80])
+    own = BackwardScratch(*refs[80:])
+    p = Place(n)
+    nz, group = p.nz, p.group
+    t = own.drb.shape[0]
+    nc = t // CH
+    members = 2 * group
+    gains, gbuf, tmp, acc = ref.gv, own.g, own.tmp, own.acc
+    vr, gr, mg = own.vr, own.gr, own.mg
+    flat = Weights(own.vq.reshape(D, 3 * D), own.vo.reshape(D, D), own.vu.reshape(D, FF))
+    stored = (own.vq, own.vo, own.vu)
+    lane_t = lanes(t)
+    lane = lanes(CH)
+    low = lane < HEAD
+    row = lax.broadcasted_iota(jnp.int32, (CH, CH), 0)
+    tril, triu = row >= lane, row <= lane
+
+    def load(layer, *wanted):
+        for dst in wanted:
+            k = [dst is x for x in v].index(True)
+            pltpu.make_async_copy(source[layer][k], dst, own.l_sem.at[k]).start()
+
+    def loaded(*wanted):
+        for dst in wanted:
+            k = [dst is x for x in v].index(True)
+            finish(dst, own.l_sem.at[k])
+
+    def load_w(layer, k):
+        w = (ref.wq, ref.wo, ref.wu)[k]
+        pltpu.make_async_copy(w.at[layer], stored[k], own.w_sem.at[k]).start()
+
+    def loaded_w(k):
+        finish(stored[k], own.w_sem.at[k])
+
+    def load_wd(layer, k):
+        pltpu.make_async_copy(
+            ref.wd.at[layer, k // 2, k % 2], own.wdr.at[k % 3], own.k_sem.at[k % 3]
+        ).start()
+
+    pltpu.make_async_copy(ref.cot, gbuf.at[0], own.t_sem.at[4]).start()
+    for k in range(3):
+        load_wd(1, k)
+    load(1, v.gp)
+    load_w(1, U)
+    load(1, v.r, v.o, v.inv, v.ph)
+    load_w(1, O)
+    load_w(1, Q)
+    load(1, v.qkv, v.n2, v.ob, v.a, v.u, v.pre)
+    p.meet()
+    finish(gbuf.at[0], own.t_sem.at[4])
+
+    width = (3 * D // 2, D // 2, FF // 2, D // 2)
+    bufs = (own.bq, own.bo, own.bu, own.bd_)
+    fins = (own.fq, own.fo, own.fu, own.fd)
+    reduces = []
+    for layer in range(2):
+        line = []
+        for m in (Q, O, U, DN):
+            at = (layer * 4 + m) * 4
+            line.append(
+                Reduce(
+                    p,
+                    layer,
+                    bufs[m],
+                    own.tyd if m == DN else own.ty96.at[:, :, pl.ds(0, width[m])],
+                    lands[at : at + 4],
+                    wgrads[m],
+                    fins[m],
+                    own.r_send.at[layer, m],
+                    own.r_recv.at[layer, m],
+                    own.r_local.at[m],
+                    own.r_local.at[4 + m],
+                )
+            )
+        reduces.append(line)
+    smalls = [
+        SmallReduce(
+            p,
+            layer,
+            own.sb.at[layer],
+            [land.at[layer] for land in (own.sd, own.sy, own.sz, own.sx)],
+            small_out,
+            own.q_send.at[layer],
+            own.q_recv.at[layer],
+        )
+        for layer in range(2)
+    ]
+
+    def states_ok(o, taking):
+        return (p.r + o < members) if taking else (p.r - o >= 0)
+
+    def send_states(layer):
+        for o in range(1, members):
+            other = p.r - o
+
+            @pl.when(states_ok(o, False))
+            def _():
+                remote(
+                    own.st.at[layer],
+                    own.got.at[layer, o - 1],
+                    own.s_send.at[layer, o - 1],
+                    own.s_recv.at[layer, o - 1],
+                    (lax.div(other, group), p.d, p.i * group + lax.rem(other, group)),
+                ).start()
+
+    def take_states(layer):
+        acc0 = own.got.at[layer, 0]
+        for o in range(1, members):
+
+            @pl.when(states_ok(o, True))
+            def _():
+                finish(own.got.at[layer, o - 1], own.s_recv.at[layer, o - 1])
+                if o > 1:
+                    acc0[...] += own.got[layer, o - 1]
+
+            if o == 1:
+
+                @pl.when(jnp.logical_not(states_ok(o, True)))
+                def _():
+                    acc0[...] = jnp.zeros(acc0.shape, f32)
+
+        return acc0
+
+    def close_states(layer):
+        for o in range(1, members):
+
+            @pl.when(states_ok(o, False))
+            def _():
+                finish(own.st.at[layer], own.s_send.at[layer, o - 1])
+
+    def norm_back(x_ref, which, layer, body):
+        gain = wide(gains, layer, which * 6, 6)
+        acc[...] = jnp.zeros(acc.shape, f32)
+
+        def step(i):
+            rows = span(i, CH)
+            xh, rstd = standardize(x_ref[rows, :].astype(f32))
+            dn = tmp[rows, :]
+            acc[0:1, :] += jnp.sum(dn, 0, keepdims=True)
+            acc[1:2, :] += jnp.sum(dn * xh, 0, keepdims=True)
+            dx = dn * gain
+            body(
+                rows,
+                rstd
+                * (dx - jnp.mean(dx, -1, keepdims=True) - xh * jnp.mean(dx * xh, -1, keepdims=True)),
+            )
+
+        loop(nc, step)
+        put_rows(vr, layer, SHIFT2 if which else SHIFT1, acc[0:1, :])
+        put_rows(gr, layer, which * 6, acc[1:2, :])
+
+    def mlp_back(layer, g, events):
+        gp, r, o_, inv, ph = v.gp, v.r, v.o, v.inv, v.ph
+        drb, gs, st = own.drb, own.gs, own.st
+        loaded(v.gp)
+        for k in range(2 * nz):
+            finish(own.wdr.at[k % 3], own.k_sem.at[k % 3])
+            cols = pl.ds(k * FF // n, FF // n)
+            part = (nt(g[...], own.wdr[k % 3]) * gp[:, cols]).astype(bf16)
+            gp[:, cols] = part
+            put_rows(
+                vr, layer, UP_BIAS + 3 * k, jnp.sum(part.astype(f32), 0, keepdims=True)
+            )
+            if k + 3 < 2 * nz:
+                load_wd(layer, k + 3)
+            if k in events:
+                events[k]()
+        loaded_w(U)
+
+        def n2_col(j):
+            cols = span(j, TILE)
+            tmp[:, cols] = nt(gp[...], flat.u[cols, :])
+
+        loop(D // TILE, n2_col)
+        loaded(v.r)
+
+        def body(rows, back):
+            up = g[rows, :].astype(f32)
+            total = up + back
+            acc[2:3, :] += jnp.sum(up, 0, keepdims=True)
+            acc[3:4, :] += jnp.sum(total, 0, keepdims=True)
+            r[rows, :] = total
+            drb[rows, :] = total.astype(bf16)
+
+        norm_back(r, 1, layer, body)
+        put_rows(vr, layer, DOWN_BIAS, acc[2:3, :])
+        put_rows(vr, layer, OUT_BIAS, acc[3:4, :])
+        loaded_w(O)
+        loaded(v.inv, v.o, v.ph)
+
+        def do_col(j):
+            cols = span(j, TILE)
+            gs[:, cols] = (nt(drb[...], flat.o[cols, :]) * inv[:, cols]).astype(bf16)
+
+        loop(D // TILE, do_col)
+        low_t = lane_t < HEAD
+
+        def pair(k):
+            cols = span(k, CH)
+            gv = gs[:, cols]
+            prod = gv.astype(f32) * o_[:, cols]
+            e0 = -jnp.sum(jnp.where(low_t, prod, 0.0), -1, keepdims=True)
+            e1 = -jnp.sum(jnp.where(low_t, 0.0, prod), -1, keepdims=True)
+            swapped = jnp.where(low_t, e1, e0)
+            inv[:, cols] = swapped
+            for hh in range(2):
+                ge = with_error(gv, swapped, lane_t, hh)
+                full = tn(ge, ph[:, span(2 * k + hh, CH)])
+                st[layer, span(2 * k + hh, HEAD), :] = full[hh * HEAD : (hh + 1) * HEAD]
+                at = HEAD * (1 - hh)
+                st[layer, pl.ds(D + 2 * k + hh, 1), :] = full[at : at + 1] + full[at + 1 : at + 2]
+
+        loop(PAIRS, pair)
+        st[layer, D + H :, :] = jnp.zeros((STATE_ROWS - D - H, CH), f32)
+        send_states(layer)
+
+    def weight_grad(layer, m, keep):
+        red = reduces[layer][m]
+        buf, c = red.buf, red.c
+        base = (p.d if keep else 1 - p.d) * c
+        if keep:
+            red.got_core()
+        elif layer == 0:
+            reduces[1][m].close()
+        if m == DN:
+            rhs = gbuf[1 - layer, :, pl.ds(pl.multiple_of(base, CH), c)]
+
+            def fetch(k):
+                pltpu.make_async_copy(
+                    hidden[layer].at[:, pl.ds(k * FF // n, FF // n)],
+                    own.hidr.at[k % 3],
+                    own.h_sem.at[k % 3],
+                ).start()
+                if keep:
+                    pltpu.make_async_copy(
+                        red.land_d.at[k // 2, k % 2], own.tmpd.at[k % 3], own.t_sem.at[k % 3]
+                    ).start()
+
+            for k in range(3):
+                fetch(k)
+            for k in range(2 * nz):
+                finish(own.hidr.at[k % 3], own.h_sem.at[k % 3])
+                val = tn(own.hidr[k % 3], rhs)
+                if keep:
+                    finish(own.tmpd.at[k % 3], own.t_sem.at[k % 3])
+                    val = val + own.tmpd[k % 3].astype(f32)
+                buf[k // 2, k % 2] = val.astype(bf16)
+                if k + 3 < 2 * nz:
+                    fetch(k + 3)
+        else:
+            lhs = (v.a, v.ob, v.n2)[m]
+            rhs = (v.qkv, own.drb, v.gp)[m]
+            step = 384
+            count = c // step
+
+            def fetch(k):
+                pltpu.make_async_copy(
+                    red.land_d.at[:, :, :, pl.ds(k * step, step)],
+                    own.tmp96.at[k % 2],
+                    own.t_sem.at[k % 2],
+                ).start()
+
+            if keep:
+                for k in range(min(2, count)):
+                    fetch(k)
+            for k in range(count):
+                val = tn(lhs[...], rhs[:, pl.ds(pl.multiple_of(base + k * step, CH), step)])
+                if keep:
+                    finish(own.tmp96.at[k % 2], own.t_sem.at[k % 2])
+                for zi in range(nz):
+                    for yi in range(2):
+                        at = (zi * 2 + yi) * red.r
+                        part = val[at : at + red.r]
+                        if keep:
+                            part = part + own.tmp96[k % 2, zi, yi].astype(f32)
+                        buf[zi, yi, :, pl.ds(k * step, step)] = part.astype(bf16)
+                if keep and k + 2 < count:
+                    fetch(k + 2)
+        if keep:
+            red.send_y()
+        else:
+            red.send_core()
+
+    def mix_back(layer, events):
+        qkv, ph, gs, es = v.qkv, v.ph, own.gs, v.inv
+        bd = ref.bd.at[layer]
+        s1 = take_states(layer)
+        loaded(v.qkv, v.pre)
+        s0 = v.pre
+
+        def pair(k):
+            cols = span(k, CH)
+            vcols = pl.ds(pl.multiple_of(2 * D + k * CH, CH), CH)
+            kcols = pl.ds(pl.multiple_of(D + k * CH, CH), CH)
+
+            def keys(rows, hh):
+                return ph[rows, pl.ds(pl.multiple_of((H + 2 * k + hh) * CH, CH), CH)]
+
+            before = []
+            s = s0[cols, :]
+            tot = [s0[pl.ds(D + 2 * k + hh, 1), :] for hh in range(2)]
+            for c in range(nc):
+                rows = pl.ds(c * CH, CH)
+                before.append([with_totals(s, tot[hh], row, hh, True) for hh in range(2)])
+                if c < nc - 1:
+                    val = qkv[rows, vcols]
+                    new = []
+                    for hh in range(2):
+                        kh = keys(rows, hh)
+                        new.append(tn(val, kh)[hh * HEAD : (hh + 1) * HEAD])
+                        tot[hh] = tot[hh] + jnp.sum(kh.astype(f32), 0, keepdims=True)
+                    s = s + jnp.concatenate(new, 0)
+            ds = s1[cols, :]
+            dtot = [s1[pl.ds(D + 2 * k + hh, 1), :] for hh in range(2)]
+            acc_q = jnp.zeros((CH, 2 * CH), f32)
+            acc_k = jnp.zeros((CH, 2 * CH), f32)
+            sums = [jnp.zeros((1, CH), f32) for _ in range(3)]
+            for c in reversed(range(nc)):
+                rows = pl.ds(c * CH, CH)
+                val = qkv[rows, vcols]
+                gv = gs[rows, cols]
+                ev = es[rows, cols]
+                dsl = ds.astype(bf16)
+                dl_q, dl_k, dv, new = [], [], [], []
+                for hh in range(2):
+                    qh = ph[rows, span(2 * k + hh, CH)]
+                    kh = keys(rows, hh)
+                    ge = with_error(gv, ev, lane, hh)
+                    v1 = with_ones(val, lane, hh)
+                    after = with_totals(ds, dtot[hh], row, hh, False)
+                    da = jnp.where(tril, nt(ge, v1), 0.0).astype(bf16)
+                    dat = jnp.where(triu, nt(v1, ge), 0.0).astype(bf16)
+                    at = jnp.where(triu, nt(kh, qh), 0.0).astype(bf16)
+                    dq = nn(da, kh) + nn(ge, before[c][hh])
+                    dk = nn(dat, qh) + nn(v1, after)
+                    dv.append(nn(at, gv) + nt(kh, dsl))
+                    for p_, d_, to in ((qh, dq, dl_q), (kh, dk, dl_k)):
+                        pf = p_.astype(f32)
+                        to.append((pf * (d_ - half_sums(pf * d_, low))).astype(bf16))
+                    full = tn(ge, qh)
+                    new.append(full[hh * HEAD : (hh + 1) * HEAD])
+                    first = HEAD * (1 - hh)
+                    dtot[hh] = dtot[hh] + full[first : first + 1] + full[first + 1 : first + 2]
+                ds = ds + jnp.concatenate(new, 0)
+                dl_q = jnp.concatenate(dl_q, 1)
+                dl_k = jnp.concatenate(dl_k, 1)
+                acc_q = acc_q + tn(qkv[rows, cols], dl_q)
+                acc_k = acc_k + tn(qkv[rows, kcols], dl_k)
+                parts = (
+                    (cols, nt(dl_q, bd[k])),
+                    (kcols, nt(dl_k, bd[PAIRS + k])),
+                    (vcols, jnp.where(low, dv[0], dv[1])),
+                )
+                for i, (where, new_) in enumerate(parts):
+                    new_ = new_.astype(bf16)
+                    qkv[rows, where] = new_
+                    sums[i] = sums[i] + jnp.sum(new_.astype(f32), 0, keepdims=True)
+            for i in range(3):
+                vr[layer, pl.ds(QKV_BIAS + i * PAIRS + k, 1), :] = sums[i]
+            for which, total in enumerate((acc_q, acc_k)):
+                for hh in range(2):
+                    blk = total[hh * HEAD : (hh + 1) * HEAD, hh * CH : (hh + 1) * CH]
+                    mg[which * H + 2 * k + hh] = blk - pltpu.roll(blk, HEAD, 1)
+
+        loop(PAIRS, pair, events)
+        loaded_w(Q)
+
+        def n1_col(j):
+            cols = span(j, TILE)
+            tmp[:, cols] = nt(qkv[...], flat.q[cols, :])
+
+        loop(D // TILE, n1_col)
+        loaded(v.u)
+        du = gbuf.at[layer]
+
+        def body(rows, back):
+            du[rows, :] = (v.r[rows, :] + back).astype(bf16)
+
+        norm_back(v.u, 0, layer, body)
+
+    closing = []
+
+    def deliver(layer):
+        for k in range(4):
+            to = p.jj * 4 + k
+            src = gbuf.at[layer, pl.ds(k * CH, CH), :]
+            dst = gin.at[0, p.i, p.x]
+            slot = p.i * 2 + p.x
+            mine = (to == p.j) & (p.x == layer)
+            copy = remote(
+                src, dst, own.d_send.at[layer, k], own.d_recv.at[slot], p.at(x=layer, j=to)
+            )
+
+            @pl.when(jnp.logical_not(mine))
+            def _():
+                copy.start()
+
+            @pl.when(mine)
+            def _():
+                pltpu.make_async_copy(src, dst, own.d_recv.at[slot]).start()
+
+            def close(copy=copy, mine=mine):
+                @pl.when(jnp.logical_not(mine))
+                def _():
+                    copy.wait_send()
+
+            closing.append(close)
+
+    def pack_small(layer):
+        sb = own.sb
+        for k in range(n):
+            at, gat = (33 * k) // 4, (3 * k) // 2
+            zi, yi = k // 2, k % 2
+            sb[layer, zi, yi, 0:9] = vr[layer, at : at + 9, :]
+            sb[layer, zi, yi, 9:11] = gr[layer, gat : gat + 2, :]
+            sb[layer, zi, yi, 11:16] = jnp.zeros((5, CH), f32)
+            h0, h1, h2 = (mg[3 * k + i] for i in range(3))
+            left = jnp.concatenate([h0, h1[: HEAD // 2]], 0)
+            right = jnp.concatenate([h1[HEAD // 2 :], h2], 0)
+            sb[layer, zi, yi, 16:SMALL_OUT] = jnp.where(lanes(96) < HEAD, left, -right)
+        smalls[layer].send_core()
+
+    vr[...] = jnp.zeros(vr.shape, f32)
+    gr[...] = jnp.zeros(gr.shape, f32)
+    r1, r0 = reduces[1], reduces[0]
+    s1, s0 = smalls[1], smalls[0]
+
+    def run(*steps):
+        def all_():
+            for step in steps:
+                step()
+
+        return all_
+
+    mlp_back(1, gbuf.at[0], {})
+    load(0, v.o)
+    load_w(0, U)
+    load_w(0, O)
+    for k in range(3):
+        load_wd(0, k)
+    loaded(v.n2, v.ob, v.a)
+    for m in (DN, U, O):
+        weight_grad(1, m, False)
+    for m in (DN, U, O):
+        weight_grad(1, m, True)
+    load(0, v.gp, v.n2, v.ob)
+    mix_back(1, {4: r1[DN].step_y})
+    load_w(0, Q)
+    load(0, v.r, v.inv, v.ph, v.u, v.pre)
+    deliver(1)
+    pack_small(1)
+    weight_grad(1, Q, False)
+    r1[U].step_y()
+    weight_grad(1, Q, True)
+    s1.step_d()
+    load(0, v.qkv)
+    load(0, v.a)
+
+    mlp_back(
+        0,
+        gbuf.at[1],
+        {2: r1[DN].step_z, 4: r1[O].step_y, 6: s1.step_y, 7: run(r1[DN].step_x)},
+    )
+    loaded(v.n2, v.ob, v.a)
+    weight_grad(0, DN, False)
+    r1[U].step_z()
+    weight_grad(0, U, False)
+    r1[O].step_z()
+    weight_grad(0, O, False)
+    r1[Q].step_y()
+    s1.step_z()
+    weight_grad(0, DN, True)
+    weight_grad(0, U, True)
+    weight_grad(0, O, True)
+    mix_back(
+        0,
+        {
+            0: run(r1[U].step_x, r1[O].step_x, s1.step_x),
+            2: r1[Q].step_z,
+            3: run(r1[Q].step_x, r0[DN].step_y),
+        },
+    )
+    deliver(0)
+    pack_small(0)
+    weight_grad(0, Q, False)
+    r0[U].step_y()
+    weight_grad(0, Q, True)
+    s0.step_d()
+    r0[DN].step_z()
+    r0[O].step_y()
+    s0.step_y()
+    r0[DN].step_x()
+    r0[U].step_z()
+    r0[Q].step_y()
+    r0[O].step_z()
+    s0.step_z()
+    r0[U].step_x()
+    r0[O].step_x()
+    s0.step_x()
+    r0[Q].step_z()
+    r0[Q].step_x()
+
+    for m in (Q, O, U, DN):
+        r0[m].close()
+        r1[m].end()
+        r0[m].end()
+    s1.close()
+    s0.close()
+    for layer in range(2):
+        close_states(layer)
+
+        @pl.when(p.x == layer)
+        def _():
+            for slot in range(8):
+                finish(gin.at[0, slot // 2, slot % 2], own.d_recv.at[slot])
+
+    for close in closing:
+        close()
+
+
+def backward_pass(n, cot, gains, bds, full, tokens, kept):
+    t = cot.shape[0]
+    nz = n // 2
+    args = [cot, gains, bds] + list(full)
+    for u, k in zip((tokens, kept[0].res), kept):
+        read = Loaded(k.gp, k.r, k.o, k.inv, k.ph, k.qkv, k.n2, k.ob, k.a, u, k.pre)
+        args += list(read)
+    args += [k.hid for k in kept]
+    widths = (3 * D // 2, D // 2, FF // 2, D // 2)
+    rows = (D // n, D // n, D // n, FF // n)
+    outs = [shape((1, 4, 2, CH, D), bf16)]
+    outs += [shape((r, 2 * c), f32) for r, c in zip(rows, widths)]
+    outs += [shape((SMALL_OUT, CH), f32)]
+    for _ in range(2):
+        for r, c in zip(rows, widths):
+            outs += [
+                shape((nz, 2, r, c), bf16),
+                shape((nz, r, c), bf16),
+                shape((nz - 1, r, c), bf16),
+                shape((r, c), bf16),
+            ]
+    specs = [ANY] * 5 + [VMEM] + [ANY] * (len(outs) - 6)
+    ins = [ANY, VMEM, VMEM] + [ANY] * (len(args) - 3)
+    scratch = [pltpu.VMEM(a.shape, a.dtype) for a in read]
+
+    def vmem(*dims, kind=f32):
+        scratch.append(pltpu.VMEM(dims, kind))
+
+    vmem(2, t, D, kind=bf16)
+    vmem(t, D, kind=bf16)
+    vmem(t, D, kind=bf16)
+    vmem(t, D)
+    vmem(8, D)
+    vmem(2, STATE_ROWS, CH)
+    vmem(2, n // 2 - 1, STATE_ROWS, CH)
+    vmem(2 * H, HEAD, CH)
+    vmem(2, VEC_ROWS, CH)
+    vmem(2, GAIN_ROWS, CH)
+    vmem(3, t, FF // n, kind=bf16)
+    vmem(3, FF // n, D, kind=bf16)
+    for w in full[:3]:
+        vmem(*w.shape[1:], kind=bf16)
+    for r, c in zip(rows, widths):
+        vmem(nz, 2, r, c, kind=bf16)
+    vmem(2, nz, 2, D // n, 384, kind=bf16)
+    vmem(3, FF // n, D // 2, kind=bf16)
+    for r, c in zip(rows, widths):
+        vmem(r, c)
+    vmem(nz, D // n, FF // 2, kind=bf16)
+    vmem(nz, FF // n, D // 2, kind=bf16)
+    vmem(2, nz, 2, SMALL_OUT, CH)
+    vmem(2, nz, 2, SMALL_OUT, CH)
+    vmem(2, nz, SMALL_OUT, CH)
+    vmem(2, nz - 1, SMALL_OUT, CH)
+    vmem(2, SMALL_OUT, CH)
+    dma = pltpu.SemaphoreType.DMA
+    scratch += [dma((2, 4, 7)), dma((2, 4, 7)), dma((8,)), dma((2, 7)), dma((2, 7))]
+    scratch += [dma((2, n // 2 - 1)), dma((2, n // 2 - 1)), dma((2, 4)), dma((8,)), dma((4,))]
+    scratch += [dma((len(read),)), dma((3,)), dma((5,)), dma((3,))]
+    got = call(
+        functools.partial(backward_kernel, n),
+        outs,
+        scratch,
+        ins,
+        args,
+        8 * t * D * (4 * D + 2 * FF),
+        specs,
+        cid=1,
+    )
+    return got[:6]
+
+
+def shards(inputs, cotangent, *weights):
+    n = lax.axis_size("seq")
+    d, j = lax.axis_index("dp"), lax.axis_index("seq")
+    qkv_w, out_w, up_w, down_w, map_w, bias_w, gain_w = (w[0] for w in weights)
+
+    def halved(w):
+        width = w.shape[1] // 2
+        return lax.dynamic_slice_in_dim(w, d * width, width, 1).astype(bf16)
+
+    def placed(vector, offset, rows):
+        flat = jnp.zeros((rows * CH,), f32)
+        return lax.dynamic_update_slice(flat, vector, (offset,)).reshape(rows, CH)
+
+    bias_at, gain_at = (j % 4) * 32, (j % 2) * 64
+    small = jnp.concatenate(
+        [
+            placed(bias_w, bias_at, 9),
+            placed(gain_w, gain_at, 2),
+            jnp.zeros((5, CH), f32),
+            jnp.concatenate([map_w, -map_w], 1),
+        ]
+    ).astype(bf16)
+    full, layer_out, gains, bds, tokens, cot, kept = forward_pass(
+        n, inputs, cotangent, small, halved(qkv_w), halved(out_w), halved(up_w), halved(down_w)
+    )
+    grads, g_qkv, g_out, g_up, g_down, g_small = backward_pass(n, cot, gains, bds, full, tokens, kept)
+    maps = jnp.concatenate([g_small[16:, :HEAD], g_small[16:, HEAD:]])
+    bias = lax.dynamic_slice_in_dim(g_small[:9].reshape(-1), bias_at, bias_w.shape[0])
+    gain = lax.dynamic_slice_in_dim(g_small[9:11].reshape(-1), gain_at, gain_w.shape[0])
+    return (
+        layer_out,
+        grads,
+        g_qkv[None],
+        g_out[None],
+        g_up[None],
+        g_down[None],
+        maps[None],
+        bias[None],
+        gain[None],
+    )
+
+
 def solution(mesh):
-    placed = (
-        P("dp", None, "seq", None),
-        P("dp", None, "seq", None),
-        P("section", "seq", None),
-        P("section", "seq", None),
-        P("section", "seq", None),
-        P("section", "seq", None),
-        P("section", "seq", None),
-        P("section", "seq"),
-        P("section", "seq"),
-    )
+    tokens = P("dp", None, "seq", None)
+    matrix = P("section", "seq", None)
+    vector = P("section", "seq")
+    stacked = P("section", "dp", None, "seq", None)
+    chosen = shards if mesh.shape["seq"] == 8 else plain_shards
     return jax.shard_map(
-        shards,
+        chosen,
         mesh=mesh,
-        in_specs=placed,
-        out_specs=(
-            P("section", "dp", None, "seq", None),
-            P("section", "dp", None, "seq", None),
-            P("section", "seq", None),
-            P("section", "seq", None),
-            P("section", "seq", None),
-            P("section", "seq", None),
-            P("section", "seq", None),
-            P("section", "seq"),
-            P("section", "seq"),
-        ),
+        in_specs=(tokens, tokens) + (matrix,) * 5 + (vector,) * 2,
+        out_specs=(stacked, stacked) + (matrix,) * 5 + (vector,) * 2,
         check_vma=False,
     )

time: 3410 us -> 702 us (0.21)
  waiting for transfers between devices: 1460 us -> 0 us
  Pallas kernels: 0 us -> 671 us
  blocking collectives: 541 us -> 0 us
  local copies, waits for them, and re-layouts: 543 us -> 20 us
  matrix products: 439 us -> 0 us
  other arithmetic: 360 us -> 1.47 us
    pallas_call x0 -> x2, Pallas kernels: none -> 671 us  [call(): pl.pallas_call(kernel, out_shape=outs, in_specs=specs, out_specs=out_spec...]
    all_gather x10 -> x0, waiting for transfers between devices: 548 us -> none  [the longest x6 337 us: carried_in(): gathered = jax.tree.map(lambda a: lax.all_gather(a, axis), part)]
    reduce_scatter x4 -> x0, waiting for transfers between devices: 524 us -> none  [the longest x1 166 us: reduce_grads(): lax.psum_scatter(g_down, 'seq', scatter_dimension=1, tiled=True)]
    dot_general x102 -> x0, matrix products: 418 us -> none  [the longest x54 195 us: precise(): jnp.einsum(pattern, left_side, right_side, precision=MAXIMUM_ACCURACY)]
    psum x7 -> x0, blocking collectives: 306 us -> none  [the longest x3 154 us: attend_back(): overall = lax.psum((state_sum, total_sum), 'seq')]
    unnamed x15 -> x0, waiting for transfers between devices: 220 us -> none
    all_gather x7 -> x0, blocking collectives: 209 us -> none  [the longest x6 184 us: carried_in(): gathered = jax.tree.map(lambda a: lax.all_gather(a, axis), part)]
    dynamic_slice x72 -> x2, local copies, waits for them, and re-layouts: 173 us -> 0.71 us  [the longest x1 0.64 us: shards(): lax.dynamic_slice_in_dim(g_small[9:11].reshape(-1), gain_at, gain_w.shape...]
  transfers between devices with their start and end apart: 30 -> 0, of which waited for: 23 -> 0; matrix products, arithmetic and copies ran while one was open for 27% -> 0% of each run, Pallas kernels for 0% -> 0%
where the time goes in v2:
time: 702 us; the launch traced here: 693 us
  Pallas kernels  671 us (96%)
  local copies, waits for them, and re-layouts  20 us (3%)
    pallas_call x2, Pallas kernels, call(): pl.pallas_call(kernel, out_shape=outs, in_specs=specs, out_specs=out_spec...  671 us

profile of v2, /device:TPU:13, one launch (start us, length us, event | category | flops | bytes accessed | tf_op | source)
XLA Modules:
  0.0 693.1 jit_solution(4763602812085679870)
XLA Ops:
  0.6 0.0 copy-start
  0.7 1.0 dynamic_update_slice.7
  1.7 0.1 pad.4.clone
  1.7 0.7 reduce
  2.5 0.3 dynamic_update_slice.6
  2.7 1.6 fusion.3.refs_4_
  4.3 0.9 copy.18
  5.2 0.7 maximum_maximum_fusion.refs_2_
  6.0 1.7 fusion.2.refs_3_
  7.7 0.0 copy-done
  7.7 0.7 fusion.1.refs_6_
  8.5 1.8 fusion.refs_5_
  10.3 292.7 %shard_map.160 = (bf16[2,4,2,96,2304]{4,3,2,1,0:T(8,128)(2,1)}, bf16[2,4,2,96,768]{4,3,2,1,0:T(8,128)(2,1)}, bf16[2,4,2,96,3072]{4,3,2,1,0:T(8,128)(2,1)}, bf16[...) custom-call(bf16[4,2,128,768]{3,2,1,0:T(8,128)(2,1)} %refs_0_.1, ...), custom_call_target="tpu_custom_call" | custom-call | flops 14495514624 | bytes 77254656 | tf_op jit(solution)/shard_map/pallas_call | solution.py:606
  303.0 0.0 copy-start.2
  303.0 377.9 %shard_map.161 = (bf16[1,4,2,128,768]{4,3,2,1,0:T(8,128)(2,1)}, f32[96,2304]{1,0:T(8,128)}, f32[96,768]{1,0:T(8,128)}, f32[96,3072]{1,0:T(8,128)}, f32[384,768]{...) custom-call(bf16[512,768]{1,0:T(8,128)(2,1)} %get-tuple-element.48.r, ...), custom_call_target="tpu_custom_call" | custom-call | flops 28991029248 | bytes 104292352 | tf_op jit(solution)/shard_map/pallas_call | solution.py:606
  680.9 0.7 slice_bitcast_fusion.1
  681.6 0.6 dynamic_slice.23
  682.2 0.7 slice_bitcast_fusion
  682.9 0.1 dynamic_slice.22
  683.0 0.6 broadcast_in_dim.38
  683.6 0.9 fusion.5
  684.5 0.7 copy.20
  685.3 0.0 copy-done.2
  685.3 0.0 copy-start.3
  685.3 1.1 copy.29
  686.4 0.8 copy-done.3
  687.2 0.0 copy-start.6
  687.2 1.1 copy.30
  688.4 0.6 copy-done.6
  689.0 0.0 copy-start.7
  689.0 0.0 copy-start.5
  689.0 0.9 copy.31
  689.9 0.2 copy-done.7
  690.1 0.0 copy-start.4
  690.1 0.7 copy.32
  690.8 0.0 copy-done.5
  690.8 0.0 copy-start.1
  690.8 1.0 copy.33
  691.8 0.0 copy-done.4
  691.8 1.0 copy.34
  692.9 0.0 copy-done.1
  (5 shorter events, 0.0 us)
Async XLA Ops:
  0.6 7.1 %copy-start = (f32[1,384,768]{2,1,0:T(8,128)S(1)}, f32[1,384,768]{2,1,0:T(8,128)}, u32[]{:S(2)}) copy-start(f32[1,384,768]{2,1,0:T(8,128)} %param.14) | copy-start | bytes 3538948
  303.0 382.3 %copy-start.2 = (bf16[1,4,2,128,768]{4,3,2,1,0:T(8,128)(2,1)S(1)}, bf16[1,4,2,128,768]{4,3,2,1,0:T(8,128)(2,1)}, u32[]{:S(2)}) copy-start(bf16[1,4,2,128,768]{4,3,2,1,0:T(8,128)(2,1)} %get-tuple-element.107) | copy-start | bytes 4718596
  685.3 2.0 copy-start.3
  687.2 1.7 copy-start.6
  689.0 1.1 copy-start.7
  689.0 1.8 copy-start.5
  690.1 1.7 copy-start.4
  690.8 2.0 copy-start.1

commit v3 on v2

--- a/solution.py
+++ b/solution.py
@@ -508,7 +508,6 @@
     go: Any
     gu: Any
     gd: Any
-    lay: Any
     gv: Any
     bd: Any
     tok_out: Any
@@ -519,7 +518,9 @@
     tok: Any
     sm: Any
     vec: Any
+    mt: Any
     st: Any
+    stb: Any
     got: Any
     vq: Any
     vo: Any
@@ -532,8 +533,6 @@
     c_recv: Any
     s_send: Any
     s_recv: Any
-    d_send: Any
-    d_recv: Any
     w_sem: Any
     o_sem: Any
     m_sem: Any
@@ -589,6 +588,14 @@
 
 def finish(dst, sem):
     pltpu.make_async_copy(dst, dst, sem).wait()
+
+
+def arrived(dst, recv):
+    finish(dst, recv)
+
+
+def departed(src, send):
+    finish(src, send)
 
 
 def shape(dims, kind):
@@ -637,6 +644,17 @@
     return p / half_sums(p, low)
 
 
+def split_states(src, dst):
+    hi = src[...].astype(bf16)
+    dst[0:STATE_ROWS] = hi
+    dst[STATE_ROWS:] = (src[D:] - hi[D:].astype(f32)).astype(bf16)
+
+
+def add_states(dst, src):
+    dst[...] += src[0:STATE_ROWS].astype(f32)
+    dst[D:] += src[STATE_ROWS:].astype(f32)
+
+
 class Place:
     def __init__(self, n):
         self.n, self.nz, self.group = n, n // 2, n // 4
@@ -644,8 +662,8 @@
         self.d = lax.axis_index("dp")
         self.j = lax.axis_index("seq")
         self.z, self.y = lax.div(self.j, 2), lax.rem(self.j, 2)
-        self.i = lax.div(self.j, self.group)
-        self.jj = lax.rem(self.j, self.group)
+        self.i = lax.rem(self.z, 2) * 2 + self.y
+        self.jj = lax.div(self.z, 2)
         self.r = self.x * self.group + self.jj
 
     def at(self, x=None, d=None, z=None, y=None, j=None):
@@ -657,6 +675,10 @@
 
     def zpos(self, o):
         return lax.rem(self.z + o + self.nz, self.nz)
+
+    def member(self, r):
+        z = lax.rem(r, self.group) * 2 + lax.rem(self.z, 2)
+        return (lax.div(r, self.group), self.d, z * 2 + self.y)
 
     def meet(self):
         barrier = pltpu.get_barrier_semaphore()
@@ -695,8 +717,8 @@
             return slice(None)
         return pl.ds(pl.multiple_of(self.p.d * self.width, CH), self.width)
 
-    def shard(self, x, z, y):
-        return self.buf.at[x, z, y, :, self.columns()]
+    def shard(self, x, o, y):
+        return self.buf.at[x, self.p.zpos(-o), y, :, self.columns()]
 
     def column(self, x, y):
         return self.buf.at[x, :, y, :, self.columns()]
@@ -706,73 +728,87 @@
         self.sent.append(slot)
 
     def got(self, ref, slot):
-        finish(ref, self.recv.at[slot])
+        arrived(ref, self.recv.at[slot])
 
     def start(self):
         p = self.p
-        own = self.shard(p.x, p.z, p.y)
+        own = self.shard(p.x, 0, p.y)
         pltpu.make_async_copy(self.src, own, self.local).start()
         for o in range(1, p.nz):
             self.go(self.src, own, o - 1, p.at(z=p.zpos(o)))
+        self.first(0)
 
     def first(self, o):
         p = self.p
-        zi = p.zpos(-o)
-        here = self.shard(p.x, zi, p.y)
-        src = self.src if o == 0 else here
+        here = self.shard(p.x, o, p.y)
         if o > 0:
             self.got(here, o - 1)
+        src = self.src if o == 0 else here
         self.go(src, here, 3 + o, p.at(y=1 - p.y))
         self.go(src, here, 7 + o, p.at(x=1 - p.x))
 
-    def second(self, o):
+    def firsts(self):
+        for o in range(1, self.p.nz):
+            self.first(o)
+        finish(self.shard(self.p.x, 0, self.p.y), self.local)
+        self.core(0)
+
+    def seconds(self):
         p = self.p
-        zi = p.zpos(-o)
-        if self.y_last:
-            here = self.shard(1 - p.x, zi, p.y)
-            self.got(here, 7 + o)
-            self.go(here, here, 11 + o, p.at(y=1 - p.y))
-        else:
-            here = self.shard(p.x, zi, 1 - p.y)
-            self.got(here, 3 + o)
-            self.go(here, here, 11 + o, p.at(x=1 - p.x))
+        for o in range(p.nz):
+            if self.y_last:
+                here = self.shard(1 - p.x, o, p.y)
+                self.got(here, 7 + o)
+                self.go(here, here, 11 + o, p.at(y=1 - p.y))
+            else:
+                here = self.shard(p.x, o, 1 - p.y)
+                self.got(here, 3 + o)
+                self.go(here, here, 11 + o, p.at(x=1 - p.x))
+        self.core(2 if self.y_last else 1)
+
+    def thirds(self):
+        q = 1 if self.y_last else 2
+        self.wait_all(q)
+        self.core(q)
+
+    def last(self):
+        self.wait_all(3)
+        self.core(3)
+
+    def kind(self, q):
+        p = self.p
+        return (p.x if q < 2 else 1 - p.x), (p.y if q % 2 == 0 else 1 - p.y)
+
+    def wait_all(self, q):
+        x, y = self.kind(q)
+        for o in range(self.p.nz):
+            self.got(self.shard(x, o, y), (0, 3, 7, 11)[q] + o)
 
     def core(self, q):
-        p = self.p
-        x = p.x if q < 2 else 1 - p.x
-        y = p.y if q % 2 == 0 else 1 - p.y
-        if q == 0:
-            own = self.shard(p.x, p.z, p.y)
-            finish(own, self.local)
-        elif q == 3 or q == (1 if self.y_last else 2):
-            base = 11 if q == 3 else (3 if self.y_last else 7)
-            for o in range(p.nz):
-                self.got(self.shard(x, p.zpos(-o), y), base + o)
         if self.halves:
-            part = self.column(x, y)
-            self.go(part, part, 15 + q, p.at(d=1 - p.d))
+            part = self.column(*self.kind(q))
+            self.go(part, part, 15 + q, self.p.at(d=1 - self.p.d))
 
     def done(self):
-        p = self.p
         if self.halves:
+            p = self.p
+            other = pl.ds(pl.multiple_of((1 - p.d) * self.width, CH), self.width)
             for q in range(4):
-                x = p.x if q < 2 else 1 - p.x
-                y = p.y if q % 2 == 0 else 1 - p.y
-                other = pl.ds(pl.multiple_of((1 - p.d) * self.width, CH), self.width)
+                x, y = self.kind(q)
                 self.got(self.buf.at[x, :, y, :, other], 15 + q)
 
     def close(self):
         p = self.p
         for slot in self.sent:
-            ref = self.column(p.x, p.y) if slot >= 15 else self.shard(p.x, p.z, p.y)
-            finish(ref, self.send.at[slot])
+            ref = self.column(p.x, p.y) if slot >= 15 else self.shard(p.x, 0, p.y)
+            departed(ref, self.send.at[slot])
 
 
 def forward_kernel(n, *refs):
-    ref = ForwardRefs(*refs[:16])
-    saved = [Kept(*refs[16:28]), Kept(*refs[28:40])]
-    v = Kept(*refs[40:52])
-    own = ForwardScratch(*refs[52:])
+    ref = ForwardRefs(*refs[:15])
+    saved = [Kept(*refs[15:27]), Kept(*refs[27:39])]
+    v = Kept(*refs[39:51])
+    own = ForwardScratch(*refs[51:])
     p = Place(n)
     nz, group = p.nz, p.group
     t = v.a.shape[0]
@@ -793,7 +829,7 @@
 
     def collect(which, s):
         i = lax.rem(p.j + s, 4)
-        to = i * group + lax.div(p.j, 4)
+        to = (lax.div(p.z, 2) * 2 + lax.div(i, 2)) * 2 + lax.rem(i, 2)
         slot = lax.rem(p.j, 4)
         src = (ref.cot if which else ref.tokens).at[i, p.x]
         dst = (ref.cot_out if which else own.tok).at[span(slot, CH), :]
@@ -815,28 +851,18 @@
 
         return close
 
-    gs.start()
-    gs.first(0)
-    gq.start()
-    gq.first(0)
     closing = [collect(0, s) for s in range(4)]
-    for o in range(1, nz):
-        gs.first(o)
-        gq.first(o)
-    go.start()
-    gu.start()
-    go.first(0)
-    gu.first(0)
-    for o in range(nz):
-        gs.second(o)
-    for o in range(nz):
-        gq.second(o)
-    for q in range(4):
-        gs.core(q)
-    for q in range(3):
-        gq.core(q)
-
-    vec, gv, bd, sm = own.vec, ref.gv, ref.bd, own.sm
+    for g in gathers:
+        g.start()
+    gs.firsts()
+    gq.firsts()
+    gs.seconds()
+    go.firsts()
+    gq.seconds()
+    gs.thirds()
+    gs.last()
+
+    vec, gv, bd, sm, mt = own.vec, ref.gv, ref.bd, own.sm, own.mt
     vec[...] = jnp.zeros(vec.shape, f32)
     gv[...] = jnp.zeros(gv.shape, f32)
     bd[...] = jnp.zeros(bd.shape, bf16)
@@ -848,12 +874,19 @@
             gv[layer, grow : grow + 2, :] += part[9:11]
         for head in range(2 * H):
             k, at, odd = head // 3, 16 + (head % 3) * HEAD, head % 2
-            bd[layer, head // 2, odd * HEAD : (odd + 1) * HEAD, odd * CH : (odd + 1) * CH] = sm[
-                layer, k // 2, k % 2, at : at + HEAD, :
-            ]
+            both = sm[layer, k // 2, k % 2, at : at + HEAD, :].astype(f32)
+            flip = pltpu.roll(both, HEAD, 1)
+            rows = pl.ds(odd * HEAD, HEAD)
+            signed = jnp.where(lanes(HEAD) < HEAD, both, -flip)
+            bd[layer, head // 2, rows, odd * CH : (odd + 1) * CH] = signed.astype(bf16)
+            if odd:
+                turned = jnp.where(lanes(HEAD) < HEAD, 0.0, both)
+            else:
+                turned = jnp.where(lanes(HEAD) < HEAD, flip, 0.0)
+            mt[layer, head // 2, rows, :] = turned.astype(bf16)
 
     for k in range(4):
-        finish(own.tok.at[pl.ds(k * CH, CH), :], own.c_recv.at[0, k])
+        arrived(own.tok.at[pl.ds(k * CH, CH), :], own.c_recv.at[0, k])
 
     def load(g, dst, layer, k):
         pltpu.make_async_copy(g.buf.at[layer], dst, own.w_sem.at[k]).start()
@@ -861,16 +894,21 @@
     def loaded(dst, k):
         finish(dst, own.w_sem.at[k])
 
-    pending = [[], []]
-
-    def save(layer, *sources):
+    def save(layer, *sources, part=None):
         for src in sources:
             k = [src is x for x in v].index(True)
+            dst = saved[layer][k]
             if src is v.res:
                 src = src.at[layer]
-            copy = pltpu.make_async_copy(src, saved[layer][k], own.o_sem.at[layer, k])
-            copy.start()
-            pending[layer].append(copy)
+            if part is not None:
+                cols = pl.ds(part * (FF // 2), FF // 2)
+                src, dst = src.at[:, cols], dst.at[:, cols]
+            pltpu.make_async_copy(src, dst, own.o_sem.at[layer, k]).start()
+
+    def saved_all(layer, *sources):
+        for src in sources:
+            k = [src is x for x in v].index(True)
+            finish(src.at[layer] if src is v.res else src, own.o_sem.at[layer, k])
 
     flat = Weights(
         own.vq.reshape(D, 3 * D),
@@ -880,6 +918,8 @@
     )
     low = lanes(CH) < HEAD
     tril = lax.broadcasted_iota(jnp.int32, (CH, CH), 0) >= lanes(CH)
+    eye = jnp.where(lax.broadcasted_iota(jnp.int32, (CH, CH), 0) == lanes(CH), 1.0, 0.0)
+    eye = eye.astype(bf16)
 
     def norm_rows(layer, src, dst, which, shift):
         gain = wide(gv, layer, which * 6, 6)
@@ -897,8 +937,7 @@
     def project(layer, u, events):
         a, qkv, ph, st = v.a, v.qkv, v.ph, own.st
         if layer == 1:
-            for copy in pending[0]:
-                copy.wait()
+            saved_all(0, v.a, v.qkv, v.ph)
         norm_rows(layer, u, a, 0, SHIFT1)
         loaded(own.vq, 0)
         save(layer, v.a)
@@ -913,17 +952,18 @@
         save(layer, v.qkv)
 
         def pair(k):
-            def rows(i):
-                lg = nn(qkv[span(i, CH), span(k, CH)], bd[layer, k])
-                for hh in range(2):
-                    ph[span(i, CH), span(2 * k + hh, CH)] = half_softmax(
-                        lg[:, hh * CH : (hh + 1) * CH], low
-                    ).astype(bf16)
-
-            loop(nc, rows)
-
-        loop(2 * PAIRS, pair, events[1])
-        save(layer, v.ph)
+            logits = nt(mt[layer, k], qkv[:, span(k, CH)]).reshape(2, HEAD, t)
+            up = jnp.exp(logits - jnp.max(logits, 1, keepdims=True))
+            down = jnp.exp(jnp.min(logits, 1, keepdims=True) - logits)
+            up = up * (1.0 / jnp.sum(up, 1, keepdims=True))
+            down = down * (1.0 / jnp.sum(down, 1, keepdims=True))
+            both = jnp.concatenate([up, down], 1).reshape(2 * CH, t).astype(bf16)
+            for c in range(nc):
+                ph[pl.ds(c * CH, CH), span(k, 2 * CH)] = nt(
+                    eye, both[:, c * CH : (c + 1) * CH]
+                ).astype(bf16)
+
+        loop(PAIRS, lambda k: pair(k + PAIRS), events[1])
 
         def state(k):
             val = qkv[:, pl.ds(pl.multiple_of(2 * D + k * CH, CH), CH)]
@@ -937,13 +977,12 @@
 
         loop(PAIRS, state)
         st[layer, D + H :, :] = jnp.zeros((STATE_ROWS - D - H, CH), f32)
+        split_states(st.at[layer], own.stb.at[layer])
         send_states(layer, st, 1)
+        loop(PAIRS, pair, events[2])
+        save(layer, v.ph)
 
     members = 2 * group
-
-    def state_to(o, sign):
-        other = p.r + sign * o
-        return (lax.div(other, group), p.d, p.i * group + lax.rem(other, group))
 
     def send_states(layer, st, sign):
         for o in range(1, members):
@@ -952,11 +991,11 @@
             @pl.when(ok)
             def _():
                 remote(
-                    st.at[layer],
+                    own.stb.at[layer],
                     own.got.at[layer, o - 1],
                     own.s_send.at[layer, o - 1],
                     own.s_recv.at[layer, o - 1],
-                    state_to(o, sign),
+                    p.member(p.r + sign * o),
                 ).start()
 
     def take_states(layer, sign):
@@ -967,8 +1006,8 @@
 
             @pl.when(ok)
             def _():
-                finish(own.got.at[layer, o - 1], own.s_recv.at[layer, o - 1])
-                pre[...] += own.got[layer, o - 1]
+                arrived(own.got.at[layer, o - 1], own.s_recv.at[layer, o - 1])
+                add_states(pre, own.got.at[layer, o - 1])
 
     def close_states(layer, sign):
         for o in range(1, members):
@@ -976,13 +1015,17 @@
 
             @pl.when(ok)
             def _():
-                finish(own.st.at[layer], own.s_send.at[layer, o - 1])
+                departed(own.stb.at[layer], own.s_send.at[layer, o - 1])
 
     def mix(layer, u, events):
         qkv, ph, o_, inv, ob = v.qkv, v.ph, v.o, v.inv, v.ob
         r, n2, hid, gp = v.r, v.n2, v.hid, v.gp
         res = v.res.at[layer]
+        if layer == 1:
+            saved_all(0, v.pre, v.o, v.inv, v.ob, v.r, v.n2, v.hid, v.gp)
         take_states(layer, 1)
+        if layer == 1:
+            closing.extend([collect(1, s) for s in range(4)])
         save(layer, v.pre)
         s0 = v.pre
 
@@ -994,13 +1037,16 @@
                 rows = pl.ds(c * CH, CH)
                 val = qkv[rows, pl.ds(pl.multiple_of(2 * D + k * CH, CH), CH)]
                 sl = s.astype(bf16)
+                sf = (s - sl.astype(f32)).astype(bf16)
                 done = []
                 new = []
                 for hh in range(2):
                     qh = ph[rows, span(2 * k + hh, CH)]
                     kh = ph[rows, pl.ds(pl.multiple_of((H + 2 * k + hh) * CH, CH), CH)]
                     score = jnp.where(tril, nt(qh, kh), 0.0)
-                    num = nn(score.astype(bf16), val) + nt(qh, sl)
+                    hi = score.astype(bf16)
+                    lo = (score - hi.astype(f32)).astype(bf16)
+                    num = nn(hi, val) + nn(lo, val) + nt(qh, sl) + nt(qh, sf)
                     den = jnp.sum(score + qh.astype(f32) * tot[hh], -1, keepdims=True)
                     rec = 1.0 / den
                     done.append((num * rec, rec))
@@ -1035,15 +1081,15 @@
             cols = span(j, TILE)
             zt = nn(n2[...], flat.u[:, cols]) + bias_cols(layer, UP_BIAS, j)
             z2 = zt * zt
-            th = jnp.tanh(GELU_C * zt * (1.0 + GELU_A * z2))
-            half = 0.5 * (1.0 + th)
-            hid[:, cols] = (zt * half).astype(bf16)
-            gp[:, cols] = (
-                half + 0.5 * zt * (1.0 - th * th) * (GELU_C * (1.0 + 3.0 * GELU_A * z2))
-            ).astype(bf16)
-
-        loop(FF // TILE, up_col, events[3])
-        save(layer, v.hid, v.gp)
+            half = 0.5 + 0.5 * jnp.tanh(zt * (GELU_C + (GELU_C * GELU_A) * z2))
+            act = zt * half
+            hid[:, cols] = act.astype(bf16)
+            slope = 2.0 * GELU_C + (6.0 * GELU_C * GELU_A) * z2
+            gp[:, cols] = (half + act * ((1.0 - half) * slope)).astype(bf16)
+
+        halfway = FF // TILE // 2 - 1
+        loop(FF // TILE, up_col, {halfway: lambda: save(layer, v.hid, v.gp, part=0), **events[3]})
+        save(layer, v.hid, v.gp, part=1)
         events[4]()
         loaded(own.vd, 3)
 
@@ -1055,30 +1101,6 @@
 
         loop(D // TILE, down_col)
         save(layer, v.res)
-        for k in range(4):
-            to = p.jj * 4 + k
-            src = res.at[pl.ds(k * CH, CH), :]
-            dst = ref.lay.at[0, p.i, p.x]
-            slot = p.i * 2 + p.x
-            mine = (to == p.j) & (p.x == layer)
-            copy = remote(
-                src, dst, own.d_send.at[layer, k], own.d_recv.at[slot], p.at(x=layer, j=to)
-            )
-
-            @pl.when(jnp.logical_not(mine))
-            def _():
-                copy.start()
-
-            @pl.when(mine)
-            def _():
-                pltpu.make_async_copy(src, dst, own.d_recv.at[slot]).start()
-
-            def close(copy=copy, mine=mine):
-                @pl.when(jnp.logical_not(mine))
-                def _():
-                    copy.wait_send()
-
-            closing.append(close)
 
     def run(*steps):
         def go_():
@@ -1087,60 +1109,36 @@
 
         return go_
 
-    def each(count, fn, first=0):
-        return [functools.partial(fn, o) for o in range(first, count)]
-
     nothing = run()
-    gq.core(3)
+    gu.firsts()
+    go.seconds()
+    gq.thirds()
+    gq.last()
     gq.done()
     load(gq, own.vq, 0, 0)
     tok_out = pltpu.make_async_copy(own.tok, ref.tok_out, own.m_sem)
     tok_out.start()
-    project(
-        0,
-        own.tok,
-        [
-            {
-                1: run(*each(nz, go.first, 1)),
-                3: run(functools.partial(gu.first, 1)),
-                5: run(functools.partial(gu.first, 2)),
-                7: run(functools.partial(gu.first, 3), gd.start, functools.partial(gd.first, 0)),
-            },
-            {
-                1: run(*each(nz, go.second)),
-                3: run(*each(2, gu.second)),
-                5: run(functools.partial(gu.second, 2), *each(3, go.core)),
-                7: run(functools.partial(gu.second, 3), functools.partial(gd.first, 1)),
-                9: run(*each(3, gu.core), functools.partial(gd.first, 2)),
-                11: run(functools.partial(gd.first, 3)),
-            },
-        ],
-    )
+    project(0, own.tok, [{}, {0: gd.firsts, 4: gu.seconds}, {1: go.thirds, 3: gd.seconds}])
     mix(
         0,
         own.tok,
         [
-            {
-                1: run(functools.partial(go.core, 3), *each(2, gd.second)),
-                3: run(*each(nz, gd.second, 2)),
-            },
-            run(go.done, functools.partial(load, go, own.vo, 0, 1), *each(3, gd.core)),
-            run(
-                functools.partial(gu.core, 3), gu.done, functools.partial(load, gu, own.vu, 0, 2)
-            ),
+            {1: go.last, 2: gu.thirds},
+            run(go.done, functools.partial(load, go, own.vo, 0, 1), gd.thirds),
+            run(gu.last, gu.done, functools.partial(load, gu, own.vu, 0, 2)),
             {},
             run(
-                functools.partial(gd.core, 3),
-                gd.done,
-                functools.partial(load, gd, own.vd, 0, 3),
                 functools.partial(load, gq, own.vq, 1, 0),
                 functools.partial(load, go, own.vo, 1, 1),
                 functools.partial(load, gu, own.vu, 1, 2),
+                gd.last,
+                gd.done,
+                functools.partial(load, gd, own.vd, 0, 3),
             ),
         ],
     )
-    closing.extend([collect(1, s) for s in range(4)])
-    project(1, v.res.at[0], [{}, {0: functools.partial(load, gd, own.vd, 1, 3)}])
+    load(gd, own.vd, 1, 3)
+    project(1, v.res.at[0], [{}, {}, {}])
     mix(1, v.res.at[0], [{}, nothing, nothing, {}, nothing])
 
     for g in gathers:
@@ -1148,18 +1146,13 @@
     for close in closing:
         close()
     for k in range(4):
-        finish(ref.cot_out.at[pl.ds(k * CH, CH), :], own.c_recv.at[1, k])
+        arrived(ref.cot_out.at[pl.ds(k * CH, CH), :], own.c_recv.at[1, k])
     for layer in range(2):
         close_states(layer, 1)
 
-        @pl.when(p.x == layer)
-        def _():
-            for slot in range(8):
-                finish(ref.lay.at[0, slot // 2, slot % 2], own.d_recv.at[slot])
-
     tok_out.wait()
-    for copy in pending[1]:
-        copy.wait()
+    saved_all(0, v.res)
+    saved_all(1, *v)
 
 
 def forward_pass(n, tokens, cotangent, small, wq, wo, wu, wd):
@@ -1182,23 +1175,24 @@
         shape((t, D), bf16),
         shape((STATE_ROWS, CH), f32),
     ]
-    outs = full + [shape((1, 4, 2, CH, D), bf16)]
-    outs += [shape((2, GAIN_ROWS, CH), f32), shape((2, 2 * PAIRS, CH, 2 * CH), bf16)]
+    outs = full + [shape((2, GAIN_ROWS, CH), f32), shape((2, 2 * PAIRS, CH, 2 * CH), bf16)]
     outs += [shape((t, D), bf16)] * 2 + kept * 2
-    specs = [ANY] * 5 + [VMEM] * 2 + [ANY] * (len(outs) - 7)
+    specs = [ANY] * 4 + [VMEM] * 2 + [ANY] * (len(outs) - 6)
     scratch = [pltpu.VMEM(k.shape, k.dtype) for k in kept]
     scratch[10] = pltpu.VMEM((2, t, D), bf16)
     scratch += [
         pltpu.VMEM((t, D), bf16),
         pltpu.VMEM((2, nz, 2, SMALL_ROWS, CH), bf16),
         pltpu.VMEM((2, VEC_ROWS, CH), f32),
+        pltpu.VMEM((2, 2 * PAIRS, CH, CH), bf16),
         pltpu.VMEM((2, STATE_ROWS, CH), f32),
-        pltpu.VMEM((2, n // 2 - 1, STATE_ROWS, CH), f32),
+        pltpu.VMEM((2, STATE_ROWS + 16, CH), bf16),
+        pltpu.VMEM((2, n // 2 - 1, STATE_ROWS + 16, CH), bf16),
     ]
     scratch += [pltpu.VMEM(w.shape[1:], bf16) for w in full]
     dma = pltpu.SemaphoreType.DMA
     scratch += [dma((5, 19)), dma((5, 19)), dma((5,)), dma((2, 4)), dma((2, 4))]
-    scratch += [dma((2, n // 2 - 1)), dma((2, n // 2 - 1)), dma((2, 4)), dma((8,)), dma((4,))]
+    scratch += [dma((2, n // 2 - 1)), dma((2, n // 2 - 1)), dma((4,))]
     scratch += [dma((2, 12)), dma]
     got = call(
         functools.partial(forward_kernel, n),
@@ -1210,8 +1204,8 @@
         specs,
         cid=0,
     )
-    layers = [Kept(*got[9:21]), Kept(*got[21:33])]
-    return got[:4], got[4], got[5], got[6], got[7], got[8], layers
+    layers = [Kept(*got[8:20]), Kept(*got[20:32])]
+    return got[:4], got[4], got[5], got[6], got[7], layers
 
 
 def with_error(gv, swapped, lane, hh):
@@ -1273,8 +1267,8 @@
         self.go(self.buf, self.land_d, 0, self.p.at(d=1 - self.p.d))
 
     def got_core(self):
-        finish(self.buf, self.send.at[0])
-        finish(self.land_d, self.recv.at[0])
+        departed(self.buf, self.send.at[0])
+        arrived(self.land_d, self.recv.at[0])
 
     def send_y(self):
         p = self.p
@@ -1282,7 +1276,7 @@
 
     def step_y(self):
         p = self.p
-        finish(self.land_y, self.recv.at[1])
+        arrived(self.land_y, self.recv.at[1])
         self.fetch(self.land_y, self.temp)
         for i in range(1, p.nz + 1):
             zi = p.zpos(i)
@@ -1295,7 +1289,7 @@
     def step_z(self):
         p = self.p
         for i in range(1, p.nz):
-            finish(self.land_z.at[i - 1], self.recv.at[1 + i])
+            arrived(self.land_z.at[i - 1], self.recv.at[1 + i])
         self.fetch(self.land_z, self.temp.at[pl.ds(0, p.nz - 1)])
         total = self.buf[p.z, p.y].astype(f32)
         for i in range(p.nz - 1):
@@ -1321,7 +1315,7 @@
 
         @pl.when(p.x == self.layer)
         def _():
-            finish(self.land_x, self.recv.at[5])
+            arrived(self.land_x, self.recv.at[5])
             self.fetch(self.land_x, self.temp.at[0])
             self.fin[...] += self.temp[0].astype(f32)
             own = self.out.at[:, self.half()]
@@ -1330,19 +1324,19 @@
 
     def close(self):
         p = self.p
-        finish(self.buf.at[:, 0], self.send.at[1])
+        departed(self.buf.at[:, 0], self.send.at[1])
         for i in range(1, p.nz):
-            finish(self.buf.at[0, 0], self.send.at[1 + i])
+            departed(self.buf.at[0, 0], self.send.at[1 + i])
 
         @pl.when(p.x != self.layer)
         def _():
-            finish(self.buf.at[0, 0], self.send.at[5])
+            departed(self.buf.at[0, 0], self.send.at[5])
 
     def end(self):
         @pl.when(self.p.x == self.layer)
         def _():
-            finish(self.fin, self.send.at[6])
-            finish(self.out.at[:, self.other()], self.recv.at[6])
+            departed(self.fin, self.send.at[6])
+            arrived(self.out.at[:, self.other()], self.recv.at[6])
             finish(self.fin, self.last)
 
 
@@ -1360,14 +1354,14 @@
 
     def step_d(self):
         p = self.p
-        finish(self.buf, self.send.at[0])
-        finish(self.land_d, self.recv.at[0])
+        departed(self.buf, self.send.at[0])
+        arrived(self.land_d, self.recv.at[0])
         self.buf[...] += self.land_d[...]
         self.go(self.buf.at[:, 1 - p.y], self.land_y, 1, p.at(y=1 - p.y))
 
     def step_y(self):
         p = self.p
-        finish(self.land_y, self.recv.at[1])
+        arrived(self.land_y, self.recv.at[1])
         for i in range(1, p.nz + 1):
             zi = p.zpos(i)
             self.buf[zi, p.y] += self.land_y[zi]
@@ -1377,7 +1371,7 @@
     def step_z(self):
         p = self.p
         for i in range(1, p.nz):
-            finish(self.land_z.at[i - 1], self.recv.at[1 + i])
+            arrived(self.land_z.at[i - 1], self.recv.at[1 + i])
         total = self.buf[p.z, p.y]
         for i in range(p.nz - 1):
             total = total + self.land_z[i]
@@ -1392,18 +1386,18 @@
 
         @pl.when(p.x == self.layer)
         def _():
-            finish(self.land_x, self.recv.at[5])
+            arrived(self.land_x, self.recv.at[5])
             self.out[...] = self.buf[p.z, p.y] + self.land_x[...]
 
     def close(self):
         p = self.p
-        finish(self.buf.at[:, 0], self.send.at[1])
+        departed(self.buf.at[:, 0], self.send.at[1])
         for i in range(1, p.nz):
-            finish(self.buf.at[0, 0], self.send.at[1 + i])
+            departed(self.buf.at[0, 0], self.send.at[1 + i])
 
         @pl.when(p.x != self.layer)
         def _():
-            finish(self.buf.at[0, 0], self.send.at[5])
+            departed(self.buf.at[0, 0], self.send.at[5])
 
 
 SMALL_OUT = 112
@@ -1425,6 +1419,8 @@
 
 class BackwardRefs(NamedTuple):
     cot: Any
+    res0: Any
+    res1: Any
     gv: Any
     bd: Any
     wq: Any
@@ -1440,6 +1436,8 @@
     tmp: Any
     acc: Any
     st: Any
+    stb: Any
+    later: Any
     got: Any
     mg: Any
     vr: Any
@@ -1486,14 +1484,14 @@
 
 
 def backward_kernel(n, *refs):
-    ref = BackwardRefs(*refs[:7])
-    source = [Loaded(*refs[7:18]), Loaded(*refs[18:29])]
-    hidden = refs[29:31]
-    gin, small_out = refs[31], refs[36]
-    wgrads = refs[32:36]
-    lands = refs[37:69]
-    v = Loaded(*refs[69:80])
-    own = BackwardScratch(*refs[80:])
+    ref = BackwardRefs(*refs[:9])
+    source = [Loaded(*refs[9:20]), Loaded(*refs[20:31])]
+    hidden = refs[31:33]
+    lay, gin, small_out = refs[33], refs[34], refs[39]
+    wgrads = refs[35:39]
+    lands = refs[40:72]
+    v = Loaded(*refs[72:83])
+    own = BackwardScratch(*refs[83:])
     p = Place(n)
     nz, group = p.nz, p.group
     t = own.drb.shape[0]
@@ -1585,42 +1583,34 @@
 
     def send_states(layer):
         for o in range(1, members):
-            other = p.r - o
-
             @pl.when(states_ok(o, False))
             def _():
                 remote(
-                    own.st.at[layer],
+                    own.stb.at[layer],
                     own.got.at[layer, o - 1],
                     own.s_send.at[layer, o - 1],
                     own.s_recv.at[layer, o - 1],
-                    (lax.div(other, group), p.d, p.i * group + lax.rem(other, group)),
+                    p.member(p.r - o),
                 ).start()
 
     def take_states(layer):
-        acc0 = own.got.at[layer, 0]
+        later = own.later
+        later[...] = jnp.zeros(later.shape, f32)
         for o in range(1, members):
 
             @pl.when(states_ok(o, True))
             def _():
-                finish(own.got.at[layer, o - 1], own.s_recv.at[layer, o - 1])
-                if o > 1:
-                    acc0[...] += own.got[layer, o - 1]
-
-            if o == 1:
-
-                @pl.when(jnp.logical_not(states_ok(o, True)))
-                def _():
-                    acc0[...] = jnp.zeros(acc0.shape, f32)
-
-        return acc0
+                arrived(own.got.at[layer, o - 1], own.s_recv.at[layer, o - 1])
+                add_states(later, own.got.at[layer, o - 1])
+
+        return later
 
     def close_states(layer):
         for o in range(1, members):
 
             @pl.when(states_ok(o, False))
             def _():
-                finish(own.st.at[layer], own.s_send.at[layer, o - 1])
+                departed(own.stb.at[layer], own.s_send.at[layer, o - 1])
 
     def norm_back(x_ref, which, layer, body):
         gain = wide(gains, layer, which * 6, 6)
@@ -1706,6 +1696,7 @@
 
         loop(PAIRS, pair)
         st[layer, D + H :, :] = jnp.zeros((STATE_ROWS - D - H, CH), f32)
+        split_states(st.at[layer], own.stb.at[layer])
         send_states(layer)
 
     def weight_grad(layer, m, keep):
@@ -1790,12 +1781,15 @@
             def keys(rows, hh):
                 return ph[rows, pl.ds(pl.multiple_of((H + 2 * k + hh) * CH, CH), CH)]
 
-            before = []
+            before, finer = [], []
             s = s0[cols, :]
             tot = [s0[pl.ds(D + 2 * k + hh, 1), :] for hh in range(2)]
             for c in range(nc):
                 rows = pl.ds(c * CH, CH)
+                fine = (s - s.astype(bf16).astype(f32)).astype(bf16)
+                none = jnp.zeros_like(fine)
                 before.append([with_totals(s, tot[hh], row, hh, True) for hh in range(2)])
+                finer.append([jnp.where(row < HEAD, fine, none), jnp.where(row < HEAD, none, fine)])
                 if c < nc - 1:
                     val = qkv[rows, vcols]
                     new = []
@@ -1825,7 +1819,7 @@
                     da = jnp.where(tril, nt(ge, v1), 0.0).astype(bf16)
                     dat = jnp.where(triu, nt(v1, ge), 0.0).astype(bf16)
                     at = jnp.where(triu, nt(kh, qh), 0.0).astype(bf16)
-                    dq = nn(da, kh) + nn(ge, before[c][hh])
+                    dq = nn(da, kh) + nn(ge, before[c][hh]) + nn(ge, finer[c][hh])
                     dk = nn(dat, qh) + nn(v1, after)
                     dv.append(nn(at, gv) + nt(kh, dsl))
                     for p_, d_, to in ((qh, dq, dl_q), (kh, dk, dl_k)):
@@ -1874,16 +1868,16 @@
 
     closing = []
 
-    def deliver(layer):
+    def deliver(which, layer, rows):
+        out = gin if which else lay
+        send, recv = own.d_send.at[which, layer], own.d_recv.at[which]
         for k in range(4):
             to = p.jj * 4 + k
-            src = gbuf.at[layer, pl.ds(k * CH, CH), :]
-            dst = gin.at[0, p.i, p.x]
+            src = rows.at[pl.ds(k * CH, CH), :]
+            dst = out.at[0, p.i, p.x]
             slot = p.i * 2 + p.x
             mine = (to == p.j) & (p.x == layer)
-            copy = remote(
-                src, dst, own.d_send.at[layer, k], own.d_recv.at[slot], p.at(x=layer, j=to)
-            )
+            copy = remote(src, dst, send.at[k], recv.at[slot], p.at(x=layer, j=to))
 
             @pl.when(jnp.logical_not(mine))
             def _():
@@ -1891,7 +1885,7 @@
 
             @pl.when(mine)
             def _():
-                pltpu.make_async_copy(src, dst, own.d_recv.at[slot]).start()
+                pltpu.make_async_copy(src, dst, recv.at[slot]).start()
 
             def close(copy=copy, mine=mine):
                 @pl.when(jnp.logical_not(mine))
@@ -1926,6 +1920,8 @@
 
         return all_
 
+    deliver(0, 0, ref.res0)
+    deliver(0, 1, ref.res1)
     mlp_back(1, gbuf.at[0], {})
     load(0, v.o)
     load_w(0, U)
@@ -1941,7 +1937,7 @@
     mix_back(1, {4: r1[DN].step_y})
     load_w(0, Q)
     load(0, v.r, v.inv, v.ph, v.u, v.pre)
-    deliver(1)
+    deliver(1, 1, gbuf.at[1])
     pack_small(1)
     weight_grad(1, Q, False)
     r1[U].step_y()
@@ -1974,7 +1970,7 @@
             3: run(r1[Q].step_x, r0[DN].step_y),
         },
     )
-    deliver(0)
+    deliver(1, 0, gbuf.at[0])
     pack_small(0)
     weight_grad(0, Q, False)
     r0[U].step_y()
@@ -2005,8 +2001,9 @@
 
         @pl.when(p.x == layer)
         def _():
-            for slot in range(8):
-                finish(gin.at[0, slot // 2, slot % 2], own.d_recv.at[slot])
+            for which, out in enumerate((lay, gin)):
+                for slot in range(8):
+                    arrived(out.at[0, slot // 2, slot % 2], own.d_recv.at[which, slot])
 
     for close in closing:
         close()
@@ -2015,14 +2012,14 @@
 def backward_pass(n, cot, gains, bds, full, tokens, kept):
     t = cot.shape[0]
     nz = n // 2
-    args = [cot, gains, bds] + list(full)
+    args = [cot, kept[0].res, kept[1].res, gains, bds] + list(full)
     for u, k in zip((tokens, kept[0].res), kept):
         read = Loaded(k.gp, k.r, k.o, k.inv, k.ph, k.qkv, k.n2, k.ob, k.a, u, k.pre)
         args += list(read)
     args += [k.hid for k in kept]
     widths = (3 * D // 2, D // 2, FF // 2, D // 2)
     rows = (D // n, D // n, D // n, FF // n)
-    outs = [shape((1, 4, 2, CH, D), bf16)]
+    outs = [shape((1, 4, 2, CH, D), bf16)] * 2
     outs += [shape((r, 2 * c), f32) for r, c in zip(rows, widths)]
     outs += [shape((SMALL_OUT, CH), f32)]
     for _ in range(2):
@@ -2033,8 +2030,8 @@
                 shape((nz - 1, r, c), bf16),
                 shape((r, c), bf16),
             ]
-    specs = [ANY] * 5 + [VMEM] + [ANY] * (len(outs) - 6)
-    ins = [ANY, VMEM, VMEM] + [ANY] * (len(args) - 3)
+    specs = [ANY] * 6 + [VMEM] + [ANY] * (len(outs) - 7)
+    ins = [ANY] * 3 + [VMEM] * 2 + [ANY] * (len(args) - 5)
     scratch = [pltpu.VMEM(a.shape, a.dtype) for a in read]
 
     def vmem(*dims, kind=f32):
@@ -2046,7 +2043,9 @@
     vmem(t, D)
     vmem(8, D)
     vmem(2, STATE_ROWS, CH)
-    vmem(2, n // 2 - 1, STATE_ROWS, CH)
+    vmem(2, STATE_ROWS + 16, CH, kind=bf16)
+    vmem(STATE_ROWS, CH)
+    vmem(2, n // 2 - 1, STATE_ROWS + 16, CH, kind=bf16)
     vmem(2 * H, HEAD, CH)
     vmem(2, VEC_ROWS, CH)
     vmem(2, GAIN_ROWS, CH)
@@ -2069,7 +2068,7 @@
     vmem(2, SMALL_OUT, CH)
     dma = pltpu.SemaphoreType.DMA
     scratch += [dma((2, 4, 7)), dma((2, 4, 7)), dma((8,)), dma((2, 7)), dma((2, 7))]
-    scratch += [dma((2, n // 2 - 1)), dma((2, n // 2 - 1)), dma((2, 4)), dma((8,)), dma((4,))]
+    scratch += [dma((2, n // 2 - 1)), dma((2, n // 2 - 1)), dma((2, 2, 4)), dma((2, 8)), dma((4,))]
     scratch += [dma((len(read),)), dma((3,)), dma((5,)), dma((3,))]
     got = call(
         functools.partial(backward_kernel, n),
@@ -2081,7 +2080,7 @@
         specs,
         cid=1,
     )
-    return got[:6]
+    return got[:7]
 
 
 def shards(inputs, cotangent, *weights):
@@ -2097,19 +2096,22 @@
         flat = jnp.zeros((rows * CH,), f32)
         return lax.dynamic_update_slice(flat, vector, (offset,)).reshape(rows, CH)
 
+    turned = jnp.swapaxes(map_w.reshape(-1, HEAD, HEAD), 1, 2).reshape(map_w.shape)
     bias_at, gain_at = (j % 4) * 32, (j % 2) * 64
     small = jnp.concatenate(
         [
             placed(bias_w, bias_at, 9),
             placed(gain_w, gain_at, 2),
             jnp.zeros((5, CH), f32),
-            jnp.concatenate([map_w, -map_w], 1),
+            jnp.concatenate([map_w, turned], 1),
         ]
     ).astype(bf16)
-    full, layer_out, gains, bds, tokens, cot, kept = forward_pass(
+    full, gains, bds, tokens, cot, kept = forward_pass(
         n, inputs, cotangent, small, halved(qkv_w), halved(out_w), halved(up_w), halved(down_w)
     )
-    grads, g_qkv, g_out, g_up, g_down, g_small = backward_pass(n, cot, gains, bds, full, tokens, kept)
+    layer_out, grads, g_qkv, g_out, g_up, g_down, g_small = backward_pass(
+        n, cot, gains, bds, full, tokens, kept
+    )
     maps = jnp.concatenate([g_small[16:, :HEAD], g_small[16:, HEAD:]])
     bias = lax.dynamic_slice_in_dim(g_small[:9].reshape(-1), bias_at, bias_w.shape[0])
     gain = lax.dynamic_slice_in_dim(g_small[9:11].reshape(-1), gain_at, gain_w.shape[0])

time: 702 us -> 534 us (0.76)
  Pallas kernels: 671 us -> 500 us
    pallas_call x2, Pallas kernels: 671 us -> 500 us  [call(): pl.pallas_call(kernel, out_shape=outs, in_specs=specs, out_specs=out_spec...]
where the time goes in v3:
time: 534 us; the launch traced here: 524 us
  Pallas kernels  500 us (94%)
  local copies, waits for them, and re-layouts  21 us (4%)
    pallas_call x2, Pallas kernels, call(): pl.pallas_call(kernel, out_shape=outs, in_specs=specs, out_specs=out_spec...  500 us

profile of v3, /device:TPU:13, one launch (start us, length us, event | category | flops | bytes accessed | tf_op | source)
XLA Modules:
  0.0 523.9 jit_solution(14044166170327984280)
XLA Ops:
  0.6 0.0 copy-start
  0.7 1.0 dynamic_update_slice.7
  1.7 0.1 pad.4.clone
  1.7 0.7 reduce
  2.5 0.3 dynamic_update_slice.6
  2.7 0.9 copy.18
  3.7 0.1 copy.19
  3.8 0.7 maximum_maximum_fusion.refs_2_
  4.5 1.6 fusion.3.refs_4_
  6.1 1.7 fusion.2.refs_3_
  7.8 0.0 copy-done
  7.8 0.7 fusion.1.refs_6_
  8.6 1.8 fusion.refs_5_
  10.4 186.7 %shard_map.160 = (bf16[2,4,2,96,2304]{4,3,2,1,0:T(8,128)(2,1)}, bf16[2,4,2,96,768]{4,3,2,1,0:T(8,128)(2,1)}, bf16[2,4,2,96,3072]{4,3,2,1,0:T(8,128)(2,1)}, bf16[...) custom-call(bf16[4,2,128,768]{3,2,1,0:T(8,128)(2,1)} %refs_0_.1, ...), custom_call_target="tpu_custom_call" | custom-call | flops 14495514624 | bytes 75681792 | tf_op jit(solution)/shard_map/pallas_call | solution.py:613
  197.1 313.5 %shard_map.161 = (bf16[1,4,2,128,768]{4,3,2,1,0:T(8,128)(2,1)}, bf16[1,4,2,128,768]{4,3,2,1,0:T(8,128)(2,1)}, f32[96,2304]{1,0:T(8,128)}, f32[96,768]{1,0:T(8,12...) custom-call(bf16[512,768]{1,0:T(8,128)(2,1)} %get-tuple-element.48.r, ...), custom_call_target="tpu_custom_call" | custom-call | flops 28991029248 | bytes 107438080 | tf_op jit(solution)/shard_map/pallas_call | solution.py:613
  510.7 0.7 slice_bitcast_fusion.1
  511.3 0.6 dynamic_slice.23
  512.0 0.7 slice_bitcast_fusion
  512.7 0.1 dynamic_slice.22
  512.8 0.6 broadcast_in_dim.38
  513.4 0.9 fusion.4
  514.3 0.7 copy.20
  515.0 0.0 copy-start.2
  515.0 2.8 copy.29
  517.8 0.0 copy-done.2
  517.8 0.0 copy-start.5
  517.8 1.1 copy.30
  519.0 0.6 copy-done.5
  519.5 0.0 copy-start.6
  519.5 0.0 copy-start.4
  519.6 0.9 copy.31
  520.5 0.2 copy-done.6
  520.7 0.0 copy-start.3
  520.7 0.7 copy.32
  521.4 0.0 copy-done.4
  521.4 0.0 copy-start.1
  521.4 1.0 copy.33
  522.4 0.0 copy-done.3
  522.4 1.0 copy.34
  523.4 0.0 copy-done.1
  (4 shorter events, 0.0 us)
Async XLA Ops:
  0.6 7.2 %copy-start = (f32[1,384,768]{2,1,0:T(8,128)S(1)}, f32[1,384,768]{2,1,0:T(8,128)}, u32[]{:S(2)}) copy-start(f32[1,384,768]{2,1,0:T(8,128)} %param.14) | copy-start | bytes 3538948
  515.0 2.8 copy-start.2
  517.8 1.7 copy-start.5
  519.5 1.1 copy-start.6
  519.5 1.8 copy-start.4
  520.7 1.7 copy-start.3
  521.4 2.0 copy-start.1

commit v4 on v3

--- a/solution.py
+++ b/solution.py
@@ -475,7 +475,7 @@
 bf16 = jnp.bfloat16
 GELU_C = 0.7978845608028654
 GELU_A = 0.044715
-SMALL_ROWS = 208
+SMALL_ROWS = 128
 VEC_ROWS = 72
 GAIN_ROWS = 16
 SHIFT1, QKV_BIAS, OUT_BIAS, SHIFT2, UP_BIAS, DOWN_BIAS = 0, 6, 24, 30, 36, 60
@@ -512,13 +512,22 @@
     bd: Any
     tok_out: Any
     cot_out: Any
+    lay: Any
 
 
 class ForwardScratch(NamedTuple):
+    wq: Any
+    wo: Any
+    wu: Any
+    wd: Any
+    hq: Any
+    ho: Any
+    hu: Any
+    hd: Any
     tok: Any
     sm: Any
     vec: Any
-    mt: Any
+    maps: Any
     st: Any
     stb: Any
     got: Any
@@ -533,6 +542,8 @@
     c_recv: Any
     s_send: Any
     s_recv: Any
+    d_send: Any
+    d_recv: Any
     w_sem: Any
     o_sem: Any
     m_sem: Any
@@ -560,6 +571,10 @@
 
 def tn(a, b):
     return lax.dot_general(a, b, (((0,), (0,)), ((), ())), preferred_element_type=f32)
+
+
+def tt(a, b):
+    return lax.dot_general(a, b, (((0,), (1,)), ((), ())), preferred_element_type=f32)
 
 
 def loop(count, body, events=None):
@@ -662,6 +677,7 @@
         self.d = lax.axis_index("dp")
         self.j = lax.axis_index("seq")
         self.z, self.y = lax.div(self.j, 2), lax.rem(self.j, 2)
+        self.zh, self.zl = lax.div(self.z, 2), lax.rem(self.z, 2)
         self.i = lax.rem(self.z, 2) * 2 + self.y
         self.jj = lax.div(self.z, 2)
         self.r = self.x * self.group + self.jj
@@ -704,127 +720,225 @@
     )
 
 
+def hand_over(p, layer, rows, out, send, recv):
+    closing = []
+    for k in range(4):
+        to = p.jj * 4 + k
+        src = rows.at[pl.ds(k * CH, CH), :]
+        dst = out.at[0, p.i, p.x]
+        slot = p.i * 2 + p.x
+        mine = (to == p.j) & (p.x == layer)
+        copy = remote(src, dst, send.at[k], recv.at[slot], p.at(x=layer, j=to))
+
+        @pl.when(jnp.logical_not(mine))
+        def _():
+            copy.start()
+
+        @pl.when(mine)
+        def _():
+            pltpu.make_async_copy(src, dst, recv.at[slot]).start()
+
+        def close(copy=copy, mine=mine):
+            @pl.when(jnp.logical_not(mine))
+            def _():
+                copy.wait_send()
+
+        closing.append(close)
+    return closing
+
+
+def handed_over(p, layer, out, recv):
+    @pl.when(p.x == layer)
+    def _():
+        for slot in range(8):
+            arrived(out.at[0, slot // 2, slot % 2], recv.at[slot])
+
+
+def signal(sem, to):
+    pl.semaphore_signal(sem, inc=1, device_id=to, device_id_type=MESH)
+
+
 class Gather:
-    def __init__(self, place, src, buf, send, recv, local, y_last, halves=True):
+    def __init__(self, place, src, buf, send, recv, local, y_last, eager=False, by_rows=False):
         self.p, self.src, self.buf = place, src, buf
         self.send, self.recv, self.local = send, recv, local
-        self.y_last, self.halves = y_last, halves
-        self.width = src.shape[1]
-        self.sent = []
-
-    def columns(self):
-        if not self.halves:
-            return slice(None)
-        return pl.ds(pl.multiple_of(self.p.d * self.width, CH), self.width)
+        self.y_last, self.eager, self.by_rows = y_last, eager, by_rows
+        self.rows, self.width = src.shape
+        self.sent = ([], [], [])
+
+    def part(self, d):
+        if self.by_rows:
+            return pl.ds(pl.multiple_of(d * self.rows, 16), self.rows), slice(None)
+        return slice(None), pl.ds(pl.multiple_of(d * self.width, CH), self.width)
 
     def shard(self, x, o, y):
-        return self.buf.at[x, self.p.zpos(-o), y, :, self.columns()]
-
-    def column(self, x, y):
-        return self.buf.at[x, :, y, :, self.columns()]
-
-    def go(self, src, dst, slot, to):
-        remote(src, dst, self.send.at[slot], self.recv.at[slot], to).start()
-        self.sent.append(slot)
+        return self.buf.at[x, self.p.zpos(-o), y, *self.part(self.p.d)]
+
+    def go(self, src, dst, out, slot, to, plane):
+        remote(src, dst, self.send.at[out], self.recv.at[slot], to).start()
+        self.sent[plane].append(out)
 
     def got(self, ref, slot):
         arrived(ref, self.recv.at[slot])
 
-    def start(self):
+    def own(self, o):
+        return self.src if o == 0 else self.shard(self.p.x, o, self.p.y)
+
+    def send_y(self, o, plane):
+        p = self.p
+        self.go(self.own(o), self.shard(p.x, o, p.y), 3 + o, 3 + o, p.at(y=1 - p.y), plane)
+
+    def send_x(self, o, plane):
+        p = self.p
+        self.go(self.own(o), self.shard(p.x, o, p.y), 7 + o, 7 + o, p.at(x=1 - p.x), plane)
+
+    def core(self, q, plane):
+        x, y = self.kind(q)
+        part = self.buf.at[x, :, y, *self.part(self.p.d)]
+        self.go(part, part, 15 + q, 15 + q, self.p.at(d=1 - self.p.d), plane)
+
+    def kind(self, q):
+        p = self.p
+        return (p.x if q < 2 else 1 - p.x), (p.y if q % 2 == 0 else 1 - p.y)
+
+    def wait_all(self, q):
+        x, y = self.kind(q)
+        for o in range(self.p.nz):
+            self.got(self.shard(x, o, y), (0, 3, 7, 11)[q] + o)
+
+    def begin(self):
         p = self.p
         own = self.shard(p.x, 0, p.y)
         pltpu.make_async_copy(self.src, own, self.local).start()
         for o in range(1, p.nz):
-            self.go(self.src, own, o - 1, p.at(z=p.zpos(o)))
-        self.first(0)
-
-    def first(self, o):
+            self.go(self.src, own, o - 1, o - 1, p.at(z=p.zpos(o)), 2)
+        self.send_x(0, 2)
+        if self.eager:
+            self.send_y(0, 2)
+        else:
+
+            @pl.when(p.x == 0)
+            def _():
+                self.send_y(0, 0)
+
+    def early(self):
+        @pl.when(self.p.x == 1)
+        def _():
+            for o in range(1, self.p.nz):
+                self.got(self.shard(self.p.x, o, self.p.y), o - 1)
+                self.send_x(o, 1)
+                if self.eager:
+                    self.send_y(o, 1)
+
+    def spread(self, layer):
+        p, nz = self.p, self.p.nz
+
+        @pl.when(p.x == layer)
+        def _():
+            for o in range(nz):
+                if layer == 0 and o > 0:
+                    self.got(self.shard(p.x, o, p.y), o - 1)
+                    self.send_x(o, layer)
+                if o > 0 if layer == 0 else not self.eager:
+                    self.send_y(o, layer)
+            finish(self.shard(p.x, 0, p.y), self.local)
+            self.core(0, layer)
+
+        @pl.when(p.x != layer)
+        def _():
+            if self.y_last[layer]:
+                for o in range(nz):
+                    here = self.shard(1 - p.x, o, p.y)
+                    self.got(here, 7 + o)
+                    self.go(here, here, 11 + o, 11 + o, p.at(y=1 - p.y), 1 - layer)
+            else:
+                self.wait_all(2)
+            self.core(2, 1 - layer)
+
+    def hop(self, layer):
         p = self.p
-        here = self.shard(p.x, o, p.y)
-        if o > 0:
-            self.got(here, o - 1)
-        src = self.src if o == 0 else here
-        self.go(src, here, 3 + o, p.at(y=1 - p.y))
-        self.go(src, here, 7 + o, p.at(x=1 - p.x))
-
-    def firsts(self):
-        for o in range(1, self.p.nz):
-            self.first(o)
-        finish(self.shard(self.p.x, 0, self.p.y), self.local)
-        self.core(0)
-
-    def seconds(self):
+        if not self.y_last[layer]:
+
+            @pl.when(p.x == layer)
+            def _():
+                for o in range(p.nz):
+                    here = self.shard(p.x, o, 1 - p.y)
+                    self.got(here, 3 + o)
+                    self.go(here, here, 19 + o, 11 + o, p.at(x=1 - p.x), layer)
+                self.core(1, layer)
+
+    def last(self, layer):
         p = self.p
-        for o in range(p.nz):
-            if self.y_last:
-                here = self.shard(1 - p.x, o, p.y)
-                self.got(here, 7 + o)
-                self.go(here, here, 11 + o, p.at(y=1 - p.y))
-            else:
-                here = self.shard(p.x, o, 1 - p.y)
-                self.got(here, 3 + o)
-                self.go(here, here, 11 + o, p.at(x=1 - p.x))
-        self.core(2 if self.y_last else 1)
-
-    def thirds(self):
-        q = 1 if self.y_last else 2
-        self.wait_all(q)
-        self.core(q)
-
-    def last(self):
-        self.wait_all(3)
-        self.core(3)
-
-    def kind(self, q):
+        if self.y_last[layer]:
+
+            @pl.when(p.x == layer)
+            def _():
+                self.wait_all(1)
+                self.core(1, layer)
+
+        @pl.when(p.x != layer)
+        def _():
+            self.wait_all(3)
+            self.core(3, 1 - layer)
+
+    def done(self, layer):
         p = self.p
-        return (p.x if q < 2 else 1 - p.x), (p.y if q % 2 == 0 else 1 - p.y)
-
-    def wait_all(self, q):
-        x, y = self.kind(q)
-        for o in range(self.p.nz):
-            self.got(self.shard(x, o, y), (0, 3, 7, 11)[q] + o)
-
-    def core(self, q):
-        if self.halves:
-            part = self.column(*self.kind(q))
-            self.go(part, part, 15 + q, self.p.at(d=1 - self.p.d))
-
-    def done(self):
-        if self.halves:
-            p = self.p
-            other = pl.ds(pl.multiple_of((1 - p.d) * self.width, CH), self.width)
-            for q in range(4):
-                x, y = self.kind(q)
-                self.got(self.buf.at[x, :, y, :, other], 15 + q)
+        other = self.part(1 - p.d)
+        for plane in range(2):
+
+            @pl.when(p.x == plane)
+            def _():
+                for q in (0, 1) if plane == layer else (2, 3):
+                    x, y = self.kind(q)
+                    self.got(self.buf.at[x, :, y, *other], 15 + q)
 
     def close(self):
         p = self.p
-        for slot in self.sent:
-            ref = self.column(p.x, p.y) if slot >= 15 else self.shard(p.x, 0, p.y)
-            departed(ref, self.send.at[slot])
+
+        def leave(slots):
+            for slot in slots:
+                ref = self.shard(p.x, 0, p.y)
+                if 15 <= slot < 19:
+                    ref = self.buf.at[p.x, :, p.y, *self.part(p.d)]
+                departed(ref, self.send.at[slot])
+
+        leave(self.sent[2])
+        for plane in range(2):
+
+            @pl.when(p.x == plane)
+            def _():
+                leave(self.sent[plane])
 
 
 def forward_kernel(n, *refs):
-    ref = ForwardRefs(*refs[:15])
-    saved = [Kept(*refs[15:27]), Kept(*refs[27:39])]
-    v = Kept(*refs[39:51])
-    own = ForwardScratch(*refs[51:])
+    ref = ForwardRefs(*refs[:16])
+    saved = [Kept(*refs[16:28]), Kept(*refs[28:40])]
+    v = Kept(*refs[40:52])
+    own = ForwardScratch(*refs[52:])
     p = Place(n)
     nz, group = p.nz, p.group
     t = v.a.shape[0]
     nc = t // CH
+    mine = ((ref.wq, own.wq, own.hq), (ref.wo, own.wo, own.ho))
+    mine += ((ref.wu, own.wu, own.hu), (ref.wd, own.wd, own.hd))
+    for k, (src, wide_, _) in enumerate(mine):
+        width = wide_.shape[1]
+        cols = pl.ds(pl.multiple_of(p.d * width, CH), width)
+        pltpu.make_async_copy(src.at[:, cols], wide_, own.w_sem.at[k]).start()
     p.meet()
-
-    def gather(k, src, buf, y_last, halves=True):
-        return Gather(
-            p, src, buf, own.g_send.at[k], own.g_recv.at[k], own.g_local.at[k], y_last, halves
-        )
-
-    gs = gather(0, ref.small, own.sm, False, False)
-    gq = gather(1, ref.wq, ref.gq, True)
-    go = gather(2, ref.wo, ref.go, False)
-    gu = gather(3, ref.wu, ref.gu, False)
-    gd = gather(4, ref.wd, ref.gd, True)
+    for k, (_, wide_, half) in enumerate(mine):
+        finish(wide_, own.w_sem.at[k])
+        half[...] = wide_[...].astype(bf16)
+
+    def gather(k, src, buf, y_last, eager=False, by_rows=False):
+        sems = (own.g_send.at[k], own.g_recv.at[k], own.g_local.at[k])
+        return Gather(p, src, buf, *sems, y_last, eager, by_rows)
+
+    gs = gather(0, ref.small, own.sm, (True, True), True, True)
+    gq = gather(1, own.hq, ref.gq, (True, True), True)
+    go = gather(2, own.ho, ref.go, (True, False))
+    gu = gather(3, own.hu, ref.gu, (True, False))
+    gd = gather(4, own.hd, ref.gd, (False, True))
     gathers = (gs, gq, go, gu, gd)
 
     def collect(which, s):
@@ -851,18 +965,24 @@
 
         return close
 
+    gs.begin()
+    gq.begin()
     closing = [collect(0, s) for s in range(4)]
-    for g in gathers:
-        g.start()
-    gs.firsts()
-    gq.firsts()
-    gs.seconds()
-    go.firsts()
-    gq.seconds()
-    gs.thirds()
-    gs.last()
-
-    vec, gv, bd, sm, mt = own.vec, ref.gv, ref.bd, own.sm, own.mt
+    for g in (go, gu, gd):
+        g.begin()
+    gs.early()
+    gs.spread(0)
+    gq.early()
+    gq.spread(0)
+    gs.spread(1)
+    gs.last(0)
+    go.early()
+    go.spread(0)
+    gs.last(1)
+    gs.done(0)
+    gs.done(1)
+
+    vec, gv, bd, sm, maps = own.vec, ref.gv, ref.bd, own.sm, own.maps
     vec[...] = jnp.zeros(vec.shape, f32)
     gv[...] = jnp.zeros(gv.shape, f32)
     bd[...] = jnp.zeros(bd.shape, bf16)
@@ -872,18 +992,19 @@
             row, grow = (33 * k) // 4, (3 * k) // 2
             vec[layer, row : row + 9, :] += part[0:9]
             gv[layer, grow : grow + 2, :] += part[9:11]
-        for head in range(2 * H):
-            k, at, odd = head // 3, 16 + (head % 3) * HEAD, head % 2
-            both = sm[layer, k // 2, k % 2, at : at + HEAD, :].astype(f32)
-            flip = pltpu.roll(both, HEAD, 1)
-            rows = pl.ds(odd * HEAD, HEAD)
-            signed = jnp.where(lanes(HEAD) < HEAD, both, -flip)
-            bd[layer, head // 2, rows, odd * CH : (odd + 1) * CH] = signed.astype(bf16)
-            if odd:
-                turned = jnp.where(lanes(HEAD) < HEAD, 0.0, both)
-            else:
-                turned = jnp.where(lanes(HEAD) < HEAD, flip, 0.0)
-            mt[layer, head // 2, rows, :] = turned.astype(bf16)
+        first = lanes(HEAD) < HEAD
+        for k in range(n):
+            packed = sm[layer, k // 2, k % 2, 16:112, :].astype(f32)
+            turned = pltpu.roll(packed, HEAD, 1)
+            middle = jnp.concatenate([packed[HEAD:], turned[: HEAD // 2]], 0)
+            for i, left in enumerate((packed[:HEAD], middle, turned[HEAD // 2 :])):
+                right = pltpu.roll(left, HEAD, 1)
+                pair, odd = (3 * k + i) // 2, (3 * k + i) % 2
+                rows = pl.ds(odd * HEAD, HEAD)
+                signed = jnp.where(first, left, -right)
+                bd[layer, pair, rows, odd * CH : (odd + 1) * CH] = signed.astype(bf16)
+                alone = jnp.where(first, 0.0, right) if odd else jnp.where(first, left, 0.0)
+                maps[layer, pair, rows, :] = alone.astype(bf16)
 
     for k in range(4):
         arrived(own.tok.at[pl.ds(k * CH, CH), :], own.c_recv.at[0, k])
@@ -952,7 +1073,7 @@
         save(layer, v.qkv)
 
         def pair(k):
-            logits = nt(mt[layer, k], qkv[:, span(k, CH)]).reshape(2, HEAD, t)
+            logits = tt(maps[layer, k], qkv[:, span(k, CH)]).reshape(2, HEAD, t)
             up = jnp.exp(logits - jnp.max(logits, 1, keepdims=True))
             down = jnp.exp(jnp.min(logits, 1, keepdims=True) - logits)
             up = up * (1.0 / jnp.sum(up, 1, keepdims=True))
@@ -1026,6 +1147,7 @@
         take_states(layer, 1)
         if layer == 1:
             closing.extend([collect(1, s) for s in range(4)])
+            closing.extend(hand_over(p, 0, v.res.at[0], ref.lay, own.d_send, own.d_recv))
         save(layer, v.pre)
         s0 = v.pre
 
@@ -1110,36 +1232,80 @@
         return go_
 
     nothing = run()
-    gu.firsts()
-    go.seconds()
-    gq.thirds()
-    gq.last()
-    gq.done()
+    gu.early()
+    go.spread(1)
+    gu.spread(0)
+    gq.last(0)
+    gu.spread(1)
+    gq.done(0)
     load(gq, own.vq, 0, 0)
     tok_out = pltpu.make_async_copy(own.tok, ref.tok_out, own.m_sem)
     tok_out.start()
-    project(0, own.tok, [{}, {0: gd.firsts, 4: gu.seconds}, {1: go.thirds, 3: gd.seconds}])
+    project(0, own.tok, [{}, {}, {}])
+    gd.early()
+    gd.spread(0)
+    gq.spread(1)
+    gd.spread(1)
+    go.last(0)
+    go.hop(1)
     mix(
         0,
         own.tok,
         [
-            {1: go.last, 2: gu.thirds},
-            run(go.done, functools.partial(load, go, own.vo, 0, 1), gd.thirds),
-            run(gu.last, gu.done, functools.partial(load, gu, own.vu, 0, 2)),
+            {
+                1: run(
+                    functools.partial(go.done, 0),
+                    functools.partial(load, go, own.vo, 0, 1),
+                    functools.partial(gd.hop, 0),
+                ),
+                3: run(
+                    functools.partial(gu.last, 0),
+                    functools.partial(gu.done, 0),
+                    functools.partial(load, gu, own.vu, 0, 2),
+                ),
+            },
+            functools.partial(gu.hop, 1),
+            nothing,
             {},
             run(
+                functools.partial(gq.last, 1),
+                functools.partial(gq.done, 1),
                 functools.partial(load, gq, own.vq, 1, 0),
-                functools.partial(load, go, own.vo, 1, 1),
-                functools.partial(load, gu, own.vu, 1, 2),
-                gd.last,
-                gd.done,
+                functools.partial(gd.last, 0),
+                functools.partial(gd.done, 0),
                 functools.partial(load, gd, own.vd, 0, 3),
             ),
         ],
     )
-    load(gd, own.vd, 1, 3)
     project(1, v.res.at[0], [{}, {}, {}])
-    mix(1, v.res.at[0], [{}, nothing, nothing, {}, nothing])
+    mix(
+        1,
+        v.res.at[0],
+        [
+            {
+                2: run(
+                    functools.partial(go.last, 1),
+                    functools.partial(go.done, 1),
+                    functools.partial(load, go, own.vo, 1, 1),
+                ),
+                4: run(
+                    functools.partial(gu.last, 1),
+                    functools.partial(gu.done, 1),
+                    functools.partial(load, gu, own.vu, 1, 2),
+                ),
+            },
+            nothing,
+            nothing,
+            {
+                1: run(
+                    functools.partial(gd.last, 1),
+                    functools.partial(gd.done, 1),
+                    functools.partial(load, gd, own.vd, 1, 3),
+                )
+            },
+            nothing,
+        ],
+    )
 
     for g in gathers:
         g.close()
@@ -1151,6 +1317,7 @@
         close_states(layer, 1)
 
     tok_out.wait()
+    handed_over(p, 0, ref.lay, own.d_recv)
     saved_all(0, v.res)
     saved_all(1, *v)
 
@@ -1159,7 +1326,7 @@
     t = 4 * CH
     nz = n // 2
     full = [
-        shape((2, nz, 2, w.shape[0], 2 * w.shape[1]), bf16) for w in (wq, wo, wu, wd)
+        shape((2, nz, 2) + w.shape, bf16) for w in (wq, wo, wu, wd)
     ]
     kept = [
         shape((t, D), bf16),
@@ -1176,10 +1343,13 @@
         shape((STATE_ROWS, CH), f32),
     ]
     outs = full + [shape((2, GAIN_ROWS, CH), f32), shape((2, 2 * PAIRS, CH, 2 * CH), bf16)]
-    outs += [shape((t, D), bf16)] * 2 + kept * 2
+    outs += [shape((t, D), bf16)] * 2 + [shape((1, 4, 2, CH, D), bf16)] + kept * 2
     specs = [ANY] * 4 + [VMEM] * 2 + [ANY] * (len(outs) - 6)
     scratch = [pltpu.VMEM(k.shape, k.dtype) for k in kept]
     scratch[10] = pltpu.VMEM((2, t, D), bf16)
+    halves = [(w.shape[0], w.shape[1] // 2) for w in (wq, wo, wu, wd)]
+    scratch += [pltpu.VMEM(half, f32) for half in halves]
+    scratch += [pltpu.VMEM(half, bf16) for half in halves]
     scratch += [
         pltpu.VMEM((t, D), bf16),
         pltpu.VMEM((2, nz, 2, SMALL_ROWS, CH), bf16),
@@ -1191,8 +1361,8 @@
     ]
     scratch += [pltpu.VMEM(w.shape[1:], bf16) for w in full]
     dma = pltpu.SemaphoreType.DMA
-    scratch += [dma((5, 19)), dma((5, 19)), dma((5,)), dma((2, 4)), dma((2, 4))]
-    scratch += [dma((2, n // 2 - 1)), dma((2, n // 2 - 1)), dma((4,))]
+    scratch += [dma((5, 23)), dma((5, 19)), dma((5,)), dma((2, 4)), dma((2, 4))]
+    scratch += [dma((2, n // 2 - 1)), dma((2, n // 2 - 1)), dma((4,)), dma((8,)), dma((4,))]
     scratch += [dma((2, 12)), dma]
     got = call(
         functools.partial(forward_kernel, n),
@@ -1204,8 +1374,8 @@
         specs,
         cid=0,
     )
-    layers = [Kept(*got[8:20]), Kept(*got[20:32])]
-    return got[:4], got[4], got[5], got[6], got[7], layers
+    layers = [Kept(*got[9:21]), Kept(*got[21:33])]
+    return got[:4], got[4], got[5], got[6], got[7], got[8], layers
 
 
 def with_error(gv, swapped, lane, hh):
@@ -1248,52 +1418,63 @@
 
 
 class Reduce:
-    def __init__(self, place, layer, buf, temp, land, out, fin, send, recv, local, last):
-        self.p, self.layer, self.buf, self.temp = place, layer, buf, temp
-        self.land_d, self.land_y, self.land_z, self.land_x = land
-        self.out, self.fin, self.local, self.last = out, fin, local, last
-        self.send, self.recv = send, recv
-        self.r, self.c = buf.shape[2], buf.shape[3]
+    def __init__(self, place, layer, buf, land, out, fin, sems, credit):
+        self.p, self.layer, self.buf, self.fin = place, layer, buf, fin
+        self.land_y, self.land_z, self.land_x, self.stage = land
+        self.own, self.other = out
+        self.send, self.recv, self.last = sems
+        self.credit_y, self.credit_a, self.credit_b = credit
 
     def go(self, src, dst, slot, to):
         remote(src, dst, self.send.at[slot], self.recv.at[slot], to).start()
 
-    def fetch(self, src, dst):
-        copy = pltpu.make_async_copy(src, dst, self.local)
-        copy.start()
-        copy.wait()
-
-    def send_core(self):
-        self.go(self.buf, self.land_d, 0, self.p.at(d=1 - self.p.d))
-
-    def got_core(self):
-        departed(self.buf, self.send.at[0])
-        arrived(self.land_d, self.recv.at[0])
-
     def send_y(self):
         p = self.p
-        self.go(self.buf.at[:, 1 - p.y], self.land_y, 1, p.at(y=1 - p.y))
+        if self.layer == 0:
+            pl.semaphore_wait(self.credit_y, 1)
+        self.go(self.buf.at[:, 1 - p.y], self.land_y, 0, p.at(y=1 - p.y))
+
+    def add(self, zi, more):
+        kept = self.buf.at[zi, self.p.y]
+        kept[...] = (kept[...].astype(f32) + more.astype(f32)).astype(bf16)
 
     def step_y(self):
         p = self.p
-        arrived(self.land_y, self.recv.at[1])
-        self.fetch(self.land_y, self.temp)
-        for i in range(1, p.nz + 1):
-            zi = p.zpos(i)
-            self.buf[zi, p.y] = (
-                self.buf[zi, p.y].astype(f32) + self.temp[zi].astype(f32)
-            ).astype(bf16)
-            if i < p.nz:
-                self.go(self.buf.at[zi, p.y], self.land_z.at[i - 1], 1 + i, p.at(z=zi))
+        near = p.z + 1 - 2 * p.zl
+        arrived(self.land_y, self.recv.at[0])
+        if self.layer == 0:
+            pl.semaphore_wait(self.credit_a, 1)
+        for h in range(2):
+            zi = 2 * h + 1 - p.zl
+            self.add(zi, self.land_y[zi])
+            self.go(self.buf.at[zi, p.y], self.land_z.at[h], 1 + h, p.at(z=near))
+        for h in range(2):
+            zi = 2 * h + p.zl
+            self.add(zi, self.land_y[zi])
+        if self.layer == 1:
+            signal(self.credit_y, p.at(y=1 - p.y))
+
+    def step_a(self):
+        p = self.p
+        near = p.z + 1 - 2 * p.zl
+        far = p.z + 2 - 4 * p.zh
+        if self.layer == 0:
+            pl.semaphore_wait(self.credit_b, 1)
+        for h in range(2):
+            arrived(self.land_z.at[h], self.recv.at[1 + h])
+        away = 2 * (1 - p.zh) + p.zl
+        self.add(away, self.land_z[1 - p.zh])
+        self.go(self.buf.at[away, p.y], self.land_z.at[2], 3, p.at(z=far))
+        self.add(p.z, self.land_z[p.zh])
+        if self.layer == 1:
+            signal(self.credit_a, p.at(z=near))
 
     def step_z(self):
         p = self.p
-        for i in range(1, p.nz):
-            arrived(self.land_z.at[i - 1], self.recv.at[1 + i])
-        self.fetch(self.land_z, self.temp.at[pl.ds(0, p.nz - 1)])
-        total = self.buf[p.z, p.y].astype(f32)
-        for i in range(p.nz - 1):
-            total = total + self.temp[i].astype(f32)
+        arrived(self.land_z.at[2], self.recv.at[3])
+        total = self.buf[p.z, p.y].astype(f32) + self.land_z[2].astype(f32)
+        if self.layer == 1:
+            signal(self.credit_b, p.at(z=p.z + 2 - 4 * p.zh))
 
         @pl.when(p.x == self.layer)
         def _():
@@ -1301,106 +1482,50 @@
 
         @pl.when(p.x != self.layer)
         def _():
-            self.buf[p.z, p.y] = total.astype(bf16)
-            self.go(self.buf.at[p.z, p.y], self.land_x, 5, p.at(x=1 - p.x))
-
-    def half(self):
-        return pl.ds(pl.multiple_of(self.p.d * self.c, CH), self.c)
-
-    def other(self):
-        return pl.ds(pl.multiple_of((1 - self.p.d) * self.c, CH), self.c)
+            self.stage[...] = total.astype(bf16)
+            self.go(self.stage, self.land_x, 4, p.at(x=1 - p.x))
 
     def step_x(self):
         p = self.p
 
         @pl.when(p.x == self.layer)
         def _():
-            arrived(self.land_x, self.recv.at[5])
-            self.fetch(self.land_x, self.temp.at[0])
-            self.fin[...] += self.temp[0].astype(f32)
-            own = self.out.at[:, self.half()]
-            self.go(self.fin, own, 6, p.at(d=1 - p.d))
-            pltpu.make_async_copy(self.fin, own, self.last).start()
+            arrived(self.land_x, self.recv.at[4])
+            self.fin[...] += self.land_x[...].astype(f32)
+            self.go(self.fin, self.own, 5, p.at(d=1 - p.d))
+            pltpu.make_async_copy(self.fin, self.own, self.last).start()
 
     def close(self):
         p = self.p
-        departed(self.buf.at[:, 0], self.send.at[1])
+        departed(self.buf.at[:, 0], self.send.at[0])
         for i in range(1, p.nz):
-            departed(self.buf.at[0, 0], self.send.at[1 + i])
-
-        @pl.when(p.x != self.layer)
-        def _():
-            departed(self.buf.at[0, 0], self.send.at[5])
+            departed(self.buf.at[0, 0], self.send.at[i])
 
     def end(self):
         @pl.when(self.p.x == self.layer)
         def _():
-            departed(self.fin, self.send.at[6])
-            arrived(self.out.at[:, self.other()], self.recv.at[6])
+            departed(self.fin, self.send.at[5])
+            arrived(self.other, self.recv.at[5])
             finish(self.fin, self.last)
 
-
-class SmallReduce:
-    def __init__(self, place, layer, buf, land, out, send, recv):
-        self.p, self.layer, self.buf, self.out = place, layer, buf, out
-        self.land_d, self.land_y, self.land_z, self.land_x = land
-        self.send, self.recv = send, recv
-
-    def go(self, src, dst, slot, to):
-        remote(src, dst, self.send.at[slot], self.recv.at[slot], to).start()
-
-    def send_core(self):
-        self.go(self.buf, self.land_d, 0, self.p.at(d=1 - self.p.d))
-
-    def step_d(self):
-        p = self.p
-        departed(self.buf, self.send.at[0])
-        arrived(self.land_d, self.recv.at[0])
-        self.buf[...] += self.land_d[...]
-        self.go(self.buf.at[:, 1 - p.y], self.land_y, 1, p.at(y=1 - p.y))
-
-    def step_y(self):
-        p = self.p
-        arrived(self.land_y, self.recv.at[1])
-        for i in range(1, p.nz + 1):
-            zi = p.zpos(i)
-            self.buf[zi, p.y] += self.land_y[zi]
-            if i < p.nz:
-                self.go(self.buf.at[zi, p.y], self.land_z.at[i - 1], 1 + i, p.at(z=zi))
-
-    def step_z(self):
-        p = self.p
-        for i in range(1, p.nz):
-            arrived(self.land_z.at[i - 1], self.recv.at[1 + i])
-        total = self.buf[p.z, p.y]
-        for i in range(p.nz - 1):
-            total = total + self.land_z[i]
-        self.buf[p.z, p.y] = total
-
-        @pl.when(p.x != self.layer)
+        @pl.when(self.p.x != self.layer)
         def _():
-            self.go(self.buf.at[p.z, p.y], self.land_x, 5, p.at(x=1 - p.x))
-
-    def step_x(self):
-        p = self.p
-
-        @pl.when(p.x == self.layer)
-        def _():
-            arrived(self.land_x, self.recv.at[5])
-            self.out[...] = self.buf[p.z, p.y] + self.land_x[...]
-
-    def close(self):
-        p = self.p
-        departed(self.buf.at[:, 0], self.send.at[1])
-        for i in range(1, p.nz):
-            departed(self.buf.at[0, 0], self.send.at[1 + i])
-
-        @pl.when(p.x != self.layer)
-        def _():
-            departed(self.buf.at[0, 0], self.send.at[5])
-
-
-SMALL_OUT = 112
+            departed(self.stage, self.send.at[4])
+
+
+SMALL_OUT = 128
+Q, O, U, DN, SM = range(5)
+PARTS = (
+    (Q, 0, 96, 0, 384),
+    (Q, 0, 96, 384, 384),
+    (Q, 0, 96, 768, 384),
+    (O, 0, 96, 0, 384),
+    (U, 0, 96, 0, 768),
+    (U, 0, 96, 768, 768),
+    (DN, 0, 192, 0, 384),
+    (DN, 192, 192, 0, 384),
+    (SM, 0, 64, 0, CH),
+)
 
 
 class Loaded(NamedTuple):
@@ -1419,7 +1544,6 @@
 
 class BackwardRefs(NamedTuple):
     cot: Any
-    res0: Any
     res1: Any
     gv: Any
     bd: Any
@@ -1451,24 +1575,44 @@
     bo: Any
     bu: Any
     bd_: Any
-    tmp96: Any
-    tmpd: Any
+    bs: Any
+    yq: Any
+    yo: Any
+    yu: Any
+    yd: Any
+    ys: Any
+    zq: Any
+    zo: Any
+    zu: Any
+    zd: Any
+    zs: Any
+    xq: Any
+    xo: Any
+    xu: Any
+    xd: Any
+    xs: Any
+    wq: Any
+    wo: Any
+    wu: Any
+    wd: Any
+    ws: Any
     fq: Any
     fo: Any
     fu: Any
     fd: Any
-    ty96: Any
-    tyd: Any
+    fs: Any
+    tmp96: Any
+    tmpd: Any
     sb: Any
     sd: Any
-    sy: Any
-    sz: Any
-    sx: Any
     r_send: Any
     r_recv: Any
-    r_local: Any
-    q_send: Any
-    q_recv: Any
+    r_last: Any
+    credit_y: Any
+    credit_a: Any
+    credit_b: Any
+    m_send: Any
+    m_recv: Any
     s_send: Any
     s_recv: Any
     d_send: Any
@@ -1480,18 +1624,15 @@
     k_sem: Any
 
 
-Q, O, U, DN = range(4)
-
-
 def backward_kernel(n, *refs):
-    ref = BackwardRefs(*refs[:9])
-    source = [Loaded(*refs[9:20]), Loaded(*refs[20:31])]
-    hidden = refs[31:33]
-    lay, gin, small_out = refs[33], refs[34], refs[39]
-    wgrads = refs[35:39]
-    lands = refs[40:72]
-    v = Loaded(*refs[72:83])
-    own = BackwardScratch(*refs[83:])
+    ref = BackwardRefs(*refs[:8])
+    source = [Loaded(*refs[8:19]), Loaded(*refs[19:30])]
+    hidden = refs[30:32]
+    lay, gin, small_out = refs[32], refs[33], refs[38]
+    wgrads = refs[34:38]
+    lands = refs[39:47]
+    v = Loaded(*refs[47:58])
+    own = BackwardScratch(*refs[58:])
     p = Place(n)
     nz, group = p.nz, p.group
     t = own.drb.shape[0]
@@ -1542,41 +1683,57 @@
     finish(gbuf.at[0], own.t_sem.at[4])
 
     width = (3 * D // 2, D // 2, FF // 2, D // 2)
-    bufs = (own.bq, own.bo, own.bu, own.bd_)
-    fins = (own.fq, own.fo, own.fu, own.fd)
+    bufs = (own.bq, own.bo, own.bu, own.bd_, own.bs)
+    spots = (
+        (own.yq, own.yo, own.yu, own.yd, own.ys),
+        (own.zq, own.zo, own.zu, own.zd, own.zs),
+        (own.xq, own.xo, own.xu, own.xd, own.xs),
+        (own.wq, own.wo, own.wu, own.wd, own.ws),
+    )
+    fins = (own.fq, own.fo, own.fu, own.fd, own.fs)
     reduces = []
     for layer in range(2):
-        line = []
-        for m in (Q, O, U, DN):
-            at = (layer * 4 + m) * 4
-            line.append(
+        line = [[] for _ in range(5)]
+        for k, (m, r0_, r_, c0_, c_) in enumerate(PARTS):
+            rows, cols = pl.ds(r0_, r_), pl.ds(c0_, c_)
+            out = []
+            for side in (p.d, 1 - p.d):
+                if m == SM:
+                    out.append(small_out.at[pl.ds(pl.multiple_of(side * r_, r_), r_), :])
+                else:
+                    at = pl.ds(pl.multiple_of(side * width[m] + c0_, CH), c_)
+                    out.append(wgrads[m].at[rows, at])
+            line[m].append(
                 Reduce(
                     p,
                     layer,
-                    bufs[m],
-                    own.tyd if m == DN else own.ty96.at[:, :, pl.ds(0, width[m])],
-                    lands[at : at + 4],
-                    wgrads[m],
-                    fins[m],
-                    own.r_send.at[layer, m],
-                    own.r_recv.at[layer, m],
-                    own.r_local.at[m],
-                    own.r_local.at[4 + m],
+                    bufs[m].at[:, :, rows, cols],
+                    (
+                        spots[0][m].at[:, rows, cols],
+                        spots[1][m].at[:, rows, cols],
+                        spots[2][m].at[rows, cols],
+                        spots[3][m].at[rows, cols],
+                    ),
+                    out,
+                    fins[m].at[rows, cols],
+                    (own.r_send.at[layer, k], own.r_recv.at[layer, k], own.r_last.at[layer, k]),
+                    (own.credit_y.at[k], own.credit_a.at[k], own.credit_b.at[k]),
                 )
             )
         reduces.append(line)
-    smalls = [
-        SmallReduce(
-            p,
-            layer,
-            own.sb.at[layer],
-            [land.at[layer] for land in (own.sd, own.sy, own.sz, own.sx)],
-            small_out,
-            own.q_send.at[layer],
-            own.q_recv.at[layer],
-        )
-        for layer in range(2)
-    ]
+
+    def step(name, layer, *which):
+        def all_():
+            for m in which:
+                for part in reduces[layer][m]:
+                    name(part)
+
+        return all_
+
+    step_y = functools.partial(step, Reduce.step_y)
+    step_a = functools.partial(step, Reduce.step_a)
+    step_z = functools.partial(step, Reduce.step_z)
+    step_x = functools.partial(step, Reduce.step_x)
 
     def states_ok(o, taking):
         return (p.r + o < members) if taking else (p.r - o >= 0)
@@ -1700,13 +1857,18 @@
         send_states(layer)
 
     def weight_grad(layer, m, keep):
-        red = reduces[layer][m]
-        buf, c = red.buf, red.c
+        parts = reduces[layer][m]
+        buf, c = bufs[m], width[m]
+        r = buf.shape[2]
+        land_d = lands[layer * 4 + m]
+        send, recv = own.m_send.at[layer, m], own.m_recv.at[layer, m]
         base = (p.d if keep else 1 - p.d) * c
         if keep:
-            red.got_core()
+            departed(buf, send)
+            arrived(land_d, recv)
         elif layer == 0:
-            reduces[1][m].close()
+            for part in reduces[1][m]:
+                part.close()
         if m == DN:
             rhs = gbuf[1 - layer, :, pl.ds(pl.multiple_of(base, CH), c)]
 
@@ -1718,7 +1880,7 @@
                 ).start()
                 if keep:
                     pltpu.make_async_copy(
-                        red.land_d.at[k // 2, k % 2], own.tmpd.at[k % 3], own.t_sem.at[k % 3]
+                        land_d.at[k // 2, k % 2], own.tmpd.at[k % 3], own.t_sem.at[k % 3]
                     ).start()
 
             for k in range(3):
@@ -1735,12 +1897,12 @@
         else:
             lhs = (v.a, v.ob, v.n2)[m]
             rhs = (v.qkv, own.drb, v.gp)[m]
-            step = 384
-            count = c // step
+            wide_ = 384
+            count = c // wide_
 
             def fetch(k):
                 pltpu.make_async_copy(
-                    red.land_d.at[:, :, :, pl.ds(k * step, step)],
+                    land_d.at[:, :, :, pl.ds(k * wide_, wide_)],
                     own.tmp96.at[k % 2],
                     own.t_sem.at[k % 2],
                 ).start()
@@ -1749,22 +1911,26 @@
                 for k in range(min(2, count)):
                     fetch(k)
             for k in range(count):
-                val = tn(lhs[...], rhs[:, pl.ds(pl.multiple_of(base + k * step, CH), step)])
+                val = tn(lhs[...], rhs[:, pl.ds(pl.multiple_of(base + k * wide_, CH), wide_)])
                 if keep:
                     finish(own.tmp96.at[k % 2], own.t_sem.at[k % 2])
                 for zi in range(nz):
                     for yi in range(2):
-                        at = (zi * 2 + yi) * red.r
-                        part = val[at : at + red.r]
+                        at = (zi * 2 + yi) * r
+                        part = val[at : at + r]
                         if keep:
                             part = part + own.tmp96[k % 2, zi, yi].astype(f32)
-                        buf[zi, yi, :, pl.ds(k * step, step)] = part.astype(bf16)
+                        buf[zi, yi, :, pl.ds(k * wide_, wide_)] = part.astype(bf16)
                 if keep and k + 2 < count:
                     fetch(k + 2)
-        if keep:
-            red.send_y()
-        else:
-            red.send_core()
+                each = count // len(parts)
+                if keep and (k + 1) % each == 0:
+                    parts[k // each].send_y()
+        if keep and m == DN:
+            for part in parts:
+                part.send_y()
+        if not keep:
+            remote(buf, land_d, send, recv, p.at(d=1 - p.d)).start()
 
     def mix_back(layer, events):
         qkv, ph, gs, es = v.qkv, v.ph, own.gs, v.inv
@@ -1869,50 +2035,44 @@
     closing = []
 
     def deliver(which, layer, rows):
-        out = gin if which else lay
-        send, recv = own.d_send.at[which, layer], own.d_recv.at[which]
-        for k in range(4):
-            to = p.jj * 4 + k
-            src = rows.at[pl.ds(k * CH, CH), :]
-            dst = out.at[0, p.i, p.x]
-            slot = p.i * 2 + p.x
-            mine = (to == p.j) & (p.x == layer)
-            copy = remote(src, dst, send.at[k], recv.at[slot], p.at(x=layer, j=to))
-
-            @pl.when(jnp.logical_not(mine))
-            def _():
-                copy.start()
-
-            @pl.when(mine)
-            def _():
-                pltpu.make_async_copy(src, dst, recv.at[slot]).start()
-
-            def close(copy=copy, mine=mine):
-                @pl.when(jnp.logical_not(mine))
-                def _():
-                    copy.wait_send()
-
-            closing.append(close)
+        sems = own.d_send.at[which, layer], own.d_recv.at[which]
+        closing.extend(hand_over(p, layer, rows, gin if which else lay, *sems))
+
+    def small_rows(side):
+        return pl.ds(pl.multiple_of(side * 64, 64), 64)
 
     def pack_small(layer):
         sb = own.sb
         for k in range(n):
             at, gat = (33 * k) // 4, (3 * k) // 2
             zi, yi = k // 2, k % 2
-            sb[layer, zi, yi, 0:9] = vr[layer, at : at + 9, :]
-            sb[layer, zi, yi, 9:11] = gr[layer, gat : gat + 2, :]
-            sb[layer, zi, yi, 11:16] = jnp.zeros((5, CH), f32)
+            sb[zi, yi, 0:9] = vr[layer, at : at + 9, :]
+            sb[zi, yi, 9:11] = gr[layer, gat : gat + 2, :]
+            sb[zi, yi, 11:16] = jnp.zeros((5, CH), f32)
             h0, h1, h2 = (mg[3 * k + i] for i in range(3))
             left = jnp.concatenate([h0, h1[: HEAD // 2]], 0)
             right = jnp.concatenate([h1[HEAD // 2 :], h2], 0)
-            sb[layer, zi, yi, 16:SMALL_OUT] = jnp.where(lanes(96) < HEAD, left, -right)
-        smalls[layer].send_core()
+            sb[zi, yi, 16:112] = jnp.where(lanes(96) < HEAD, left, -right)
+            sb[zi, yi, 112:] = jnp.zeros((16, CH), f32)
+        remote(
+            sb.at[:, :, small_rows(1 - p.d), :],
+            own.sd.at[layer],
+            own.m_send.at[layer, SM],
+            own.m_recv.at[layer, SM],
+            p.at(d=1 - p.d),
+        ).start()
+
+    def small_core(layer):
+        part = reduces[layer][SM][0]
+        departed(own.sd.at[layer], own.m_send.at[layer, SM])
+        arrived(own.sd.at[layer], own.m_recv.at[layer, SM])
+        if layer == 0:
+            reduces[1][SM][0].close()
+        part.buf[...] = (own.sb[:, :, small_rows(p.d), :] + own.sd[layer]).astype(bf16)
+        part.send_y()
 
     vr[...] = jnp.zeros(vr.shape, f32)
     gr[...] = jnp.zeros(gr.shape, f32)
-    r1, r0 = reduces[1], reduces[0]
-    s1, s0 = smalls[1], smalls[0]
-
     def run(*steps):
         def all_():
             for step in steps:
@@ -1920,90 +2080,104 @@
 
         return all_
 
-    deliver(0, 0, ref.res0)
     deliver(0, 1, ref.res1)
-    mlp_back(1, gbuf.at[0], {})
+    weight_grad(1, DN, False)
+    mlp_back(1, gbuf.at[0], {4: functools.partial(weight_grad, 1, DN, True)})
     load(0, v.o)
     load_w(0, U)
     load_w(0, O)
     for k in range(3):
         load_wd(0, k)
     loaded(v.n2, v.ob, v.a)
-    for m in (DN, U, O):
-        weight_grad(1, m, False)
-    for m in (DN, U, O):
-        weight_grad(1, m, True)
+    weight_grad(1, U, False)
+    weight_grad(1, O, False)
+    weight_grad(1, U, True)
+    weight_grad(1, O, True)
     load(0, v.gp, v.n2, v.ob)
-    mix_back(1, {4: r1[DN].step_y})
+    mix_back(1, {1: step_y(1, DN), 5: step_a(1, DN)})
     load_w(0, Q)
     load(0, v.r, v.inv, v.ph, v.u, v.pre)
-    deliver(1, 1, gbuf.at[1])
     pack_small(1)
+    step_y(1, U)()
     weight_grad(1, Q, False)
-    r1[U].step_y()
     weight_grad(1, Q, True)
-    s1.step_d()
-    load(0, v.qkv)
-    load(0, v.a)
-
+    small_core(1)
+    load(0, v.qkv, v.a)
+
+    step_z(1, DN)()
+    weight_grad(0, DN, False)
+    step_y(1, O)()
     mlp_back(
         0,
         gbuf.at[1],
-        {2: r1[DN].step_z, 4: r1[O].step_y, 6: s1.step_y, 7: run(r1[DN].step_x)},
+        {4: functools.partial(weight_grad, 0, DN, True), 6: step_a(1, U), 7: step_x(1, DN)},
     )
     loaded(v.n2, v.ob, v.a)
-    weight_grad(0, DN, False)
-    r1[U].step_z()
+    step_a(1, O)()
+    step_z(1, U)()
     weight_grad(0, U, False)
-    r1[O].step_z()
+    step_y(1, Q, SM)()
+    weight_grad(0, U, True)
+    step_z(1, O)()
     weight_grad(0, O, False)
-    r1[Q].step_y()
-    s1.step_z()
-    weight_grad(0, DN, True)
-    weight_grad(0, U, True)
     weight_grad(0, O, True)
+    step_x(1, U)()
     mix_back(
         0,
         {
-            0: run(r1[U].step_x, r1[O].step_x, s1.step_x),
-            2: r1[Q].step_z,
-            3: run(r1[Q].step_x, r0[DN].step_y),
+            0: step_x(1, O),
+            1: step_a(1, Q, SM),
+            3: step_y(0, DN),
+            4: step_z(1, Q, SM),
         },
     )
-    deliver(1, 0, gbuf.at[0])
     pack_small(0)
     weight_grad(0, Q, False)
-    r0[U].step_y()
+    step_a(0, DN)()
+    step_x(1, Q, SM)()
     weight_grad(0, Q, True)
-    s0.step_d()
-    r0[DN].step_z()
-    r0[O].step_y()
-    s0.step_y()
-    r0[DN].step_x()
-    r0[U].step_z()
-    r0[Q].step_y()
-    r0[O].step_z()
-    s0.step_z()
-    r0[U].step_x()
-    r0[O].step_x()
-    s0.step_x()
-    r0[Q].step_z()
-    r0[Q].step_x()
-
-    for m in (Q, O, U, DN):
-        r0[m].close()
-        r1[m].end()
-        r0[m].end()
-    s1.close()
-    s0.close()
+    small_core(0)
+    step_y(0, U)()
+    step_y(0, O)()
+    step_z(0, DN)()
+    deliver(1, 1, gbuf.at[1])
+    deliver(1, 0, gbuf.at[0])
+    first, second, third = reduces[0][Q]
+    step_x(0, DN)()
+    first.step_y()
+    step_a(0, U)()
+    step_a(0, O)()
+    second.step_y()
+    first.step_a()
+    step_z(0, U)()
+    step_z(0, O)()
+    third.step_y()
+    second.step_a()
+    step_x(0, U)()
+    step_x(0, O)()
+    step_y(0, SM)()
+    first.step_z()
+    third.step_a()
+    step_a(0, SM)()
+    second.step_z()
+    first.step_x()
+    third.step_z()
+    step_z(0, SM)()
+    second.step_x()
+    third.step_x()
+    step_x(0, SM)()
+
+    for m in range(5):
+        for part in reduces[0][m]:
+            part.close()
+        for layer in range(2):
+            for part in reduces[layer][m]:
+                part.end()
     for layer in range(2):
         close_states(layer)
 
-        @pl.when(p.x == layer)
-        def _():
-            for which, out in enumerate((lay, gin)):
-                for slot in range(8):
-                    arrived(out.at[0, slot // 2, slot % 2], own.d_recv.at[which, slot])
+        handed_over(p, layer, gin, own.d_recv.at[1])
+    handed_over(p, 1, lay, own.d_recv.at[0])
 
     for close in closing:
         close()
@@ -2012,7 +2186,7 @@
 def backward_pass(n, cot, gains, bds, full, tokens, kept):
     t = cot.shape[0]
     nz = n // 2
-    args = [cot, kept[0].res, kept[1].res, gains, bds] + list(full)
+    args = [cot, kept[1].res, gains, bds] + list(full)
     for u, k in zip((tokens, kept[0].res), kept):
         read = Loaded(k.gp, k.r, k.o, k.inv, k.ph, k.qkv, k.n2, k.ob, k.a, u, k.pre)
         args += list(read)
@@ -2022,16 +2196,9 @@
     outs = [shape((1, 4, 2, CH, D), bf16)] * 2
     outs += [shape((r, 2 * c), f32) for r, c in zip(rows, widths)]
     outs += [shape((SMALL_OUT, CH), f32)]
-    for _ in range(2):
-        for r, c in zip(rows, widths):
-            outs += [
-                shape((nz, 2, r, c), bf16),
-                shape((nz, r, c), bf16),
-                shape((nz - 1, r, c), bf16),
-                shape((r, c), bf16),
-            ]
-    specs = [ANY] * 6 + [VMEM] + [ANY] * (len(outs) - 7)
-    ins = [ANY] * 3 + [VMEM] * 2 + [ANY] * (len(args) - 5)
+    outs += [shape((nz, 2, r, c), bf16) for r, c in zip(rows, widths)] * 2
+    specs = [ANY] * len(outs)
+    ins = [ANY] * 2 + [VMEM] * 2 + [ANY] * (len(args) - 4)
     scratch = [pltpu.VMEM(a.shape, a.dtype) for a in read]
 
     def vmem(*dims, kind=f32):
@@ -2053,21 +2220,21 @@
     vmem(3, FF // n, D, kind=bf16)
     for w in full[:3]:
         vmem(*w.shape[1:], kind=bf16)
-    for r, c in zip(rows, widths):
-        vmem(nz, 2, r, c, kind=bf16)
+    sizes = list(zip(rows, widths)) + [(64, CH)]
+    for lead in ((nz, 2), (nz,), (nz - 1,), (), ()):
+        for size in sizes:
+            vmem(*lead, *size, kind=bf16)
+    for size in sizes:
+        vmem(*size)
     vmem(2, nz, 2, D // n, 384, kind=bf16)
     vmem(3, FF // n, D // 2, kind=bf16)
-    for r, c in zip(rows, widths):
-        vmem(r, c)
-    vmem(nz, D // n, FF // 2, kind=bf16)
-    vmem(nz, FF // n, D // 2, kind=bf16)
-    vmem(2, nz, 2, SMALL_OUT, CH)
-    vmem(2, nz, 2, SMALL_OUT, CH)
-    vmem(2, nz, SMALL_OUT, CH)
-    vmem(2, nz - 1, SMALL_OUT, CH)
-    vmem(2, SMALL_OUT, CH)
+    vmem(nz, 2, SMALL_OUT, CH)
+    vmem(2, nz, 2, 64, CH)
     dma = pltpu.SemaphoreType.DMA
-    scratch += [dma((2, 4, 7)), dma((2, 4, 7)), dma((8,)), dma((2, 7)), dma((2, 7))]
+    regular = pltpu.SemaphoreType.REGULAR
+    count = len(PARTS)
+    scratch += [dma((2, count, 6)), dma((2, count, 6)), dma((2, count))]
+    scratch += [regular((count,))] * 3 + [dma((2, 5)), dma((2, 5))]
     scratch += [dma((2, n // 2 - 1)), dma((2, n // 2 - 1)), dma((2, 2, 4)), dma((2, 8)), dma((4,))]
     scratch += [dma((len(read),)), dma((3,)), dma((5,)), dma((3,))]
     got = call(
@@ -2079,8 +2246,46 @@
         8 * t * D * (4 * D + 2 * FF),
         specs,
         cid=1,
+        vmem=63,
     )
     return got[:7]
+
+
+def settle_kernel(lay0, lay1, *refs):
+    rest, small, outs, held, sems = refs[:5], refs[5], refs[6:13], refs[13:19], refs[19]
+    x = lax.axis_index("section")
+    for plane, src in enumerate((lay0, lay1)):
+
+        @pl.when(x == plane)
+        def _():
+            pltpu.make_async_copy(src, held[0], sems.at[0]).start()
+
+    for i, src in enumerate(rest):
+        pltpu.make_async_copy(src, held[1 + i], sems.at[1 + i]).start()
+    both = small[16:112, :]
+    outs[6][0:96, :] = both[:, :HEAD]
+    outs[6][96:, :] = pltpu.roll(both, HEAD, 1)[:, :HEAD]
+    copies = []
+    for i, buf in enumerate(held):
+        finish(buf, sems.at[i])
+        copies.append(pltpu.make_async_copy(buf, outs[i], sems.at[6 + i]))
+        copies[-1].start()
+    for copy in copies:
+        copy.wait()
+
+
+def settle(lay0, lay1, rest, small):
+    arrays = [lay0, lay1, *rest, small]
+    outs = [shape(a.shape, a.dtype) for a in (lay0, *rest)]
+    return call(
+        settle_kernel,
+        outs + [shape((192, HEAD), f32)],
+        [pltpu.VMEM(o.shape, o.dtype) for o in outs] + [pltpu.SemaphoreType.DMA((12,))],
+        [ANY] * 7 + [VMEM],
+        arrays,
+        1,
+        [ANY] * 6 + [VMEM],
+    )
 
 
 def shards(inputs, cotangent, *weights):
@@ -2088,31 +2293,26 @@
     d, j = lax.axis_index("dp"), lax.axis_index("seq")
     qkv_w, out_w, up_w, down_w, map_w, bias_w, gain_w = (w[0] for w in weights)
 
-    def halved(w):
-        width = w.shape[1] // 2
-        return lax.dynamic_slice_in_dim(w, d * width, width, 1).astype(bf16)
-
     def placed(vector, offset, rows):
         flat = jnp.zeros((rows * CH,), f32)
         return lax.dynamic_update_slice(flat, vector, (offset,)).reshape(rows, CH)
 
-    turned = jnp.swapaxes(map_w.reshape(-1, HEAD, HEAD), 1, 2).reshape(map_w.shape)
     bias_at, gain_at = (j % 4) * 32, (j % 2) * 64
     small = jnp.concatenate(
         [
             placed(bias_w, bias_at, 9),
             placed(gain_w, gain_at, 2),
             jnp.zeros((5, CH), f32),
-            jnp.concatenate([map_w, turned], 1),
+            jnp.concatenate([map_w[:96], map_w[96:]], 1),
+            jnp.zeros((16, CH), f32),
         ]
     ).astype(bf16)
-    full, gains, bds, tokens, cot, kept = forward_pass(
-        n, inputs, cotangent, small, halved(qkv_w), halved(out_w), halved(up_w), halved(down_w)
-    )
-    layer_out, grads, g_qkv, g_out, g_up, g_down, g_small = backward_pass(
-        n, cot, gains, bds, full, tokens, kept
-    )
-    maps = jnp.concatenate([g_small[16:, :HEAD], g_small[16:, HEAD:]])
+    small = lax.dynamic_slice_in_dim(small, d * 64, 64, 0)
+    full, gains, bds, tokens, cot, lay0, kept = forward_pass(
+        n, inputs, cotangent, small, qkv_w, out_w, up_w, down_w
+    )
+    lay1, *rest, g_small = backward_pass(n, cot, gains, bds, full, tokens, kept)
+    layer_out, grads, g_qkv, g_out, g_up, g_down, maps = settle(lay0, lay1, rest, g_small)
     bias = lax.dynamic_slice_in_dim(g_small[:9].reshape(-1), bias_at, bias_w.shape[0])
     gain = lax.dynamic_slice_in_dim(g_small[9:11].reshape(-1), gain_at, gain_w.shape[0])
     return (

time: 534 us -> 469 us (0.88)
  Pallas kernels: 500 us -> 453 us
  local copies, waits for them, and re-layouts: 21 us -> 7.08 us
    pallas_call x2 -> x3, Pallas kernels: 500 us -> 453 us  [call(): pl.pallas_call(kernel, out_shape=outs, in_specs=specs, out_specs=out_spec...]
    unnamed x22 -> x2, local copies, waits for them, and re-layouts: 10.1 us -> 2.55 us
    convert_element_type x4 -> x0, local copies, waits for them, and re-layouts: 5.83 us -> none  [halved(): return lax.dynamic_slice_in_dim(w, d * width, width, 1).astype(bf16)]
where the time goes in v4:
time: 469 us; the launch traced here: 462 us
  Pallas kernels  453 us (97%)
  local copies, waits for them, and re-layouts  7.08 us (2%)
    pallas_call x3, Pallas kernels, call(): pl.pallas_call(kernel, out_shape=outs, in_specs=specs, out_specs=out_spec...  453 us

profile of v4, /device:TPU:13, one launch (start us, length us, event | category | flops | bytes accessed | tf_op | source)
XLA Modules:
  0.0 462.1 jit_solution(10261017863518522155)
XLA Ops:
  0.7 0.9 dynamic_update_slice.7
  1.6 0.7 reduce
  2.3 0.3 dynamic_update_slice.6
  2.6 0.9 copy.18
  3.5 0.1 pad_maximum_fusion
  3.6 0.1 concatenate.9
  3.7 0.6 constant_dynamic-slice_fusion.refs_2_
  4.3 191.6 %shard_map.160 = (bf16[2,4,2,96,2304]{4,3,2,1,0:T(8,128)(2,1)}, bf16[2,4,2,96,768]{4,3,2,1,0:T(8,128)(2,1)}, bf16[2,4,2,96,3072]{4,3,2,1,0:T(8,128)(2,1)}, bf16[...) custom-call(bf16[4,2,128,768]{3,2,1,0:T(8,128)(2,1)} %refs_0_.1, ...), custom_call_target="tpu_custom_call" | custom-call | flops 14495514624 | bytes 79872000 | tf_op jit(solution)/shard_map/pallas_call | solution.py:628
  196.0 254.7 %shard_map.161 = (bf16[1,4,2,128,768]{4,3,2,1,0:T(8,128)(2,1)}, bf16[1,4,2,128,768]{4,3,2,1,0:T(8,128)(2,1)}, f32[96,2304]{1,0:T(8,128)}, f32[96,768]{1,0:T(8,12...) custom-call(bf16[512,768]{1,0:T(8,128)(2,1)} %get-tuple-element.57.r, ...), custom_call_target="tpu_custom_call" | custom-call | flops 28991029248 | bytes 92504064 | tf_op jit(solution)/shard_map/pallas_call | solution.py:628
  450.7 6.9 %shard_map.162 = (bf16[1,4,2,128,768]{4,3,2,1,0:T(8,128)(2,1)}, bf16[1,4,2,128,768]{4,3,2,1,0:T(8,128)(2,1)}, f32[96,2304]{1,0:T(8,128)}, f32[96,768]{1,0:T(8,12...) custom-call(bf16[1,4,2,128,768]{4,3,2,1,0:T(8,128)(2,1)} %get-tuple-element.56.lay0, ...), custom_call_target="tpu_custom_call" | custom-call | flops 1 | bytes 15056896 | tf_op jit(solution)/shard_map/pallas_call | solution.py:628
  457.6 0.7 slice_bitcast_fusion.3
  458.3 0.7 slice_bitcast_fusion.2
  459.0 0.1 dynamic_slice.10
  459.0 0.6 broadcast_in_dim.42
  459.6 0.6 dynamic_slice.11
  460.3 1.6 copy.19
  (5 shorter events, 0.0 us)

commit v5 on v4

--- a/solution.py
+++ b/solution.py
@@ -1790,7 +1790,7 @@
         put_rows(vr, layer, SHIFT2 if which else SHIFT1, acc[0:1, :])
         put_rows(gr, layer, which * 6, acc[1:2, :])
 
-    def mlp_back(layer, g, events):
+    def mlp_back(layer, g, events, hooks):
         gp, r, o_, inv, ph = v.gp, v.r, v.o, v.inv, v.ph
         drb, gs, st = own.drb, own.gs, own.st
         loaded(v.gp)
@@ -1806,6 +1806,7 @@
                 load_wd(layer, k + 3)
             if k in events:
                 events[k]()
+        hooks[0]()
         loaded_w(U)
 
         def n2_col(j):
@@ -1813,6 +1814,7 @@
             tmp[:, cols] = nt(gp[...], flat.u[cols, :])
 
         loop(D // TILE, n2_col)
+        hooks[1]()
         loaded(v.r)
 
         def body(rows, back):
@@ -1826,6 +1828,7 @@
         norm_back(r, 1, layer, body)
         put_rows(vr, layer, DOWN_BIAS, acc[2:3, :])
         put_rows(vr, layer, OUT_BIAS, acc[3:4, :])
+        hooks[2]()
         loaded_w(O)
         loaded(v.inv, v.o, v.ph)
 
@@ -2017,11 +2020,13 @@
                     mg[which * H + 2 * k + hh] = blk - pltpu.roll(blk, HEAD, 1)
 
         loop(PAIRS, pair, events)
+
+    def input_back(layer):
         loaded_w(Q)
 
         def n1_col(j):
             cols = span(j, TILE)
-            tmp[:, cols] = nt(qkv[...], flat.q[cols, :])
+            tmp[:, cols] = nt(v.qkv[...], flat.q[cols, :])
 
         loop(D // TILE, n1_col)
         loaded(v.u)
@@ -2082,19 +2087,28 @@
 
     deliver(0, 1, ref.res1)
     weight_grad(1, DN, False)
-    mlp_back(1, gbuf.at[0], {4: functools.partial(weight_grad, 1, DN, True)})
+    mlp_back(
+        1,
+        gbuf.at[0],
+        {},
+        (
+            run(functools.partial(loaded, v.n2), functools.partial(weight_grad, 1, U, False)),
+            functools.partial(weight_grad, 1, DN, True),
+            run(functools.partial(loaded, v.ob), functools.partial(weight_grad, 1, O, False)),
+        ),
+    )
     load(0, v.o)
     load_w(0, U)
     load_w(0, O)
     for k in range(3):
         load_wd(0, k)
-    loaded(v.n2, v.ob, v.a)
-    weight_grad(1, U, False)
-    weight_grad(1, O, False)
+    loaded(v.a)
     weight_grad(1, U, True)
     weight_grad(1, O, True)
     load(0, v.gp, v.n2, v.ob)
     mix_back(1, {1: step_y(1, DN), 5: step_a(1, DN)})
+    input_back(1)
+    deliver(1, 1, gbuf.at[1])
     load_w(0, Q)
     load(0, v.r, v.inv, v.ph, v.u, v.pre)
     pack_small(1)
@@ -2110,16 +2124,22 @@
     mlp_back(
         0,
         gbuf.at[1],
-        {4: functools.partial(weight_grad, 0, DN, True), 6: step_a(1, U), 7: step_x(1, DN)},
-    )
-    loaded(v.n2, v.ob, v.a)
-    step_a(1, O)()
-    step_z(1, U)()
-    weight_grad(0, U, False)
-    step_y(1, Q, SM)()
-    weight_grad(0, U, True)
+        {5: step_x(1, DN), 6: step_a(1, U)},
+        (
+            step_a(1, O),
+            functools.partial(weight_grad, 0, DN, True),
+            run(
+                step_z(1, U),
+                functools.partial(loaded, v.n2),
+                functools.partial(weight_grad, 0, U, False),
+            ),
+        ),
+    )
+    loaded(v.ob, v.a)
     step_z(1, O)()
     weight_grad(0, O, False)
+    weight_grad(0, U, True)
+    step_y(1, Q, SM)()
     weight_grad(0, O, True)
     step_x(1, U)()
     mix_back(
@@ -2131,21 +2151,21 @@
             4: step_z(1, Q, SM),
         },
     )
-    pack_small(0)
     weight_grad(0, Q, False)
     step_a(0, DN)()
     step_x(1, Q, SM)()
     weight_grad(0, Q, True)
+    step_y(0, U)()
+    input_back(0)
+    pack_small(0)
+    step_z(0, DN)()
+    step_y(0, O)()
+    step_a(0, U)()
     small_core(0)
-    step_y(0, U)()
-    step_y(0, O)()
-    step_z(0, DN)()
-    deliver(1, 1, gbuf.at[1])
     deliver(1, 0, gbuf.at[0])
+    step_x(0, DN)()
     first, second, third = reduces[0][Q]
-    step_x(0, DN)()
     first.step_y()
-    step_a(0, U)()
     step_a(0, O)()
     second.step_y()
     first.step_a()

time: 469 us -> 464 us (0.989)
  Pallas kernels: 453 us -> 446 us
    pallas_call x3, Pallas kernels: 453 us -> 446 us  [call(): pl.pallas_call(kernel, out_shape=outs, in_specs=specs, out_specs=out_spec...]
where the time goes in v5:
time: 464 us; the launch traced here: 455 us
  Pallas kernels  446 us (96%)
  local copies, waits for them, and re-layouts  7.08 us (2%)
    pallas_call x3, Pallas kernels, call(): pl.pallas_call(kernel, out_shape=outs, in_specs=specs, out_specs=out_spec...  446 us

profile of v5, /device:TPU:13, one launch (start us, length us, event | category | flops | bytes accessed | tf_op | source)
XLA Modules:
  0.0 455.4 jit_solution(15568766665941449032)
XLA Ops:
  0.7 0.9 dynamic_update_slice.7
  1.6 0.7 reduce
  2.3 0.3 dynamic_update_slice.6
  2.6 0.9 copy.18
  3.5 0.1 pad_maximum_fusion
  3.6 0.1 concatenate.9
  3.7 0.6 constant_dynamic-slice_fusion.refs_2_
  4.3 191.7 %shard_map.160 = (bf16[2,4,2,96,2304]{4,3,2,1,0:T(8,128)(2,1)}, bf16[2,4,2,96,768]{4,3,2,1,0:T(8,128)(2,1)}, bf16[2,4,2,96,3072]{4,3,2,1,0:T(8,128)(2,1)}, bf16[...) custom-call(bf16[4,2,128,768]{3,2,1,0:T(8,128)(2,1)} %refs_0_.1, ...), custom_call_target="tpu_custom_call" | custom-call | flops 14495514624 | bytes 79872000 | tf_op jit(solution)/shard_map/pallas_call | solution.py:628
  196.0 247.7 %shard_map.161 = (bf16[1,4,2,128,768]{4,3,2,1,0:T(8,128)(2,1)}, bf16[1,4,2,128,768]{4,3,2,1,0:T(8,128)(2,1)}, f32[96,2304]{1,0:T(8,128)}, f32[96,768]{1,0:T(8,12...) custom-call(bf16[512,768]{1,0:T(8,128)(2,1)} %get-tuple-element.57.r, ...), custom_call_target="tpu_custom_call" | custom-call | flops 28991029248 | bytes 92504064 | tf_op jit(solution)/shard_map/pallas_call | solution.py:628
  443.7 6.9 %shard_map.162 = (bf16[1,4,2,128,768]{4,3,2,1,0:T(8,128)(2,1)}, bf16[1,4,2,128,768]{4,3,2,1,0:T(8,128)(2,1)}, f32[96,2304]{1,0:T(8,128)}, f32[96,768]{1,0:T(8,12...) custom-call(bf16[1,4,2,128,768]{4,3,2,1,0:T(8,128)(2,1)} %get-tuple-element.56.lay0, ...), custom_call_target="tpu_custom_call" | custom-call | flops 1 | bytes 15056896 | tf_op jit(solution)/shard_map/pallas_call | solution.py:628
  450.6 0.7 slice_bitcast_fusion.3
  451.3 0.7 slice_bitcast_fusion.2
  452.0 0.1 dynamic_slice.10
  452.1 0.6 broadcast_in_dim.42
  452.7 0.6 dynamic_slice.11
  453.3 1.6 copy.19
  (5 shorter events, 0.0 us)

commit v6 on v5

--- a/solution.py
+++ b/solution.py
@@ -2147,7 +2147,7 @@
         {
             0: step_x(1, O),
             1: step_a(1, Q, SM),
-            3: step_y(0, DN),
+            2: step_y(0, DN),
             4: step_z(1, Q, SM),
         },
     )
@@ -2155,14 +2155,14 @@
     step_a(0, DN)()
     step_x(1, Q, SM)()
     weight_grad(0, Q, True)
+    input_back(0)
+    deliver(1, 0, gbuf.at[0])
     step_y(0, U)()
-    input_back(0)
     pack_small(0)
     step_z(0, DN)()
     step_y(0, O)()
     step_a(0, U)()
     small_core(0)
-    deliver(1, 0, gbuf.at[0])
     step_x(0, DN)()
     first, second, third = reduces[0][Q]
     first.step_y()

time: 464 us -> 468 us (level)
  no operation moved by 1% of the time
where the time goes in v6:
time: 468 us; the launch traced here: 459 us
  Pallas kernels  450 us (96%)
  local copies, waits for them, and re-layouts  7.08 us (2%)
    pallas_call x3, Pallas kernels, call(): pl.pallas_call(kernel, out_shape=outs, in_specs=specs, out_specs=out_spec...  450 us

profile of v6, /device:TPU:13, one launch (start us, length us, event | category | flops | bytes accessed | tf_op | source)
XLA Modules:
  0.0 458.8 jit_solution(15922352129711517654)
XLA Ops:
  0.7 0.9 dynamic_update_slice.7
  1.6 0.7 reduce
  2.3 0.3 dynamic_update_slice.6
  2.6 0.9 copy.18
  3.5 0.1 pad_maximum_fusion
  3.6 0.1 concatenate.9
  3.7 0.6 constant_dynamic-slice_fusion.refs_2_
  4.3 191.7 %shard_map.160 = (bf16[2,4,2,96,2304]{4,3,2,1,0:T(8,128)(2,1)}, bf16[2,4,2,96,768]{4,3,2,1,0:T(8,128)(2,1)}, bf16[2,4,2,96,3072]{4,3,2,1,0:T(8,128)(2,1)}, bf16[...) custom-call(bf16[4,2,128,768]{3,2,1,0:T(8,128)(2,1)} %refs_0_.1, ...), custom_call_target="tpu_custom_call" | custom-call | flops 14495514624 | bytes 79872000 | tf_op jit(solution)/shard_map/pallas_call | solution.py:628
  196.0 251.2 %shard_map.161 = (bf16[1,4,2,128,768]{4,3,2,1,0:T(8,128)(2,1)}, bf16[1,4,2,128,768]{4,3,2,1,0:T(8,128)(2,1)}, f32[96,2304]{1,0:T(8,128)}, f32[96,768]{1,0:T(8,12...) custom-call(bf16[512,768]{1,0:T(8,128)(2,1)} %get-tuple-element.57.r, ...), custom_call_target="tpu_custom_call" | custom-call | flops 28991029248 | bytes 92504064 | tf_op jit(solution)/shard_map/pallas_call | solution.py:628
  447.2 6.9 %shard_map.162 = (bf16[1,4,2,128,768]{4,3,2,1,0:T(8,128)(2,1)}, bf16[1,4,2,128,768]{4,3,2,1,0:T(8,128)(2,1)}, f32[96,2304]{1,0:T(8,128)}, f32[96,768]{1,0:T(8,12...) custom-call(bf16[1,4,2,128,768]{4,3,2,1,0:T(8,128)(2,1)} %get-tuple-element.56.lay0, ...), custom_call_target="tpu_custom_call" | custom-call | flops 1 | bytes 15056896 | tf_op jit(solution)/shard_map/pallas_call | solution.py:628
  454.1 0.7 slice_bitcast_fusion.3
  454.8 0.7 slice_bitcast_fusion.2
  455.5 0.1 dynamic_slice.10
  455.6 0.6 broadcast_in_dim.42
  456.2 0.6 dynamic_slice.11
  456.8 1.6 copy.19
  (5 shorter events, 0.0 us)
